TPU v7x, 32 devices: a whole 2x2x4 slice. The times are simulated.
32 devices in a mesh: groups: 2 (over y), seg: 4 (over z), space: 4 (over x, core).
Axes of the slice: x: 2, y: 2, z: 4, core: 2. Of those that a mesh axis runs over, the one named last changes fastest.
Arguments:
- basis: bfloat16 [8, 16, 3, 128, 256], P(('groups', 'seg'), 'space'), parts along dimension 0, may hold values from -6 to 6
- diffusivity: float32 [8, 16, 3, 128], P(('groups', 'seg'), 'space'), parts along dimension 0, may hold values from 0.05 to 0.15
- velocity: float32 [8, 3, 16, 3, 128], P(('groups', 'seg'), None, 'space'), parts along dimension 0, may hold values from -0.1 to 0.1
- step_counts: int32 [8], P(('groups', 'seg')), parts along dimension 0, may hold values from 2 to 4, as said below
- block_order: int32 [8, 16], P('groups'), parts along dimension 0, may hold values from 0 to 15, each once within a row
Outputs:
- image: bfloat16 [8, 16, 3, 128, 256], P(('groups', 'seg'), 'space'), parts along dimension 0
- monodromy: float32 [8, 256, 256], P(('groups', 'seg')), parts along dimension 0
There are 2 independent parts, one for each index of `groups`. A program takes and returns all parts, laid end to end along the dimension named above; each array names one. Nothing has to cross between parts.
Inputs may be any that keep to these rules, and one draw needn't show every extreme that they name: `step_counts`: every segment takes two or more steps, and some segment takes 4. `block_order`: each row lists every block 0 to 15 once.
All inputs are finite; a program needn't handle non-finite values.
Results may differ from a plain program's by a relative error of at most 0.0052.
Values may be sent and summed in bfloat16 or wider, within the bound.
No kernel may reach another device: no remote copies, remote signals or barrier semaphores. Data moves between devices by JAX's collectives and lax.ppermute only.
A program may use at most 64 MiB of HBM per device.

v0:
```python
import math

import jax
import jax.numpy as jnp
from jax import lax
from jax.sharding import PartitionSpec as P

K = 256
BLOCK = 16
STEPS = 4


coupling = 0.35


def with_halo(value, sides, width):
    for axis, dim in sides:
        size, length = (lax.axis_size(axis), value.shape[dim])
        up = [(i, (i + 1) % size) for i in range(size - 1)]
        down = [(j, i) for i, j in up]
        last = lax.slice_in_dim(value, length - width, length, axis=dim)
        initial = lax.slice_in_dim(value, 0, width, axis=dim)
        before = lax.ppermute(last, axis, up)
        after = lax.ppermute(initial, axis, down)
        value = jnp.concatenate([before, value, after], axis=dim)
    return value


def from_behind(block, axis, distance):
    devices = range(lax.axis_size(axis))
    route = [((i - distance) % len(devices), i) for i in devices]
    return lax.ppermute(block, axis, route)


def carried_in(value, axis, combine, identity):
    length, position = (lax.axis_size(axis), lax.axis_index(axis))
    everything = lax.all_gather(value, axis)
    start = jnp.broadcast_to(jnp.asarray(identity, value.dtype), value.shape)

    def lap(k, before):
        reached = k < position
        new = combine(before, everything[k])
        return jnp.where(reached, new, before)

    return lax.fori_loop(0, length, lap, start)


def step_once(window, diffusivity, velocity):
    wide = window.astype(jnp.float32)
    center = wide[1:-1]
    plus_x = wide[2:]
    minus_x = wide[:-2]
    plus_y = jnp.roll(center, -1, 1)
    minus_y = jnp.roll(center, 1, 1)
    plus_z = jnp.roll(center, -1, 2)
    minus_z = jnp.roll(center, 1, 2)
    spread = diffusivity[..., None]
    laplace = plus_x + minus_x + plus_y + minus_y + plus_z + minus_z - 6.0 * center
    drift = (
        velocity[0][..., None] * (plus_x - minus_x)
        + velocity[1][..., None] * (plus_y - minus_y)
        + velocity[2][..., None] * (plus_z - minus_z)
    )
    return (center + spread * laplace - 0.5 * drift).astype(jnp.bfloat16)


def block_perm(order):
    stored = jnp.arange(K, dtype=jnp.int32)
    which = stored // BLOCK
    onehot = which[:, None] == jnp.arange(order.shape[0], dtype=jnp.int32)[None, :]
    true_col = jnp.sum(jnp.where(onehot, order[None, :], 0), axis=1) * BLOCK + stored % BLOCK
    return (jnp.arange(K, dtype=jnp.int32)[:, None] == true_col[None, :]).astype(jnp.float32)


def propagator(raw_sums, left_order, right_order, cells):
    left = block_perm(left_order)
    right = block_perm(right_order)
    inner = jnp.dot(
        left, raw_sums, precision=lax.Precision.HIGHEST, preferred_element_type=jnp.float32
    )
    true_sums = jnp.dot(
        inner, right.T, precision=lax.Precision.HIGHEST, preferred_element_type=jnp.float32
    )
    return jnp.eye(K, dtype=jnp.float32) + coupling / math.sqrt(K * cells) * true_sums


def contract(left_cols, right_cols):
    return lax.dot_general(
        left_cols.reshape(-1, K),
        right_cols.reshape(-1, K),
        (((0,), (0,)), ((), ())),
        preferred_element_type=jnp.float32,
    )


def order_row(block_order, index):
    return lax.dynamic_slice_in_dim(block_order, index, 1, 0)[0]


def chain_combine(earlier, later):
    return jnp.dot(
        later, earlier, precision=lax.Precision.HIGHEST, preferred_element_type=jnp.float32
    )


def per_device(basis, diffusivity, velocity, step_counts, block_order):
    start = basis[0]
    spread = diffusivity[0]
    drift = velocity[0]
    count = step_counts[0]
    state = start
    for turn in range(STEPS):
        window = with_halo(state, (("space", 0),), 1)
        fresh = step_once(window, spread, drift)
        state = jnp.where(turn < count, fresh, state)
    position = lax.axis_index("seg")
    total = lax.axis_size("seg")
    cells = start.shape[0] * lax.axis_size("space") * start.shape[1] * start.shape[2]
    earlier_image = from_behind(state, "seg", 1)
    raw_sums = contract(start, earlier_image)
    right_index = (position + total - 1) % total
    raw_sums = lax.psum(raw_sums.astype(jnp.bfloat16), "space").astype(jnp.float32)
    prop = propagator(
        raw_sums, order_row(block_order, position), order_row(block_order, right_index), cells
    )
    prop = from_behind(prop, "seg", -1)
    prefix = carried_in(prop, "seg", chain_combine, jnp.eye(K, dtype=jnp.float32))
    monodromy = jnp.dot(
        prop, prefix, precision=lax.Precision.HIGHEST, preferred_element_type=jnp.float32
    )
    return (state[None], monodromy[None])


def solution(mesh):
    in_specs = (
        P(("groups", "seg"), "space", None, None, None),
        P(("groups", "seg"), "space", None, None),
        P(("groups", "seg"), None, "space", None, None),
        P(("groups", "seg")),
        P("groups", None),
    )
    out_specs = (P(("groups", "seg"), "space", None, None, None), P(("groups", "seg"), None, None))
    return jax.shard_map(
        per_device, mesh=mesh, in_specs=in_specs, out_specs=out_specs, check_vma=False
    )
```

profile of v0, /device:TPU:0, one launch (start us, length us, event | category | flops | bytes accessed | tf_op | source)
XLA Modules:
  0.0 163.7 jit_solution(16445292642639492544)
XLA Ops:
  7.2 1.1 slice_bitcast_fusion.1
  8.3 2.4 %collective-permute-start = (bf16[1,3,128,256]{3,2,1,0:T(8,128)(2,1)S(1)}, bf16[1,3,128,256]{3,2,1,0:T(8,128)(2,1)S(1)}, u32[]{:S(2)}, u32[]{:S(2)}) collective-permute-start(bf16[1,3,128,256]{3,2,1,0:T(8,128)(2,1)S(1)} %get-tuple-element.130), channel_id=1, source_target_pairs={{0,1},{1,2},{2,3},{4,5},{5,6},{6,7},{8,9},{9,10},{10,11},{12,13},{... | collective-permute-start | bytes 589832 | tf_op jit(solution)/shard_map/ppermute | solution.py:23
  10.6 1.3 collective-permute-start.1
  14.1 2.0 %collective-permute-done.1 = bf16[1,3,128,256]{3,2,1,0:T(8,128)(2,1)S(1)} collective-permute-done((bf16[1,3,128,256]{3,2,1,0:T(8,128)(2,1)S(1)}, bf16[1,3,128,256]{3,2,1,0:T(8,128)(2,1)S(1)}, u32[]{:S(2)}, u32[]{:S(2)}) %collective-permute-start.1) | collective-permute-done | bytes 196640 | tf_op jit(solution)/shard_map/ppermute | solution.py:24
  16.1 1.3 maximum_convert_fusion
  19.1 2.2 %broadcast_select_fusion = bf16[4,3,128,256]{3,2,1,0:T(8,128)(2,1)S(1)} fusion(pred[]{:T(512)} %bitcast.4, f32[4,3,128]{2,1,0:T(4,128)S(1)} %copy.14, f32[4,3,128]{2,1,0:T(4,128)S(1)} %copy.13, f32[4,3,128]{2,1,0:T(4,128)S(1)} %copy.12, f32[4,3,127,256]{3,2,1,0:T(8,128)S(1)} %get-tuple-element.115, f32[4,3,1,256]{3,2,1,0:T(1,128)S(1)} %get-tuple-element.123, ...), kind=kLoop, calls=%fused_computation.33 | loop fusion | flops 9830400 | bytes 12607489 | tf_op jit(solution)/shard_map/jit(_where)/select_n | solution.py:115
  21.3 6.1 %collective-permute-start.2 = (bf16[1,3,128,256]{3,2,1,0:T(8,128)(2,1)S(1)}, bf16[1,3,128,256]{3,2,1,0:T(8,128)(2,1)S(1)}, u32[]{:S(2)}, u32[]{:S(2)}) collective-permute-start(bf16[1,3,128,256]{3,2,1,0:T(8,128)(2,1)S(1)} %get-tuple-element.128), channel_id=1, source_target_pairs={{0,1},{1,2},{2,3},{4,5},{5,6},{6,7},{8,9},{9,10},{10,11},{12,13},{... | collective-permute-start | bytes 589832 | tf_op jit(solution)/shard_map/ppermute | solution.py:23
  27.4 1.3 collective-permute-start.3
  28.7 2.0 %collective-permute-done.3 = bf16[1,3,128,256]{3,2,1,0:T(8,128)(2,1)S(1)} collective-permute-done((bf16[1,3,128,256]{3,2,1,0:T(8,128)(2,1)S(1)}, bf16[1,3,128,256]{3,2,1,0:T(8,128)(2,1)S(1)}, u32[]{:S(2)}, u32[]{:S(2)}) %collective-permute-start.3) | collective-permute-done | bytes 196640 | tf_op jit(solution)/shard_map/ppermute | solution.py:24
  31.6 2.2 %broadcast_select_fusion.1 = bf16[4,3,128,256]{3,2,1,0:T(8,128)(2,1)S(1)} fusion(bf16[4,3,128,256]{3,2,1,0:T(8,128)(2,1)S(1)} %broadcast_select_fusion, pred[]{:T(512)} %bitcast.3, f32[4,3,128]{2,1,0:T(4,128)S(1)} %copy.14, f32[4,3,128]{2,1,0:T(4,128)S(1)} %copy.13, f32[4,3,128]{2,1,0:T(4,128)S(1)} %copy.12, f32[4,3,127,256]{3,2,1,0:T(8,128)S(1)} %get-tuple-element.109, ...), kind=kLoop, calls=%fused_computation.34 | loop fusion | flops 9830400 | bytes 12607489 | tf_op jit(solution)/shard_map/jit(_where)/select_n | solution.py:115
  33.8 5.6 %collective-permute-start.4 = (bf16[1,3,128,256]{3,2,1,0:T(8,128)(2,1)S(1)}, bf16[1,3,128,256]{3,2,1,0:T(8,128)(2,1)S(1)}, u32[]{:S(2)}, u32[]{:S(2)}) collective-permute-start(bf16[1,3,128,256]{3,2,1,0:T(8,128)(2,1)S(1)} %get-tuple-element.126), channel_id=1, source_target_pairs={{0,1},{1,2},{2,3},{4,5},{5,6},{6,7},{8,9},{9,10},{10,11},{12,13},{... | collective-permute-start | bytes 589832 | tf_op jit(solution)/shard_map/ppermute | solution.py:23
  39.4 1.3 collective-permute-start.5
  40.7 2.0 %collective-permute-done.5 = bf16[1,3,128,256]{3,2,1,0:T(8,128)(2,1)S(1)} collective-permute-done((bf16[1,3,128,256]{3,2,1,0:T(8,128)(2,1)S(1)}, bf16[1,3,128,256]{3,2,1,0:T(8,128)(2,1)S(1)}, u32[]{:S(2)}, u32[]{:S(2)}) %collective-permute-start.5) | collective-permute-done | bytes 196640 | tf_op jit(solution)/shard_map/ppermute | solution.py:24
  43.6 2.2 %broadcast_select_fusion.2 = bf16[4,3,128,256]{3,2,1,0:T(8,128)(2,1)S(1)} fusion(bf16[4,3,128,256]{3,2,1,0:T(8,128)(2,1)S(1)} %broadcast_select_fusion.1, pred[]{:T(512)} %bitcast.2, f32[4,3,128]{2,1,0:T(4,128)S(1)} %copy.14, f32[4,3,128]{2,1,0:T(4,128)S(1)} %copy.13, f32[4,3,128]{2,1,0:T(4,128)S(1)} %copy.12, f32[4,3,127,256]{3,2,1,0:T(8,128)S(1)} %get-tuple-element.103, ...), kind=kLoop, calls=%fused_computation.35 | loop fusion | flops 9830400 | bytes 12607489 | tf_op jit(solution)/shard_map/jit(_where)/select_n | solution.py:115
  45.8 5.6 %collective-permute-start.6 = (bf16[1,3,128,256]{3,2,1,0:T(8,128)(2,1)S(1)}, bf16[1,3,128,256]{3,2,1,0:T(8,128)(2,1)S(1)}, u32[]{:S(2)}, u32[]{:S(2)}) collective-permute-start(bf16[1,3,128,256]{3,2,1,0:T(8,128)(2,1)S(1)} %get-tuple-element.124), channel_id=1, source_target_pairs={{0,1},{1,2},{2,3},{4,5},{5,6},{6,7},{8,9},{9,10},{10,11},{12,13},{... | collective-permute-start | bytes 589832 | tf_op jit(solution)/shard_map/ppermute | solution.py:23
  51.4 1.3 collective-permute-start.7
  52.7 2.0 %collective-permute-done.7 = bf16[1,3,128,256]{3,2,1,0:T(8,128)(2,1)S(1)} collective-permute-done((bf16[1,3,128,256]{3,2,1,0:T(8,128)(2,1)S(1)}, bf16[1,3,128,256]{3,2,1,0:T(8,128)(2,1)S(1)}, u32[]{:S(2)}, u32[]{:S(2)}) %collective-permute-start.7) | collective-permute-done | bytes 196640 | tf_op jit(solution)/shard_map/ppermute | solution.py:24
  55.6 2.2 %broadcast_select_fusion.3 = bf16[4,3,128,256]{3,2,1,0:T(8,128)(2,1)S(1)} fusion(bf16[4,3,128,256]{3,2,1,0:T(8,128)(2,1)S(1)} %broadcast_select_fusion.2, pred[]{:T(512)} %bitcast.1, f32[4,3,128]{2,1,0:T(4,128)S(1)} %copy.14, f32[4,3,128]{2,1,0:T(4,128)S(1)} %copy.13, f32[4,3,128]{2,1,0:T(4,128)S(1)} %copy.12, f32[4,3,127,256]{3,2,1,0:T(8,128)S(1)} %get-tuple-element.97, ...), kind=kLoop, calls=%fused_computation.36 | loop fusion | flops 9830400 | bytes 12607489 | tf_op jit(solution)/shard_map/jit(_where)/select_n | solution.py:115
  57.8 1.6 collective-permute-start.8
  59.5 17.7 %collective-permute-done.8 = bf16[4,3,128,256]{3,2,1,0:T(8,128)(2,1)S(1)} collective-permute-done((bf16[4,3,128,256]{3,2,1,0:T(8,128)(2,1)S(1)}, bf16[4,3,128,256]{3,2,1,0:T(8,128)(2,1)S(1)}, u32[]{:S(2)}, u32[]{:S(2)}) %collective-permute-start.8) | collective-permute-done | bytes 786464 | tf_op jit(solution)/shard_map/ppermute | solution.py:32
  77.3 1.1 fusion.4
  78.4 32.3 %all-reduce.2.cloned.1.call-done = bf16[256,256]{0,1:T(8,128)(2,1)} async-done(((bf16[256,256]{0,1:T(8,128)(2,1)}), bf16[256,256]{0,1:T(8,128)(2,1)}) %all-reduce.2.cloned.1.call-update) | async-done | bytes 131088 | tf_op jit(solution)/shard_map/psum | solution.py:122
  110.7 1.1 fusion.6
  112.2 3.4 %collective-permute-start.9 = (f32[256,256]{1,0:T(8,128)S(1)}, f32[256,256]{1,0:T(8,128)S(1)}, u32[]{:S(2)}, u32[]{:S(2)}) collective-permute-start(f32[256,256]{1,0:T(8,128)S(1)} %fusion.3), channel_id=1, source_target_pairs={{4,0},{8,4},{12,8},{0,12},{5,1},{9,5},{13,9},{1,13},{6,2},{10,6},{... | collective-permute-start | bytes 786440 | tf_op jit(solution)/shard_map/ppermute | solution.py:32
  115.6 4.5 %collective-permute-done.9 = f32[256,256]{1,0:T(8,128)S(1)} collective-permute-done((f32[256,256]{1,0:T(8,128)S(1)}, f32[256,256]{1,0:T(8,128)S(1)}, u32[]{:S(2)}, u32[]{:S(2)}) %collective-permute-start.9) | collective-permute-done | bytes 262176 | tf_op jit(solution)/shard_map/ppermute | solution.py:32
  120.9 29.3 %all-gather.3.cloned.1.call-done = f32[1024,256]{1,0:T(8,128)} async-done(((f32[256,256]{1,0:T(8,128)}), f32[1024,256]{1,0:T(8,128)}) %all-gather.3.cloned.1.call-update) | async-done | bytes 1048592 | tf_op jit(solution)/shard_map/all_gather | solution.py:37
  150.2 5.6 %while.13 = (s32[]{:T(128)}, f32[256,256]{1,0:T(8,128)S(1)}, s32[]{:T(128)}, f32[4,256,256]{2,1,0:T(8,128)}, s32[]{:T(128)}) while((s32[]{:T(128)}, f32[256,256]{1,0:T(8,128)S(1)}, s32[]{:T(128)}, f32[4,256,256]{2,1,0:T(8,128)}, s32[]{:T(128)}) %tuple.64), condition=%wide.region_4.5_spmd, body=%wide.region_3.4_spmd.sunk | while | flops 201392128 | bytes 1573447 | solution.py:45
  150.2 1.4 convolution_select_fusion.2
  151.6 1.3 convolution_select_fusion.2
  153.0 1.3 convolution_select_fusion.2
  154.4 1.3 convolution_select_fusion.2
  155.7 1.1 convolution_bitcast_fusion
  (55 shorter events, 7.0 us)
Async XLA Ops:
  7.2 103.6 %all-reduce.2.cloned.1.call-start = ((), (), s32[]{:S(2)}) async-start(), calls=%async_computation | async-start | bytes 262144 | tf_op jit(solution)/shard_map/psum | solution.py:122
  8.3 5.8 %collective-permute-start = (bf16[1,3,128,256]{3,2,1,0:T(8,128)(2,1)S(1)}, bf16[1,3,128,256]{3,2,1,0:T(8,128)(2,1)S(1)}, u32[]{:S(2)}, u32[]{:S(2)}) collective-permute-start(bf16[1,3,128,256]{3,2,1,0:T(8,128)(2,1)S(1)} %get-tuple-element.130), channel_id=1, source_target_pairs={{0,1},{1,2},{2,3},{4,5},{5,6},{6,7},{8,9},{9,10},{10,11},{12,13},{... | collective-permute-start | bytes 589832 | tf_op jit(solution)/shard_map/ppermute | solution.py:23
  10.6 5.4 %collective-permute-start.1 = (bf16[1,3,128,256]{3,2,1,0:T(8,128)(2,1)S(1)}, bf16[1,3,128,256]{3,2,1,0:T(8,128)(2,1)S(1)}, u32[]{:S(2)}, u32[]{:S(2)}) collective-permute-start(bf16[1,3,128,256]{3,2,1,0:T(8,128)(2,1)S(1)} %get-tuple-element.131), channel_id=1, source_target_pairs={{1,0},{2,1},{3,2},{5,4},{6,5},{7,6},{9,8},{10,9},{11,10},{13,12},{... | collective-permute-start | bytes 589832 | tf_op jit(solution)/shard_map/ppermute | solution.py:24
  17.9 1.1 copy-start
  21.3 7.4 %collective-permute-start.2 = (bf16[1,3,128,256]{3,2,1,0:T(8,128)(2,1)S(1)}, bf16[1,3,128,256]{3,2,1,0:T(8,128)(2,1)S(1)}, u32[]{:S(2)}, u32[]{:S(2)}) collective-permute-start(bf16[1,3,128,256]{3,2,1,0:T(8,128)(2,1)S(1)} %get-tuple-element.128), channel_id=1, source_target_pairs={{0,1},{1,2},{2,3},{4,5},{5,6},{6,7},{8,9},{9,10},{10,11},{12,13},{... | collective-permute-start | bytes 589832 | tf_op jit(solution)/shard_map/ppermute | solution.py:23
  27.4 3.3 %collective-permute-start.3 = (bf16[1,3,128,256]{3,2,1,0:T(8,128)(2,1)S(1)}, bf16[1,3,128,256]{3,2,1,0:T(8,128)(2,1)S(1)}, u32[]{:S(2)}, u32[]{:S(2)}) collective-permute-start(bf16[1,3,128,256]{3,2,1,0:T(8,128)(2,1)S(1)} %get-tuple-element.129), channel_id=1, source_target_pairs={{1,0},{2,1},{3,2},{5,4},{6,5},{7,6},{9,8},{10,9},{11,10},{13,12},{... | collective-permute-start | bytes 589832 | tf_op jit(solution)/shard_map/ppermute | solution.py:24
  33.8 6.9 %collective-permute-start.4 = (bf16[1,3,128,256]{3,2,1,0:T(8,128)(2,1)S(1)}, bf16[1,3,128,256]{3,2,1,0:T(8,128)(2,1)S(1)}, u32[]{:S(2)}, u32[]{:S(2)}) collective-permute-start(bf16[1,3,128,256]{3,2,1,0:T(8,128)(2,1)S(1)} %get-tuple-element.126), channel_id=1, source_target_pairs={{0,1},{1,2},{2,3},{4,5},{5,6},{6,7},{8,9},{9,10},{10,11},{12,13},{... | collective-permute-start | bytes 589832 | tf_op jit(solution)/shard_map/ppermute | solution.py:23
  39.4 3.3 %collective-permute-start.5 = (bf16[1,3,128,256]{3,2,1,0:T(8,128)(2,1)S(1)}, bf16[1,3,128,256]{3,2,1,0:T(8,128)(2,1)S(1)}, u32[]{:S(2)}, u32[]{:S(2)}) collective-permute-start(bf16[1,3,128,256]{3,2,1,0:T(8,128)(2,1)S(1)} %get-tuple-element.127), channel_id=1, source_target_pairs={{1,0},{2,1},{3,2},{5,4},{6,5},{7,6},{9,8},{10,9},{11,10},{13,12},{... | collective-permute-start | bytes 589832 | tf_op jit(solution)/shard_map/ppermute | solution.py:24
  45.8 6.9 %collective-permute-start.6 = (bf16[1,3,128,256]{3,2,1,0:T(8,128)(2,1)S(1)}, bf16[1,3,128,256]{3,2,1,0:T(8,128)(2,1)S(1)}, u32[]{:S(2)}, u32[]{:S(2)}) collective-permute-start(bf16[1,3,128,256]{3,2,1,0:T(8,128)(2,1)S(1)} %get-tuple-element.124), channel_id=1, source_target_pairs={{0,1},{1,2},{2,3},{4,5},{5,6},{6,7},{8,9},{9,10},{10,11},{12,13},{... | collective-permute-start | bytes 589832 | tf_op jit(solution)/shard_map/ppermute | solution.py:23
  51.4 3.3 %collective-permute-start.7 = (bf16[1,3,128,256]{3,2,1,0:T(8,128)(2,1)S(1)}, bf16[1,3,128,256]{3,2,1,0:T(8,128)(2,1)S(1)}, u32[]{:S(2)}, u32[]{:S(2)}) collective-permute-start(bf16[1,3,128,256]{3,2,1,0:T(8,128)(2,1)S(1)} %get-tuple-element.125), channel_id=1, source_target_pairs={{1,0},{2,1},{3,2},{5,4},{6,5},{7,6},{9,8},{10,9},{11,10},{13,12},{... | collective-permute-start | bytes 589832 | tf_op jit(solution)/shard_map/ppermute | solution.py:24
  55.6 3.9 %copy-start.4 = (s32[4,16]{1,0:T(4,128)S(1)}, s32[4,16]{1,0:T(4,128)}, u32[]{:S(2)}) copy-start(s32[4,16]{1,0:T(4,128)} %param.11) | copy-start | bytes 772
  57.8 54.4 %copy-start.3 = (bf16[4,3,128,256]{3,2,1,0:T(8,128)(2,1)}, bf16[4,3,128,256]{3,2,1,0:T(8,128)(2,1)S(1)}, u32[]{:S(2)}) copy-start(bf16[4,3,128,256]{3,2,1,0:T(8,128)(2,1)S(1)} %broadcast_select_fusion.3) | copy-start | bytes 2359300
  57.8 19.4 %collective-permute-start.8 = (bf16[4,3,128,256]{3,2,1,0:T(8,128)(2,1)S(1)}, bf16[4,3,128,256]{3,2,1,0:T(8,128)(2,1)S(1)}, u32[]{:S(2)}, u32[]{:S(2)}) collective-permute-start(bf16[4,3,128,256]{3,2,1,0:T(8,128)(2,1)S(1)} %broadcast_select_fusion.3), channel_id=1, source_target_pairs={{12,0},{0,4},{4,8},{8,12},{13,1},{1,5},{5,9},{9,13},{14,2},{2,6},{... | collective-permute-start | bytes 2359304 | tf_op jit(solution)/shard_map/ppermute | solution.py:32
  78.4 71.8 %all-gather.3.cloned.1.call-start = ((), (), s32[]{:S(2)}) async-start(), calls=%async_computation.1 | async-start | bytes 1310720 | tf_op jit(solution)/shard_map/all_gather | solution.py:37
  112.2 7.9 %collective-permute-start.9 = (f32[256,256]{1,0:T(8,128)S(1)}, f32[256,256]{1,0:T(8,128)S(1)}, u32[]{:S(2)}, u32[]{:S(2)}) collective-permute-start(f32[256,256]{1,0:T(8,128)S(1)} %fusion.3), channel_id=1, source_target_pairs={{4,0},{8,4},{12,8},{0,12},{5,1},{9,5},{13,9},{1,13},{6,2},{10,6},{... | collective-permute-start | bytes 786440 | tf_op jit(solution)/shard_map/ppermute | solution.py:32
  120.1 0.7 copy-start.1
  150.2 5.6 %copy-start.2 = (f32[256,256]{1,0:T(8,128)S(1)}, f32[256,256]{1,0:T(8,128)}, u32[]{:S(2)}) copy-start(f32[256,256]{1,0:T(8,128)} %copy-done.1) | copy-start | bytes 786436
Sparse Core Ops, SparseCore 0:
  78.5 32.1 all-reduce.1
  121.0 29.1 all-gather.2
where the time goes:
time: 164 us
  waiting for transfers between devices  91.9 us (56%)
  starting transfers between devices  29.8 us (18%)
  between operations  15.1 us (9%)
  other arithmetic  10.8 us (7%)
  matrix products  9.01 us (5%)
  local copies, waits for them, and re-layouts  6.86 us (4%)
    psum x1, waiting for transfers between devices, per_device(): lax.psum(raw_sums.astype(jnp.bfloat16), 'space').astype(jnp.float32)  32.3 us
    all_gather x1, waiting for transfers between devices, carried_in(): everything = lax.all_gather(value, axis)  29.3 us
    ppermute x2, waiting for transfers between devices, from_behind(): return lax.ppermute(block, axis, route)  22.3 us
    ppermute x4, starting transfers between devices, with_halo(): before = lax.ppermute(last, axis, up)  19.6 us
    select_n x4, other arithmetic, per_device(): state = jnp.where(turn < count, fresh, state)  8.74 us
    ppermute x4, waiting for transfers between devices, with_halo(): after = lax.ppermute(initial, axis, down)  8.08 us
    dot_general x4, matrix products, chain_combine(): jnp.dot(later, earlier, precision=lax.Precision.HIGHEST, preferred_elemen...  5.37 us
    ppermute x4, starting transfers between devices, with_halo(): after = lax.ppermute(initial, axis, down)  5.17 us
  transfers between devices with their start and end apart: 12, of which 8 were waited for; matrix products, arithmetic and copies ran while one was open for 1% of the time, Pallas kernels for 0%

commit v1 on v0

v1 whole, which is shorter than its diff:
```python
import math

import jax
import jax.numpy as jnp
from jax import lax
from jax.sharding import PartitionSpec as P

K = 256
BLOCK = 16
STEPS = 4
HALF = K // 2

coupling = 0.35


def swap(value, axis, bit):
    size = lax.axis_size(axis)
    return lax.ppermute(value, axis, [(i, i ^ bit) for i in range(size)])


def exchange_pairs(value, axis, first):
    size = lax.axis_size(axis)
    route = []
    for i in range(first, size - 1, 2):
        route += [(i, i + 1), (i + 1, i)]
    return lax.ppermute(value, axis, route)


def step_once(window, spread, drift):
    wide = window.astype(jnp.float32)
    center = wide[1:-1]
    plus_x = wide[2:]
    minus_x = wide[:-2]
    plus_y = jnp.roll(center, -1, 1)
    minus_y = jnp.roll(center, 1, 1)
    plus_z = jnp.roll(center, -1, 2)
    minus_z = jnp.roll(center, 1, 2)
    laplace = plus_x + minus_x + plus_y + minus_y + plus_z + minus_z - 6.0 * center
    change = (
        drift[0][..., None] * (plus_x - minus_x)
        + drift[1][..., None] * (plus_y - minus_y)
        + drift[2][..., None] * (plus_z - minus_z)
    )
    return (center + spread[..., None] * laplace - 0.5 * change).astype(jnp.bfloat16)


def block_perm(order):
    stored = jnp.arange(K, dtype=jnp.int32)
    which = stored // BLOCK
    onehot = which[:, None] == jnp.arange(order.shape[0], dtype=jnp.int32)[None, :]
    true_col = jnp.sum(jnp.where(onehot, order[None, :], 0), axis=1) * BLOCK + stored % BLOCK
    return (jnp.arange(K, dtype=jnp.int32)[:, None] == true_col[None, :]).astype(jnp.bfloat16)


def order_row(block_order, index):
    return lax.dynamic_slice_in_dim(block_order, index, 1, 0)[0]


def mul(left, right):
    return jnp.dot(left, right, preferred_element_type=jnp.float32)


def to_bf16(value):
    return value.astype(jnp.bfloat16)


def to_f32(value):
    return value.astype(jnp.float32)


def per_device(basis, diffusivity, velocity, step_counts, block_order):
    start = basis[0]
    layers = start.shape[0]
    width = STEPS
    here = lax.axis_index("seg")
    total = lax.axis_size("seg")
    place = lax.axis_index("space")
    slabs = lax.axis_size("space")
    core = place % 2
    cells = start.shape[0] * slabs * start.shape[1] * start.shape[2]
    count = step_counts[0]

    ahead = lax.ppermute(start, "seg", [((i + 1) % total, i) for i in range(total)])
    coefs = jnp.concatenate([diffusivity, velocity[0]], axis=0)
    far = exchange_pairs(start, "space", 1)
    near = exchange_pairs(start, "space", 0)
    far_coefs = exchange_pairs(coefs, "space", 1)
    near_coefs = exchange_pairs(coefs, "space", 0)
    even = core == 0
    before = jnp.where(even, far, near)[-width:]
    after = jnp.where(even, near, far)[:width]
    window = jnp.concatenate([before, start, after], axis=0)
    before_c = jnp.where(even, far_coefs, near_coefs)[:, -width:]
    after_c = jnp.where(even, near_coefs, far_coefs)[:, :width]
    coefs = jnp.concatenate([before_c, coefs, after_c], axis=1)
    for turn in range(STEPS):
        coefs = coefs[:, 1:-1]
        fresh = step_once(window, coefs[0], coefs[1:])
        window = jnp.where(turn < count, fresh, window[1:-1])
    state = window

    raw = lax.dot_general(
        ahead.reshape(-1, K),
        state.reshape(-1, K),
        (((0,), (0,)), ((), ())),
        preferred_element_type=jnp.float32,
    )
    left = block_perm(order_row(block_order, (here + 1) % total))
    right = block_perm(order_row(block_order, here))
    raw = to_bf16(mul(to_bf16(mul(left, to_bf16(raw))), right.T))
    low, high = raw[:, :HALF], raw[:, HALF:]
    mine = jnp.where(even, low, high)
    other = jnp.where(even, high, low)
    own = to_bf16(to_f32(mine) + to_f32(swap(other, "space", 1)))
    bit = 2
    summed = to_f32(own)
    while bit < slabs:
        summed = to_f32(to_bf16(summed))
        summed = summed + to_f32(swap(to_bf16(summed), "space", bit))
        bit *= 2
    half = to_bf16(summed * (coupling / math.sqrt(K * cells)))

    def whole(part):
        rest = swap(part, "space", 1)
        return jnp.where(
            even,
            jnp.concatenate([part, rest], axis=1),
            jnp.concatenate([rest, part], axis=1),
        )

    def my_half(full):
        return jnp.where(even, full[:, :HALF], full[:, HALF:])

    prefix = whole(half)
    block = prefix
    block_half = half
    bit = 1
    while bit < total:
        upper = (here // bit) % 2 == 1
        got = swap(block_half, "seg", bit)
        last = 2 * bit >= total
        if last:
            new = to_f32(my_half(prefix)) + to_f32(got) + mul(prefix, got)
            result = jnp.where(upper, new, to_f32(my_half(prefix)))
        else:
            got = whole(got)
            later = jnp.where(upper, block, got)
            earlier = jnp.where(upper, got, block)
            new = to_bf16(to_f32(later) + to_f32(earlier) + mul(later, earlier))
            extended = to_bf16(to_f32(prefix) + to_f32(got) + mul(prefix, got))
            prefix = jnp.where(upper, extended, prefix)
            block = new
            block_half = my_half(block)
        bit *= 2
    monodromy = whole(result) + jnp.eye(K, dtype=jnp.float32)
    return (state[None], monodromy[None])


def solution(mesh):
    in_specs = (
        P(("groups", "seg"), "space", None, None, None),
        P(("groups", "seg"), "space", None, None),
        P(("groups", "seg"), None, "space", None, None),
        P(("groups", "seg")),
        P("groups", None),
    )
    out_specs = (P(("groups", "seg"), "space", None, None, None), P(("groups", "seg"), None, None))
    return jax.shard_map(
        per_device, mesh=mesh, in_specs=in_specs, out_specs=out_specs, check_vma=False
    )
```

time: 164 us -> 58.7 us (0.36)
  waiting for transfers between devices: 91.9 us -> 12.6 us
  between operations: 15.1 us -> 1.75 us
  starting transfers between devices: 29.8 us -> 18 us
  matrix products: 9.01 us -> 1.46 us
  other arithmetic: 10.8 us -> 16.3 us
    psum x1 -> x0, waiting for transfers between devices: 32.3 us -> none  [per_device(): lax.psum(raw_sums.astype(jnp.bfloat16), 'space').astype(jnp.float32)]
    all_gather x1 -> x0, waiting for transfers between devices: 29.3 us -> none  [carried_in(): everything = lax.all_gather(value, axis)]
    ppermute x10 -> x12, waiting for transfers between devices: 30.3 us -> 12.6 us  [the longest x7 12.6 us: swap(): return lax.ppermute(value, axis, [(i, i ^ bit) for i in range(size)])]
    ppermute x10 -> x12, starting transfers between devices: 29.8 us -> 18 us  [the longest x7 7.21 us: swap(): return lax.ppermute(value, axis, [(i, i ^ bit) for i in range(size)])]
    convert_element_type x4, other arithmetic: 1.89 us -> 12.4 us  [step_once(): wide = window.astype(jnp.float32)]
    dot_general x8 -> x5, matrix products: 9.01 us -> 1.46 us  [the longest x4 1.04 us: mul(): return jnp.dot(left, right, preferred_element_type=jnp.float32)]
    select_n x4 -> x5, other arithmetic: 8.74 us -> 2.23 us  [the longest x1 2.09 us: per_device(): window = jnp.where(turn < count, fresh, window[1:-1])]
  transfers between devices with their start and end apart: 12 -> 12, of which waited for: 8 -> 6; matrix products, arithmetic and copies ran while one was open for 1% -> 41% of each run, Pallas kernels for 0% -> 0%
where the time goes in v1:
time: 58.7 us; the launch traced here: 58.3 us
  starting transfers between devices  18 us (31%)
  other arithmetic  16.3 us (28%)
  waiting for transfers between devices  12.6 us (21%)
  local copies, waits for them, and re-layouts  8.17 us (14%)
  between operations  1.75 us (3%)
  matrix products  1.46 us (2%)
    ppermute x7, waiting for transfers between devices, swap(): return lax.ppermute(value, axis, [(i, i ^ bit) for i in range(size)])  12.6 us
    convert_element_type x4, other arithmetic, step_once(): wide = window.astype(jnp.float32)  12.4 us
    ppermute x7, starting transfers between devices, swap(): return lax.ppermute(value, axis, [(i, i ^ bit) for i in range(size)])  7.21 us
    ppermute x4, starting transfers between devices, exchange_pairs(): return lax.ppermute(value, axis, route)  7.15 us
    ppermute x1, starting transfers between devices, per_device(): lax.ppermute(start, 'seg', [((i + 1) % total, i) for i in range(total)])  3.6 us
    slice x8, local copies, waits for them, and re-layouts, step_once(): plus_y = jnp.roll(center, -1, 1)  2.62 us
    slice x8, local copies, waits for them, and re-layouts, step_once(): plus_z = jnp.roll(center, -1, 2)  2.39 us
    select_n x1, other arithmetic, per_device(): window = jnp.where(turn < count, fresh, window[1:-1])  2.09 us
  transfers between devices with their start and end apart: 12, of which 6 were waited for; matrix products, arithmetic and copies ran while one was open for 41% of the time, Pallas kernels for 0%

profile of v1, /device:TPU:0, one launch (start us, length us, event | category | flops | bytes accessed | tf_op | source)
XLA Modules:
  0.0 58.3 jit_solution(7931496506556318071)
XLA Ops:
  0.6 0.8 %collective-permute-start = (bf16[4,3,128,256]{3,2,1,0:T(8,128)(2,1)}, bf16[4,3,128,256]{3,2,1,0:T(8,128)(2,1)S(1)}, u32[]{:S(2)}, u32[]{:S(2)}) collective-permute-start(bf16[4,3,128,256]{3,2,1,0:T(8,128)(2,1)} %bitcast.55), channel_id=1, source_target_pairs={{1,2},{2,1},{5,6},{6,5},{9,10},{10,9},{13,14},{14,13},{17,18},{18,... | collective-permute-start | bytes 2359304 | tf_op jit(solution)/shard_map/ppermute | solution.py:26
  1.5 4.3 %collective-permute-start.1 = (bf16[4,3,128,256]{3,2,1,0:T(8,128)(2,1)}, bf16[4,3,128,256]{3,2,1,0:T(8,128)(2,1)S(1)}, u32[]{:S(2)}, u32[]{:S(2)}) collective-permute-start(bf16[4,3,128,256]{3,2,1,0:T(8,128)(2,1)} %bitcast.56), channel_id=1, source_target_pairs={{0,1},{1,0},{2,3},{3,2},{4,5},{5,4},{6,7},{7,6},{8,9},{9,8},{10,11... | collective-permute-start | bytes 2359304 | tf_op jit(solution)/shard_map/ppermute | solution.py:26
  5.8 0.7 %pad_maximum_fusion.18 = f32[4,4,3,128]{3,1,2,0:T(4,128)S(1)} fusion(f32[3,4,3,128]{3,1,2,0:T(4,128)} %bitcast.60, f32[1,4,3,128]{3,1,2,0:T(4,128)} %param.6), kind=kLoop, calls=%fused_computation.60 | loop fusion | flops 6144 | bytes 49152 | tf_op jit(solution)/shard_map/concatenate | solution.py:84
  6.5 0.7 %collective-permute-start.2 = (f32[4,4,3,128]{3,1,2,0:T(4,128)S(1)}, f32[4,4,3,128]{3,1,2,0:T(4,128)S(1)}, u32[]{:S(2)}, u32[]{:S(2)}) collective-permute-start(f32[4,4,3,128]{3,1,2,0:T(4,128)S(1)} %pad_maximum_fusion.18), channel_id=1, source_target_pairs={{1,2},{2,1},{5,6},{6,5},{9,10},{10,9},{13,14},{14,13},{17,18},{18,... | collective-permute-start | bytes 73736 | tf_op jit(solution)/shard_map/ppermute | solution.py:26
  7.2 1.3 %collective-permute-start.3 = (f32[4,4,3,128]{3,1,2,0:T(4,128)S(1)}, f32[4,4,3,128]{3,1,2,0:T(4,128)S(1)}, u32[]{:S(2)}, u32[]{:S(2)}) collective-permute-start(f32[4,4,3,128]{3,1,2,0:T(4,128)S(1)} %pad_maximum_fusion.18), channel_id=1, source_target_pairs={{0,1},{1,0},{2,3},{3,2},{4,5},{5,4},{6,7},{7,6},{8,9},{9,8},{10,11... | collective-permute-start | bytes 73736 | tf_op jit(solution)/shard_map/ppermute | solution.py:26
  8.5 3.6 %collective-permute-start.4 = (bf16[4,3,128,256]{3,2,1,0:T(8,128)(2,1)}, bf16[4,3,128,256]{3,2,1,0:T(8,128)(2,1)S(1)}, u32[]{:S(2)}, u32[]{:S(2)}) collective-permute-start(bf16[4,3,128,256]{3,2,1,0:T(8,128)(2,1)} %bitcast.57), channel_id=1, source_target_pairs={{4,0},{8,4},{12,8},{0,12},{5,1},{9,5},{13,9},{1,13},{6,2},{10,6},{... | collective-permute-start | bytes 2359304 | tf_op jit(solution)/shard_map/ppermute | solution.py:83
  12.1 0.7 %slice_bitcast_fusion.14 = (f32[4,3,128]{2,0,1:T(4,128)S(1)}, f32[4,3,128]{2,0,1:T(4,128)S(1)}, f32[4,3,128]{2,0,1:T(4,128)S(1)}) fusion(f32[1,3,4,3,128]{4,2,3,1,0:T(4,128)} %param.7), kind=kLoop, calls=%fused_computation.76 | loop fusion | bytes 36864 | tf_op jit(solution)/shard_map/mul | solution.py:40
  12.9 0.8 %dynamic-slice_bitcast_fusion = (s32[16]{0:T(128)S(1)}, s32[16]{0:T(128)S(1)}) fusion(s32[4,16]{1,0:T(4,128)} %param.9, s32[]{:T(128)S(6)} %select_n.219, s32[]{:T(128)S(6)} %select_n.216), kind=kLoop, calls=%fused_computation.86 | loop fusion | bytes 264 | tf_op jit(solution)/shard_map/jit(_where)/broadcast_in_dim | solution.py:51
  14.4 0.7 %copy.37 = f32[4,3,128]{2,1,0:T(4,128)S(1)} copy(f32[4,3,128]{2,0,1:T(4,128)} %bitcast.64) | data formatting | bytes 12288 | tf_op jit(solution)/shard_map/mul | solution.py:44
  15.2 0.7 %pad_maximum_fusion.17 = f32[4,12,3,128]{3,1,2,0:T(8,128)S(1)} fusion(f32[4,4,3,128]{3,1,2,0:T(4,128)S(1)} %get-tuple-element.63, f32[3,4,3,128]{3,1,2,0:T(4,128)} %bitcast.61, f32[1,4,3,128]{3,1,2,0:T(4,128)} %param.6, f32[4,4,3,128]{3,1,2,0:T(4,128)S(1)} %get-tuple-element.62), kind=kLoop, calls=%fused_computation.52 | loop fusion | flops 55296 | bytes 147456 | tf_op jit(solution)/shard_map/concatenate | solution.py:95
  16.3 0.5 fusion.14
  16.8 0.9 %fusion.20 = (f32[10,3,127,256]{3,2,1,0:T(8,128)S(1)}, f32[10,3,127,256]{3,2,1,0:T(8,128)S(1)}) fusion(f32[12,3,128,256]{3,2,1,0:T(8,128)S(1)} %get-tuple-element.22), kind=kLoop, calls=%fused_computation.95 | loop fusion | bytes 15605760 | tf_op jit(solution)/shard_map/jit(_roll_static)/slice | solution.py:36
  17.7 0.8 %fusion.18 = (f32[10,2,128,256]{3,2,1,0:T(8,128)S(1)}, f32[10,2,128,256]{3,2,1,0:T(8,128)S(1)}) fusion(f32[12,3,128,256]{3,2,1,0:T(8,128)S(1)} %get-tuple-element.22), kind=kLoop, calls=%fused_computation.93 | loop fusion | bytes 10485760 | tf_op jit(solution)/shard_map/jit(_roll_static)/slice | solution.py:34
  18.8 5.0 %fusion.17 = (f32[10,3,128,256]{3,2,1,0:T(8,128)S(1)}, bf16[10,3,128,256]{3,2,1,0:T(8,128)(2,1)S(1)}) fusion(bf16[12,3,128,256]{3,2,1,0:T(8,128)(2,1)S(1)} %get-tuple-element.23, f32[10,3,128]{2,1,0:T(4,128)S(1)} %copy.28, f32[10,3,128]{2,1,0:T(4,128)S(1)} %copy.27, f32[10,3,128]{2,1,0:T(4,128)S(1)} %copy.26, f32[10,3,127,256]{3,2,1,0:T(8,128)S(1)} %get-tuple-element.19, ...), kind=kLoop, calls=%fused_computation.92 | loop fusion | flops 25559040 | bytes 35450880 | tf_op jit(solution)/shard_map/convert_element_type | solution.py:30
  23.8 0.6 %fusion.24 = (f32[8,3,127,256]{3,2,1,0:T(8,128)S(1)}, f32[8,3,127,256]{3,2,1,0:T(8,128)S(1)}) fusion(bf16[10,3,128,256]{3,2,1,0:T(8,128)(2,1)S(1)} %get-tuple-element.13), kind=kLoop, calls=%fused_computation.99 | loop fusion | bytes 12484608 | tf_op jit(solution)/shard_map/jit(_roll_static)/slice | solution.py:36
  24.4 0.5 fusion.22
  25.2 4.0 %fusion.16 = (f32[8,3,128,256]{3,2,1,0:T(8,128)S(1)}, bf16[8,3,128,256]{3,2,1,0:T(8,128)(2,1)S(1)}) fusion(bf16[10,3,128,256]{3,2,1,0:T(8,128)(2,1)S(1)} %get-tuple-element.13, f32[8,3,128]{2,1,0:T(4,128)S(1)} %copy.32, f32[8,3,128]{2,1,0:T(4,128)S(1)} %copy.31, f32[8,3,128]{2,1,0:T(4,128)S(1)} %copy.30, f32[8,3,127,256]{3,2,1,0:T(8,128)S(1)} %get-tuple-element.29, ...), kind=kLoop, calls=%fused_computation.91 | loop fusion | flops 20447232 | bytes 28360704 | tf_op jit(solution)/shard_map/convert_element_type | solution.py:30
  29.2 0.5 fusion.28
  30.2 3.0 %fusion.15 = (f32[6,3,128,256]{3,2,1,0:T(8,128)S(1)}, bf16[6,3,128,256]{3,2,1,0:T(8,128)(2,1)S(1)}) fusion(bf16[8,3,128,256]{3,2,1,0:T(8,128)(2,1)S(1)} %get-tuple-element.11, f32[6,3,128]{2,1,0:T(4,128)S(1)} %copy.36, f32[6,3,128]{2,1,0:T(4,128)S(1)} %copy.35, f32[6,3,128]{2,1,0:T(4,128)S(1)} %copy.34, f32[6,3,127,256]{3,2,1,0:T(8,128)S(1)} %get-tuple-element.37, ...), kind=kLoop, calls=%fused_computation.90 | loop fusion | flops 15335424 | bytes 21270528 | tf_op jit(solution)/shard_map/convert_element_type | solution.py:30
  33.8 2.1 %slice_select_fusion.3 = bf16[4,3,128,256]{3,2,1,0:T(8,128)(2,1)S(1)} fusion(bf16[6,3,128,256]{3,2,1,0:T(8,128)(2,1)S(1)} %get-tuple-element.9, pred[]{:T(512)} %bitcast, f32[4,3,128]{2,1,0:T(4,128)S(1)} %copy.40, f32[4,3,128]{2,1,0:T(4,128)S(1)} %copy.39, f32[4,3,128]{2,1,0:T(4,128)S(1)} %copy.38, f32[4,3,127,256]{3,2,1,0:T(8,128)S(1)} %get-tuple-element.47, ...), kind=kLoop, calls=%fused_computation.30 | loop fusion | flops 9830400 | bytes 12607489 | tf_op jit(solution)/shard_map/jit(_where)/select_n | solution.py:99
  36.4 0.4 convolution_convert_fusion
  36.8 1.1 %collective-permute-start.5 = (bf16[256,128]{0,1:T(8,128)(2,1)S(1)}, bf16[256,128]{0,1:T(8,128)(2,1)S(1)}, u32[]{:S(2)}, u32[]{:S(2)}) collective-permute-start(bf16[256,128]{0,1:T(8,128)(2,1)S(1)} %broadcast_select_fusion.2), channel_id=1, source_target_pairs={{0,1},{1,0},{2,3},{3,2},{4,5},{5,4},{6,7},{7,6},{8,9},{9,8},{10,11... | collective-permute-start | bytes 196616 | tf_op jit(solution)/shard_map/ppermute | solution.py:18
  37.9 0.9 %collective-permute-done.5 = bf16[256,128]{0,1:T(8,128)(2,1)S(1)} collective-permute-done((bf16[256,128]{0,1:T(8,128)(2,1)S(1)}, bf16[256,128]{0,1:T(8,128)(2,1)S(1)}, u32[]{:S(2)}, u32[]{:S(2)}) %collective-permute-start.5) | collective-permute-done | bytes 65568 | tf_op jit(solution)/shard_map/ppermute | solution.py:18
  38.9 1.7 %collective-permute-start.6 = (bf16[256,128]{0,1:T(8,128)(2,1)S(1)}, bf16[256,128]{0,1:T(8,128)(2,1)S(1)}, u32[]{:S(2)}, u32[]{:S(2)}) collective-permute-start(bf16[256,128]{0,1:T(8,128)(2,1)S(1)} %add_convert_fusion.1), channel_id=1, source_target_pairs={{0,2},{1,3},{2,0},{3,1},{4,6},{5,7},{6,4},{7,5},{8,10},{9,11},{10,... | collective-permute-start | bytes 196616 | tf_op jit(solution)/shard_map/ppermute | solution.py:18
  40.6 2.7 %collective-permute-done.6 = bf16[256,128]{0,1:T(8,128)(2,1)S(1)} collective-permute-done((bf16[256,128]{0,1:T(8,128)(2,1)S(1)}, bf16[256,128]{0,1:T(8,128)(2,1)S(1)}, u32[]{:S(2)}, u32[]{:S(2)}) %collective-permute-start.6) | collective-permute-done | bytes 65568 | tf_op jit(solution)/shard_map/ppermute | solution.py:18
  43.3 1.6 %collective-permute-start.8 = (bf16[256,128]{0,1:T(8,128)(2,1)S(1)}, bf16[256,128]{0,1:T(8,128)(2,1)S(1)}, u32[]{:S(2)}, u32[]{:S(2)}) collective-permute-start(bf16[256,128]{0,1:T(8,128)(2,1)S(1)} %multiply_convert_fusion), channel_id=1, source_target_pairs={{0,4},{4,0},{8,12},{12,8},{1,5},{5,1},{9,13},{13,9},{2,6},{6,2},{1... | collective-permute-start | bytes 196616 | tf_op jit(solution)/shard_map/ppermute | solution.py:18
  45.0 2.7 %collective-permute-done.8 = bf16[256,128]{0,1:T(8,128)(2,1)S(1)} collective-permute-done((bf16[256,128]{0,1:T(8,128)(2,1)S(1)}, bf16[256,128]{0,1:T(8,128)(2,1)S(1)}, u32[]{:S(2)}, u32[]{:S(2)}) %collective-permute-start.8) | collective-permute-done | bytes 65568 | tf_op jit(solution)/shard_map/ppermute | solution.py:18
  47.7 1.2 %collective-permute-done.9 = bf16[256,128]{0,1:T(8,128)(2,1)S(1)} collective-permute-done((bf16[256,128]{0,1:T(8,128)(2,1)S(1)}, bf16[256,128]{0,1:T(8,128)(2,1)S(1)}, u32[]{:S(2)}, u32[]{:S(2)}) %collective-permute-start.9) | collective-permute-done | bytes 65568 | tf_op jit(solution)/shard_map/ppermute | solution.py:18
  49.2 2.7 %collective-permute-start.10 = (bf16[256,128]{0,1:T(8,128)(2,1)S(1)}, bf16[256,128]{0,1:T(8,128)(2,1)S(1)}, u32[]{:S(2)}, u32[]{:S(2)}) collective-permute-start(bf16[256,128]{0,1:T(8,128)(2,1)S(1)} %slice_select_fusion.4), channel_id=1, source_target_pairs={{0,8},{4,12},{8,0},{12,4},{1,9},{5,13},{9,1},{13,5},{2,10},{6,14},... | collective-permute-start | bytes 196616 | tf_op jit(solution)/shard_map/ppermute | solution.py:18
  52.0 3.8 %collective-permute-done.10 = bf16[256,128]{0,1:T(8,128)(2,1)S(1)} collective-permute-done((bf16[256,128]{0,1:T(8,128)(2,1)S(1)}, bf16[256,128]{0,1:T(8,128)(2,1)S(1)}, u32[]{:S(2)}, u32[]{:S(2)}) %collective-permute-start.10) | collective-permute-done | bytes 65568 | tf_op jit(solution)/shard_map/ppermute | solution.py:18
  56.1 1.3 %collective-permute-done.11 = f32[256,128]{0,1:T(8,128)S(1)} collective-permute-done((f32[256,128]{0,1:T(8,128)S(1)}, f32[256,128]{0,1:T(8,128)S(1)}, u32[]{:S(2)}, u32[]{:S(2)}) %collective-permute-start.11) | collective-permute-done | bytes 131104 | tf_op jit(solution)/shard_map/ppermute | solution.py:18
  57.4 0.8 %copy.42 = f32[1,256,256]{2,1,0:T(8,128)} copy(f32[1,256,256]{1,2,0:T(8,128)S(1)} %fusion.2) | data formatting | bytes 524288
  (56 shorter events, 3.3 us)
Async XLA Ops:
  0.6 15.6 %copy-start = (bf16[1,4,3,128,256]{4,3,2,1,0:T(8,128)(2,1)S(1)}, bf16[1,4,3,128,256]{4,3,2,1,0:T(8,128)(2,1)}, u32[]{:S(2)}) copy-start(bf16[1,4,3,128,256]{4,3,2,1,0:T(8,128)(2,1)} %param.5) | copy-start | bytes 2359300
  0.6 15.5 %collective-permute-start = (bf16[4,3,128,256]{3,2,1,0:T(8,128)(2,1)}, bf16[4,3,128,256]{3,2,1,0:T(8,128)(2,1)S(1)}, u32[]{:S(2)}, u32[]{:S(2)}) collective-permute-start(bf16[4,3,128,256]{3,2,1,0:T(8,128)(2,1)} %bitcast.55), channel_id=1, source_target_pairs={{1,2},{2,1},{5,6},{6,5},{9,10},{10,9},{13,14},{14,13},{17,18},{18,... | collective-permute-start | bytes 2359304 | tf_op jit(solution)/shard_map/ppermute | solution.py:26
  1.5 14.7 %collective-permute-start.1 = (bf16[4,3,128,256]{3,2,1,0:T(8,128)(2,1)}, bf16[4,3,128,256]{3,2,1,0:T(8,128)(2,1)S(1)}, u32[]{:S(2)}, u32[]{:S(2)}) collective-permute-start(bf16[4,3,128,256]{3,2,1,0:T(8,128)(2,1)} %bitcast.56), channel_id=1, source_target_pairs={{0,1},{1,0},{2,3},{3,2},{4,5},{5,4},{6,7},{7,6},{8,9},{9,8},{10,11... | collective-permute-start | bytes 2359304 | tf_op jit(solution)/shard_map/ppermute | solution.py:26
  6.5 8.6 %collective-permute-start.2 = (f32[4,4,3,128]{3,1,2,0:T(4,128)S(1)}, f32[4,4,3,128]{3,1,2,0:T(4,128)S(1)}, u32[]{:S(2)}, u32[]{:S(2)}) collective-permute-start(f32[4,4,3,128]{3,1,2,0:T(4,128)S(1)} %pad_maximum_fusion.18), channel_id=1, source_target_pairs={{1,2},{2,1},{5,6},{6,5},{9,10},{10,9},{13,14},{14,13},{17,18},{18,... | collective-permute-start | bytes 73736 | tf_op jit(solution)/shard_map/ppermute | solution.py:26
  7.2 7.9 %collective-permute-start.3 = (f32[4,4,3,128]{3,1,2,0:T(4,128)S(1)}, f32[4,4,3,128]{3,1,2,0:T(4,128)S(1)}, u32[]{:S(2)}, u32[]{:S(2)}) collective-permute-start(f32[4,4,3,128]{3,1,2,0:T(4,128)S(1)} %pad_maximum_fusion.18), channel_id=1, source_target_pairs={{0,1},{1,0},{2,3},{3,2},{4,5},{5,4},{6,7},{7,6},{8,9},{9,8},{10,11... | collective-permute-start | bytes 73736 | tf_op jit(solution)/shard_map/ppermute | solution.py:26
  8.5 27.4 %collective-permute-start.4 = (bf16[4,3,128,256]{3,2,1,0:T(8,128)(2,1)}, bf16[4,3,128,256]{3,2,1,0:T(8,128)(2,1)S(1)}, u32[]{:S(2)}, u32[]{:S(2)}) collective-permute-start(bf16[4,3,128,256]{3,2,1,0:T(8,128)(2,1)} %bitcast.57), channel_id=1, source_target_pairs={{4,0},{8,4},{12,8},{0,12},{5,1},{9,5},{13,9},{1,13},{6,2},{10,6},{... | collective-permute-start | bytes 2359304 | tf_op jit(solution)/shard_map/ppermute | solution.py:83
  35.9 13.2 %copy-start.1 = (bf16[4,3,128,256]{3,2,1,0:T(8,128)(2,1)}, bf16[4,3,128,256]{3,2,1,0:T(8,128)(2,1)S(1)}, u32[]{:S(2)}) copy-start(bf16[4,3,128,256]{3,2,1,0:T(8,128)(2,1)S(1)} %slice_select_fusion.3) | copy-start | bytes 2359300
  36.8 2.0 %collective-permute-start.5 = (bf16[256,128]{0,1:T(8,128)(2,1)S(1)}, bf16[256,128]{0,1:T(8,128)(2,1)S(1)}, u32[]{:S(2)}, u32[]{:S(2)}) collective-permute-start(bf16[256,128]{0,1:T(8,128)(2,1)S(1)} %broadcast_select_fusion.2), channel_id=1, source_target_pairs={{0,1},{1,0},{2,3},{3,2},{4,5},{5,4},{6,7},{7,6},{8,9},{9,8},{10,11... | collective-permute-start | bytes 196616 | tf_op jit(solution)/shard_map/ppermute | solution.py:18
  38.9 4.4 %collective-permute-start.6 = (bf16[256,128]{0,1:T(8,128)(2,1)S(1)}, bf16[256,128]{0,1:T(8,128)(2,1)S(1)}, u32[]{:S(2)}, u32[]{:S(2)}) collective-permute-start(bf16[256,128]{0,1:T(8,128)(2,1)S(1)} %add_convert_fusion.1), channel_id=1, source_target_pairs={{0,2},{1,3},{2,0},{3,1},{4,6},{5,7},{6,4},{7,5},{8,10},{9,11},{10,... | collective-permute-start | bytes 196616 | tf_op jit(solution)/shard_map/ppermute | solution.py:18
  43.3 4.3 %collective-permute-start.8 = (bf16[256,128]{0,1:T(8,128)(2,1)S(1)}, bf16[256,128]{0,1:T(8,128)(2,1)S(1)}, u32[]{:S(2)}, u32[]{:S(2)}) collective-permute-start(bf16[256,128]{0,1:T(8,128)(2,1)S(1)} %multiply_convert_fusion), channel_id=1, source_target_pairs={{0,4},{4,0},{8,12},{12,8},{1,5},{5,1},{9,13},{13,9},{2,6},{6,2},{1... | collective-permute-start | bytes 196616 | tf_op jit(solution)/shard_map/ppermute | solution.py:18
  45.0 2.7 %collective-permute-start.7 = (bf16[256,128]{0,1:T(8,128)(2,1)S(1)}, bf16[256,128]{0,1:T(8,128)(2,1)S(1)}, u32[]{:S(2)}, u32[]{:S(2)}) collective-permute-start(bf16[256,128]{0,1:T(8,128)(2,1)S(1)} %multiply_convert_fusion), channel_id=1, source_target_pairs={{0,1},{1,0},{2,3},{3,2},{4,5},{5,4},{6,7},{7,6},{8,9},{9,8},{10,11... | collective-permute-start | bytes 196616 | tf_op jit(solution)/shard_map/ppermute | solution.py:18
  47.7 1.3 %collective-permute-start.9 = (bf16[256,128]{0,1:T(8,128)(2,1)S(1)}, bf16[256,128]{0,1:T(8,128)(2,1)S(1)}, u32[]{:S(2)}, u32[]{:S(2)}) collective-permute-start(bf16[256,128]{0,1:T(8,128)(2,1)S(1)} %collective-permute-done.8), channel_id=1, source_target_pairs={{0,1},{1,0},{2,3},{3,2},{4,5},{5,4},{6,7},{7,6},{8,9},{9,8},{10,11... | collective-permute-start | bytes 196616 | tf_op jit(solution)/shard_map/ppermute | solution.py:18
  49.2 6.6 %collective-permute-start.10 = (bf16[256,128]{0,1:T(8,128)(2,1)S(1)}, bf16[256,128]{0,1:T(8,128)(2,1)S(1)}, u32[]{:S(2)}, u32[]{:S(2)}) collective-permute-start(bf16[256,128]{0,1:T(8,128)(2,1)S(1)} %slice_select_fusion.4), channel_id=1, source_target_pairs={{0,8},{4,12},{8,0},{12,4},{1,9},{5,13},{9,1},{13,5},{2,10},{6,14},... | collective-permute-start | bytes 196616 | tf_op jit(solution)/shard_map/ppermute | solution.py:18
  56.0 1.4 %collective-permute-start.11 = (f32[256,128]{0,1:T(8,128)S(1)}, f32[256,128]{0,1:T(8,128)S(1)}, u32[]{:S(2)}, u32[]{:S(2)}) collective-permute-start(f32[256,128]{0,1:T(8,128)S(1)} %convert_select_fusion), channel_id=1, source_target_pairs={{0,1},{1,0},{2,3},{3,2},{4,5},{5,4},{6,7},{7,6},{8,9},{9,8},{10,11... | collective-permute-start | bytes 393224 | tf_op jit(solution)/shard_map/ppermute | solution.py:18

commit v2 on v1

--- a/solution.py
+++ b/solution.py
@@ -3,6 +3,8 @@
 import jax
 import jax.numpy as jnp
 from jax import lax
+from jax.experimental import pallas as pl
+from jax.experimental.pallas import tpu as pltpu
 from jax.sharding import PartitionSpec as P
 
 K = 256
@@ -26,22 +28,192 @@
     return lax.ppermute(value, axis, route)
 
 
-def step_once(window, spread, drift):
-    wide = window.astype(jnp.float32)
-    center = wide[1:-1]
-    plus_x = wide[2:]
-    minus_x = wide[:-2]
-    plus_y = jnp.roll(center, -1, 1)
-    minus_y = jnp.roll(center, 1, 1)
-    plus_z = jnp.roll(center, -1, 2)
-    minus_z = jnp.roll(center, 1, 2)
-    laplace = plus_x + minus_x + plus_y + minus_y + plus_z + minus_z - 6.0 * center
-    change = (
-        drift[0][..., None] * (plus_x - minus_x)
-        + drift[1][..., None] * (plus_y - minus_y)
-        + drift[2][..., None] * (plus_z - minus_z)
-    )
-    return (center + spread[..., None] * laplace - 0.5 * change).astype(jnp.bfloat16)
+ROWS = 144
+TOP = 8
+CHUNK = 16
+FIELDS = 4
+NEAR_LAYERS = (6, 4, 2)
+
+
+def spread_coefs(columns, column, flip, out, plane):
+    def field(k):
+        return jnp.broadcast_to(columns[:, column + k : column + k + 1], (columns.shape[0], HALF))
+
+    diffusion = field(0)
+    along_u = -field(1) if flip else field(1)
+    along_y = field(2)
+    along_z = field(3)
+    out[plane, 0] = 1.0 - 6.0 * diffusion
+    out[plane, 1] = diffusion - along_u
+    out[plane, 2] = diffusion + along_u
+    out[plane, 3] = diffusion - along_y
+    out[plane, 4] = diffusion + along_y
+    out[plane, 5] = diffusion - along_z
+    out[plane, 6] = diffusion + along_z
+
+
+def unpack_layer(source, index, dest, slot):
+    ys, zs = source.shape[1], source.shape[2]
+    for y in range(ys):
+        for h in range(2):
+            lanes = slice(h * HALF, (h + 1) * HALF)
+            value = source[index, y, :, lanes].astype(jnp.float32)
+            dest[slot, y, h, TOP : TOP + zs, :] = value
+            dest[slot, y, h, TOP - 1 : TOP, :] = value[zs - 1 : zs]
+            dest[slot, y, h, TOP + zs : TOP + zs + 1, :] = value[0:1]
+
+
+def step_layer(source, index, coefs, layer, active, store):
+    ys = source.shape[1]
+    zs = coefs.shape[2]
+    for y in range(ys):
+        above, below = (y + 1) % ys, (y + ys - 1) % ys
+        for z in range(0, zs, CHUNK):
+            factor = [coefs[layer * ys + y, k, z : z + CHUNK, :] for k in range(7)]
+            rows = slice(TOP + z, TOP + z + CHUNK)
+            for h in range(2):
+                center = source[index, y, h, rows, :]
+                new = factor[0] * center
+                new += factor[1] * source[index + 1, y, h, rows, :]
+                new += factor[2] * source[index - 1, y, h, rows, :]
+                new += factor[3] * source[index, above, h, rows, :]
+                new += factor[4] * source[index, below, h, rows, :]
+                new += factor[5] * source[index, y, h, TOP + z + 1 : TOP + z + CHUNK + 1, :]
+                new += factor[6] * source[index, y, h, TOP + z - 1 : TOP + z + CHUNK - 1, :]
+                if active is not None:
+                    new = jnp.where(active, new, center)
+                store(y, h, z, new.astype(jnp.bfloat16))
+
+
+def into_level(dest, slot, zs):
+    def store(y, h, z, rows):
+        wide = rows.astype(jnp.float32)
+        dest[slot, y, h, TOP + z : TOP + z + CHUNK, :] = wide
+        if z == 0:
+            dest[slot, y, h, TOP + zs : TOP + zs + 1, :] = wide[0:1]
+        if z + CHUNK == zs:
+            dest[slot, y, h, TOP - 1 : TOP, :] = wide[CHUNK - 1 : CHUNK]
+
+    return store
+
+
+def near_kernel(info, near, own, near_coefs, own_coefs, mid1, mid2, mid3, level0, level1, level2, level3, coefs):
+    odd = info[0]
+    count = info[1]
+    ys, zs = own.shape[1], own.shape[2]
+    group = ys * FIELDS
+    table = jnp.concatenate(
+        [own_coefs[...], near_coefs[...], jnp.zeros((128 - 2 * 4 * group, zs), jnp.float32)], axis=0
+    ).T
+    for j in range(6):
+        u = j - 3
+        for y in range(ys):
+            if u < 0:
+                spread_coefs(table, (4 + (-1 - u)) * group + y * FIELDS, True, coefs, j * ys + y)
+            else:
+                spread_coefs(table, u * group + y * FIELDS, False, coefs, j * ys + y)
+
+    def fill(k, _):
+        flipped = jnp.where(odd == 1, 3 - k, k)
+        unpack_layer(near, flipped, level0, 3 - k)
+        unpack_layer(own, 3 - flipped, level0, 4 + k)
+        return 0
+
+    lax.fori_loop(0, 4, fill, 0)
+    levels = (level0, level1, level2, level3)
+    for t, layers in enumerate(NEAR_LAYERS):
+        source, dest = levels[t], levels[t + 1]
+        active = None if t < 2 else count > t
+
+        def one(j, _):
+            step_layer(source, j + 1, coefs, j + t, active, into_level(dest, j, zs))
+            return 0
+
+        lax.fori_loop(0, layers, one, 0)
+    mid1[...] = level1[4:6]
+    mid2[...] = level2[2:4]
+    mid3[...] = level3[...]
+
+
+def far_kernel(info, own, far, own_coefs, far_coefs, mid1, mid2, mid3, out, level0, level1, level2, level3, coefs):
+    odd = info[0]
+    count = info[1]
+    ys, zs = own.shape[1], own.shape[2]
+    group = ys * FIELDS
+    table = jnp.concatenate(
+        [own_coefs[...], far_coefs[...], jnp.zeros((128 - 2 * 4 * group, zs), jnp.float32)], axis=0
+    ).T
+    for u in range(7):
+        for y in range(ys):
+            if u < 4:
+                spread_coefs(table, u * group + y * FIELDS, False, coefs, u * ys + y)
+            else:
+                spread_coefs(table, (4 + 7 - u) * group + y * FIELDS, True, coefs, u * ys + y)
+
+    def fill_own(k, _):
+        unpack_layer(own, jnp.where(odd == 1, 2 + k, 1 - k), level0, k)
+        return 0
+
+    def fill_far(k, _):
+        unpack_layer(far, jnp.where(odd == 1, k, 3 - k), level0, 2 + k)
+        return 0
+
+    lax.fori_loop(0, 2, fill_own, 0)
+    lax.fori_loop(0, 4, fill_far, 0)
+    level1[0:2] = mid1[...]
+    level2[0:2] = mid2[...]
+    level3[0:2] = mid3[...]
+    levels = (level0, level1, level2, level3)
+    for t in range(STEPS):
+        source = levels[t]
+        active = None if t < 2 else count > t
+
+        def one(j, _):
+            if t < STEPS - 1:
+                store = into_level(levels[t + 1], 2 + j, zs)
+            else:
+                layer = jnp.where(odd == 1, j, 3 - j)
+
+                def store(y, h, z, rows):
+                    out[layer, y, z : z + CHUNK, h * HALF : (h + 1) * HALF] = rows
+
+            step_layer(source, 1 + j, coefs, 3 - t + j, active, store)
+            return 0
+
+        lax.fori_loop(0, 4, one, 0)
+
+
+def run_steps(info, near, own, far, near_coefs, own_coefs, far_coefs):
+    ys, zs = own.shape[1], own.shape[2]
+    vmem = pl.BlockSpec(memory_space=pltpu.VMEM)
+    smem = pl.BlockSpec(memory_space=pltpu.SMEM)
+    work = ys * zs * K
+
+    def level(layers):
+        return pltpu.VMEM((layers, ys, 2, ROWS, HALF), jnp.float32)
+
+    def factors(layers):
+        return pltpu.VMEM((layers * ys, 7, zs, HALF), jnp.float32)
+
+    mid = jax.ShapeDtypeStruct((2, ys, 2, ROWS, HALF), jnp.float32)
+    mids = pl.pallas_call(
+        near_kernel,
+        out_shape=(mid, mid, mid),
+        in_specs=[smem] + [vmem] * 4,
+        out_specs=(vmem,) * 3,
+        scratch_shapes=[level(8), level(6), level(4), level(2), factors(6)],
+        compiler_params=pltpu.CompilerParams(vmem_limit_bytes=36 * 2**20),
+        cost_estimate=pl.CostEstimate(flops=12 * 20 * work, bytes_accessed=8 * 2**20, transcendentals=0),
+    )(info, near, own, near_coefs, own_coefs)
+    return pl.pallas_call(
+        far_kernel,
+        out_shape=jax.ShapeDtypeStruct(own.shape, own.dtype),
+        in_specs=[smem] + [vmem] * 7,
+        out_specs=vmem,
+        scratch_shapes=[level(6)] * 4 + [factors(7)],
+        compiler_params=pltpu.CompilerParams(vmem_limit_bytes=36 * 2**20),
+        cost_estimate=pl.CostEstimate(flops=16 * 20 * work, bytes_accessed=8 * 2**20, transcendentals=0),
+    )(info, own, far, own_coefs, far_coefs, *mids)
 
 
 def block_perm(order):
@@ -70,8 +242,6 @@
 
 def per_device(basis, diffusivity, velocity, step_counts, block_order):
     start = basis[0]
-    layers = start.shape[0]
-    width = STEPS
     here = lax.axis_index("seg")
     total = lax.axis_size("seg")
     place = lax.axis_index("space")
@@ -81,23 +251,16 @@
     count = step_counts[0]
 
     ahead = lax.ppermute(start, "seg", [((i + 1) % total, i) for i in range(total)])
-    coefs = jnp.concatenate([diffusivity, velocity[0]], axis=0)
+    even = core == 0
+    fields = jnp.concatenate([diffusivity, 0.5 * velocity[0]], axis=0)
+    turned = fields[:, ::-1] * jnp.array([1.0, -1.0, 1.0, 1.0], jnp.float32)[:, None, None, None]
+    coefs = jnp.where(even, turned, fields).transpose(1, 2, 0, 3).reshape(-1, fields.shape[-1])
     far = exchange_pairs(start, "space", 1)
     near = exchange_pairs(start, "space", 0)
     far_coefs = exchange_pairs(coefs, "space", 1)
     near_coefs = exchange_pairs(coefs, "space", 0)
-    even = core == 0
-    before = jnp.where(even, far, near)[-width:]
-    after = jnp.where(even, near, far)[:width]
-    window = jnp.concatenate([before, start, after], axis=0)
-    before_c = jnp.where(even, far_coefs, near_coefs)[:, -width:]
-    after_c = jnp.where(even, near_coefs, far_coefs)[:, :width]
-    coefs = jnp.concatenate([before_c, coefs, after_c], axis=1)
-    for turn in range(STEPS):
-        coefs = coefs[:, 1:-1]
-        fresh = step_once(window, coefs[0], coefs[1:])
-        window = jnp.where(turn < count, fresh, window[1:-1])
-    state = window
+    info = jnp.stack([core, count]).astype(jnp.int32)
+    state = run_steps(info, near, start, far, near_coefs, coefs, far_coefs)
 
     raw = lax.dot_general(
         ahead.reshape(-1, K),

time: 58.7 us -> 49.9 us (0.85)
  other arithmetic: 16.3 us -> 0.36 us
  Pallas kernels: 0 us -> 11.7 us
  starting transfers between devices: 18 us -> 12.8 us
  local copies, waits for them, and re-layouts: 8.17 us -> 3.99 us
  waiting for transfers between devices: 12.6 us -> 16.6 us
  matrix products: 1.46 us -> 2.59 us
    convert_element_type x4 -> x0, other arithmetic: 12.4 us -> none  [step_once(): wide = window.astype(jnp.float32)]
    pallas_call x0 -> x2, Pallas kernels: none -> 11.7 us  [the longest x1 6.78 us: run_steps(): pl.pallas_call(far_kernel, out_shape=jax.ShapeDtypeStruct(own.shape, own....]
    slice x16 -> x0, local copies, waits for them, and re-layouts: 5.01 us -> none  [the longest x8 2.62 us: step_once(): plus_y = jnp.roll(center, -1, 1)]
    ppermute x7, waiting for transfers between devices: 12.6 us -> 16.6 us  [swap(): return lax.ppermute(value, axis, [(i, i ^ bit) for i in range(size)])]
    ppermute x7, starting transfers between devices: 7.21 us -> 3.67 us  [swap(): return lax.ppermute(value, axis, [(i, i ^ bit) for i in range(size)])]
    unnamed x5 -> x13, local copies, waits for them, and re-layouts: 0.85 us -> 3.94 us
    ppermute x4, starting transfers between devices: 7.15 us -> 4.46 us  [exchange_pairs(): return lax.ppermute(value, axis, route)]
    select_n x3 -> x0, other arithmetic: 2.21 us -> none  [the longest x1 2.09 us: per_device(): window = jnp.where(turn < count, fresh, window[1:-1])]
  transfers between devices with their start and end apart: 12 -> 12, of which waited for: 6 -> 6; matrix products, arithmetic and copies ran while one was open for 41% -> 1% of each run, Pallas kernels for 0% -> 24%
where the time goes in v2:
time: 49.9 us; the launch traced here: 49.5 us
  waiting for transfers between devices  16.6 us (33%)
  starting transfers between devices  12.8 us (26%)
  Pallas kernels  11.7 us (23%)
  local copies, waits for them, and re-layouts  3.99 us (8%)
  matrix products  2.59 us (5%)
  between operations  1.48 us (3%)
    ppermute x7, waiting for transfers between devices, swap(): return lax.ppermute(value, axis, [(i, i ^ bit) for i in range(size)])  16.6 us
    pallas_call x1, Pallas kernels, run_steps(): pl.pallas_call(far_kernel, out_shape=jax.ShapeDtypeStruct(own.shape, own....  6.78 us
    pallas_call x1, Pallas kernels, run_steps(): pl.pallas_call(near_kernel, out_shape=(mid, mid, mid), in_specs=[smem] +...  4.89 us
    ppermute x1, starting transfers between devices, per_device(): lax.ppermute(start, 'seg', [((i + 1) % total, i) for i in range(total)])  4.68 us
    ppermute x4, starting transfers between devices, exchange_pairs(): return lax.ppermute(value, axis, route)  4.46 us
    unnamed x13, local copies, waits for them, and re-layouts  3.94 us
    ppermute x7, starting transfers between devices, swap(): return lax.ppermute(value, axis, [(i, i ^ bit) for i in range(size)])  3.67 us
    dot_general x1, matrix products, per_device(): lax.dot_general(ahead.reshape(-1, K), state.reshape(-1, K), (((0,), (0,))...  1.55 us
  transfers between devices with their start and end apart: 12, of which 6 were waited for; matrix products, arithmetic and copies ran while one was open for 1% of the time, Pallas kernels for 24%

profile of v2, /device:TPU:0, one launch (start us, length us, event | category | flops | bytes accessed | tf_op | source)
XLA Modules:
  0.0 49.5 jit_solution(17266185683681075458)
XLA Ops:
  0.6 0.5 %collective-permute-start.2 = (bf16[4,3,128,256]{3,2,1,0:T(8,128)(2,1)}, bf16[4,3,128,256]{3,2,1,0:T(8,128)(2,1)S(1)}, u32[]{:S(2)}, u32[]{:S(2)}) collective-permute-start(bf16[4,3,128,256]{3,2,1,0:T(8,128)(2,1)} %bitcast.25), channel_id=1, source_target_pairs={{0,1},{1,0},{2,3},{3,2},{4,5},{5,4},{6,7},{7,6},{8,9},{9,8},{10,11... | collective-permute-start | bytes 2359304 | tf_op jit(solution)/shard_map/ppermute | solution.py:28
  1.2 0.7 %collective-permute-start = (bf16[4,3,128,256]{3,2,1,0:T(8,128)(2,1)}, bf16[4,3,128,256]{3,2,1,0:T(8,128)(2,1)S(1)}, u32[]{:S(2)}, u32[]{:S(2)}) collective-permute-start(bf16[4,3,128,256]{3,2,1,0:T(8,128)(2,1)} %bitcast.26), channel_id=1, source_target_pairs={{1,2},{2,1},{5,6},{6,5},{9,10},{10,9},{13,14},{14,13},{17,18},{18,... | collective-permute-start | bytes 2359304 | tf_op jit(solution)/shard_map/ppermute | solution.py:28
  1.9 4.7 %collective-permute-start.4 = (bf16[4,3,128,256]{3,2,1,0:T(8,128)(2,1)}, bf16[4,3,128,256]{3,2,1,0:T(8,128)(2,1)S(1)}, u32[]{:S(2)}, u32[]{:S(2)}) collective-permute-start(bf16[4,3,128,256]{3,2,1,0:T(8,128)(2,1)} %bitcast.27), channel_id=1, source_target_pairs={{4,0},{8,4},{12,8},{0,12},{5,1},{9,5},{13,9},{1,13},{6,2},{10,6},{... | collective-permute-start | bytes 2359304 | tf_op jit(solution)/shard_map/ppermute | solution.py:253
  6.6 0.7 %copy-done.2 = f32[1,4,3,128]{3,1,2,0:T(4,128)S(1)} copy-done((f32[1,4,3,128]{3,1,2,0:T(4,128)S(1)}, f32[1,4,3,128]{3,1,2,0:T(4,128)}, u32[]{:S(2)}) %copy-start.2) | copy-done | bytes 6168
  7.3 0.6 %copy-done.4 = f32[4]{0:T(128)S(1)} copy-done((f32[4]{0:T(128)S(1)}, f32[4]{0:T(128)}, u32[]{:S(2)}) %copy-start.4) | copy-done | bytes 40
  7.9 0.1 select_bitcast_fusion
  8.0 2.6 %collective-permute-start.3 = (f32[48,128]{1,0:T(8,128)S(1)}, f32[48,128]{1,0:T(8,128)S(1)}, u32[]{:S(2)}, u32[]{:S(2)}) collective-permute-start(f32[48,128]{1,0:T(8,128)S(1)} %bitcast.30), channel_id=1, source_target_pairs={{0,1},{1,0},{2,3},{3,2},{4,5},{5,4},{6,7},{7,6},{8,9},{9,8},{10,11... | collective-permute-start | bytes 73736 | tf_op jit(solution)/shard_map/ppermute | solution.py:28
  10.6 0.7 %collective-permute-start.1 = (f32[48,128]{1,0:T(8,128)S(1)}, f32[48,128]{1,0:T(8,128)S(1)}, u32[]{:S(2)}, u32[]{:S(2)}) collective-permute-start(f32[48,128]{1,0:T(8,128)S(1)} %bitcast.31), channel_id=1, source_target_pairs={{1,2},{2,1},{5,6},{6,5},{9,10},{10,9},{13,14},{14,13},{17,18},{18,... | collective-permute-start | bytes 73736 | tf_op jit(solution)/shard_map/ppermute | solution.py:28
  11.9 0.7 %copy-done.5 = s32[4,16]{1,0:T(4,128)S(1)} copy-done((s32[4,16]{1,0:T(4,128)S(1)}, s32[4,16]{1,0:T(4,128)}, u32[]{:S(2)}) %copy-start.5) | copy-done | bytes 280
  12.6 0.1 select_reduce_fusion.1
  12.7 0.1 pad_add_fusion.info
  12.8 1.1 %copy-done = bf16[1,4,3,128,256]{4,3,2,1,0:T(8,128)(2,1)S(1)} copy-done((bf16[1,4,3,128,256]{4,3,2,1,0:T(8,128)(2,1)S(1)}, bf16[1,4,3,128,256]{4,3,2,1,0:T(8,128)(2,1)}, u32[]{:S(2)}) %copy-start) | copy-done | bytes 786456
  13.9 4.9 %shard_map.77 = (f32[2,3,2,144,128]{4,3,2,1,0:T(8,128)S(1)}, f32[2,3,2,144,128]{4,3,2,1,0:T(8,128)S(1)}, f32[2,3,2,144,128]{4,3,2,1,0:T(8,128)S(1)}) custom-call(s32[2]{0:T(128)S(1)} %pad_add_fusion.info, bf16[4,3,128,256]{3,2,1,0:T(8,128)(2,1)S(1)} %collective-permute-done.2.near, bf16[4,3,128,256]{3,2,1,0:T(8,128)(2,1)S(1)} %bitcast.28, ...), custom_call_target="tpu_custom_call" | custom-call | flops 23592960 | bytes 8388608 | tf_op jit(solution)/shard_map/pallas_call | solution.py:199
  18.8 6.8 %shard_map.78 = bf16[4,3,128,256]{3,2,1,0:T(8,128)(2,1)} custom-call(s32[2]{0:T(128)S(1)} %pad_add_fusion.info, bf16[4,3,128,256]{3,2,1,0:T(8,128)(2,1)S(1)} %bitcast.29, bf16[4,3,128,256]{3,2,1,0:T(8,128)(2,1)S(1)} %collective-permute-done.far, f32[48,128]{1,0:T(8,128)S(1)} %bitcast.33, f32[48,128]{1,0:T(8,128)S(1)} %collective-permute-done.1.far_coefs, ...), custom_call_target="tpu_custom_call" | custom-call | flops 31457280 | bytes 8388608 | tf_op jit(solution)/shard_map/pallas_call | solution.py:208
  25.6 1.5 %fusion.1 = bf16[256,256]{1,0:T(8,128)(2,1)S(1)} fusion(bf16[4,3,128,256]{3,2,1,0:T(8,128)(2,1)} %shard_map.78, bf16[4,3,128,256]{3,2,1,0:T(8,128)(2,1)S(1)} %collective-permute-done.4), kind=kOutput, calls=%fused_computation.3 | convolution fusion | flops 201392128 | bytes 1703936 | tf_op jit(solution)/shard_map/dot_general | solution.py:265
  27.2 0.4 convolution_convert_fusion
  27.6 2.2 %collective-permute-start.5 = (bf16[256,128]{0,1:T(8,128)(2,1)S(1)}, bf16[256,128]{0,1:T(8,128)(2,1)S(1)}, u32[]{:S(2)}, u32[]{:S(2)}) collective-permute-start(bf16[256,128]{0,1:T(8,128)(2,1)S(1)} %broadcast_select_fusion), channel_id=1, source_target_pairs={{0,1},{1,0},{2,3},{3,2},{4,5},{5,4},{6,7},{7,6},{8,9},{9,8},{10,11... | collective-permute-start | bytes 196616 | tf_op jit(solution)/shard_map/ppermute | solution.py:20
  29.9 0.9 %collective-permute-done.5 = bf16[256,128]{0,1:T(8,128)(2,1)S(1)} collective-permute-done((bf16[256,128]{0,1:T(8,128)(2,1)S(1)}, bf16[256,128]{0,1:T(8,128)(2,1)S(1)}, u32[]{:S(2)}, u32[]{:S(2)}) %collective-permute-start.5) | collective-permute-done | bytes 65568 | tf_op jit(solution)/shard_map/ppermute | solution.py:20
  30.8 1.1 %collective-permute-start.6 = (bf16[256,128]{0,1:T(8,128)(2,1)S(1)}, bf16[256,128]{0,1:T(8,128)(2,1)S(1)}, u32[]{:S(2)}, u32[]{:S(2)}) collective-permute-start(bf16[256,128]{0,1:T(8,128)(2,1)S(1)} %add_convert_fusion.1), channel_id=1, source_target_pairs={{0,2},{1,3},{2,0},{3,1},{4,6},{5,7},{6,4},{7,5},{8,10},{9,11},{10,... | collective-permute-start | bytes 196616 | tf_op jit(solution)/shard_map/ppermute | solution.py:20
  32.0 3.3 %collective-permute-done.6 = bf16[256,128]{0,1:T(8,128)(2,1)S(1)} collective-permute-done((bf16[256,128]{0,1:T(8,128)(2,1)S(1)}, bf16[256,128]{0,1:T(8,128)(2,1)S(1)}, u32[]{:S(2)}, u32[]{:S(2)}) %collective-permute-start.6) | collective-permute-done | bytes 65568 | tf_op jit(solution)/shard_map/ppermute | solution.py:20
  35.2 0.1 collective-permute-start.8
  35.3 0.1 collective-permute-start.7
  35.4 4.2 %collective-permute-done.8 = bf16[256,128]{0,1:T(8,128)(2,1)S(1)} collective-permute-done((bf16[256,128]{0,1:T(8,128)(2,1)S(1)}, bf16[256,128]{0,1:T(8,128)(2,1)S(1)}, u32[]{:S(2)}, u32[]{:S(2)}) %collective-permute-start.8) | collective-permute-done | bytes 65568 | tf_op jit(solution)/shard_map/ppermute | solution.py:20
  39.6 1.2 %collective-permute-done.9 = bf16[256,128]{0,1:T(8,128)(2,1)S(1)} collective-permute-done((bf16[256,128]{0,1:T(8,128)(2,1)S(1)}, bf16[256,128]{0,1:T(8,128)(2,1)S(1)}, u32[]{:S(2)}, u32[]{:S(2)}) %collective-permute-start.9) | collective-permute-done | bytes 65568 | tf_op jit(solution)/shard_map/ppermute | solution.py:20
  40.8 0.2 fusion
  41.1 0.1 collective-permute-start.10
  41.2 0.2 fusion.3
  41.4 5.7 %collective-permute-done.10 = bf16[256,128]{0,1:T(8,128)(2,1)S(1)} collective-permute-done((bf16[256,128]{0,1:T(8,128)(2,1)S(1)}, bf16[256,128]{0,1:T(8,128)(2,1)S(1)}, u32[]{:S(2)}, u32[]{:S(2)}) %collective-permute-start.10) | collective-permute-done | bytes 65568 | tf_op jit(solution)/shard_map/ppermute | solution.py:20
  47.1 0.2 convert_select_fusion
  47.2 0.1 collective-permute-start.11
  47.3 1.3 %collective-permute-done.11 = f32[256,128]{0,1:T(8,128)S(1)} collective-permute-done((f32[256,128]{0,1:T(8,128)S(1)}, f32[256,128]{0,1:T(8,128)S(1)}, u32[]{:S(2)}, u32[]{:S(2)}) %collective-permute-start.11) | collective-permute-done | bytes 131104 | tf_op jit(solution)/shard_map/ppermute | solution.py:20
  48.7 0.8 %copy.13 = f32[1,256,256]{2,1,0:T(8,128)} copy(f32[1,256,256]{1,2,0:T(8,128)S(1)} %fusion.2) | data formatting | bytes 524288
  (27 shorter events, 0.2 us)
Async XLA Ops:
  0.6 5.9 %copy-start.3 = (f32[1,3,4,3,128]{4,2,3,1,0:T(4,128)S(1)}, f32[1,3,4,3,128]{4,2,3,1,0:T(4,128)}, u32[]{:S(2)}) copy-start(f32[1,3,4,3,128]{4,2,3,1,0:T(4,128)} %param.8) | copy-start | bytes 55300
  0.6 12.1 %collective-permute-start.2 = (bf16[4,3,128,256]{3,2,1,0:T(8,128)(2,1)}, bf16[4,3,128,256]{3,2,1,0:T(8,128)(2,1)S(1)}, u32[]{:S(2)}, u32[]{:S(2)}) collective-permute-start(bf16[4,3,128,256]{3,2,1,0:T(8,128)(2,1)} %bitcast.25), channel_id=1, source_target_pairs={{0,1},{1,0},{2,3},{3,2},{4,5},{5,4},{6,7},{7,6},{8,9},{9,8},{10,11... | collective-permute-start | bytes 2359304 | tf_op jit(solution)/shard_map/ppermute | solution.py:28
  1.2 17.7 %collective-permute-start = (bf16[4,3,128,256]{3,2,1,0:T(8,128)(2,1)}, bf16[4,3,128,256]{3,2,1,0:T(8,128)(2,1)S(1)}, u32[]{:S(2)}, u32[]{:S(2)}) collective-permute-start(bf16[4,3,128,256]{3,2,1,0:T(8,128)(2,1)} %bitcast.26), channel_id=1, source_target_pairs={{1,2},{2,1},{5,6},{6,5},{9,10},{10,9},{13,14},{14,13},{17,18},{18,... | collective-permute-start | bytes 2359304 | tf_op jit(solution)/shard_map/ppermute | solution.py:28
  1.9 23.8 %collective-permute-start.4 = (bf16[4,3,128,256]{3,2,1,0:T(8,128)(2,1)}, bf16[4,3,128,256]{3,2,1,0:T(8,128)(2,1)S(1)}, u32[]{:S(2)}, u32[]{:S(2)}) collective-permute-start(bf16[4,3,128,256]{3,2,1,0:T(8,128)(2,1)} %bitcast.27), channel_id=1, source_target_pairs={{4,0},{8,4},{12,8},{0,12},{5,1},{9,5},{13,9},{1,13},{6,2},{10,6},{... | collective-permute-start | bytes 2359304 | tf_op jit(solution)/shard_map/ppermute | solution.py:253
  6.5 0.7 %copy-start.2 = (f32[1,4,3,128]{3,1,2,0:T(4,128)S(1)}, f32[1,4,3,128]{3,1,2,0:T(4,128)}, u32[]{:S(2)}) copy-start(f32[1,4,3,128]{3,1,2,0:T(4,128)} %param.7) | copy-start | bytes 18436
  7.2 0.7 %copy-start.4 = (f32[4]{0:T(128)S(1)}, f32[4]{0:T(128)}, u32[]{:S(2)}) copy-start(f32[4]{0:T(128)} %constant.98.clone) | copy-start | bytes 52
  8.0 4.8 %collective-permute-start.3 = (f32[48,128]{1,0:T(8,128)S(1)}, f32[48,128]{1,0:T(8,128)S(1)}, u32[]{:S(2)}, u32[]{:S(2)}) collective-permute-start(f32[48,128]{1,0:T(8,128)S(1)} %bitcast.30), channel_id=1, source_target_pairs={{0,1},{1,0},{2,3},{3,2},{4,5},{5,4},{6,7},{7,6},{8,9},{9,8},{10,11... | collective-permute-start | bytes 73736 | tf_op jit(solution)/shard_map/ppermute | solution.py:28
  10.6 8.2 %collective-permute-start.1 = (f32[48,128]{1,0:T(8,128)S(1)}, f32[48,128]{1,0:T(8,128)S(1)}, u32[]{:S(2)}, u32[]{:S(2)}) collective-permute-start(f32[48,128]{1,0:T(8,128)S(1)} %bitcast.31), channel_id=1, source_target_pairs={{1,2},{2,1},{5,6},{6,5},{9,10},{10,9},{13,14},{14,13},{17,18},{18,... | collective-permute-start | bytes 73736 | tf_op jit(solution)/shard_map/ppermute | solution.py:28
  11.9 0.7 %copy-start.5 = (s32[4,16]{1,0:T(4,128)S(1)}, s32[4,16]{1,0:T(4,128)}, u32[]{:S(2)}) copy-start(s32[4,16]{1,0:T(4,128)} %param.10) | copy-start | bytes 772
  12.8 1.1 %copy-start = (bf16[1,4,3,128,256]{4,3,2,1,0:T(8,128)(2,1)S(1)}, bf16[1,4,3,128,256]{4,3,2,1,0:T(8,128)(2,1)}, u32[]{:S(2)}) copy-start(bf16[1,4,3,128,256]{4,3,2,1,0:T(8,128)(2,1)} %param.6) | copy-start | bytes 2359300
  13.9 4.9 %copy-start.1 = (bf16[1,4,3,128,256]{4,3,2,1,0:T(8,128)(2,1)S(1)}, bf16[1,4,3,128,256]{4,3,2,1,0:T(8,128)(2,1)}, u32[]{:S(2)}) copy-start(bf16[1,4,3,128,256]{4,3,2,1,0:T(8,128)(2,1)} %param.6) | copy-start | bytes 2359300
  27.6 3.1 %collective-permute-start.5 = (bf16[256,128]{0,1:T(8,128)(2,1)S(1)}, bf16[256,128]{0,1:T(8,128)(2,1)S(1)}, u32[]{:S(2)}, u32[]{:S(2)}) collective-permute-start(bf16[256,128]{0,1:T(8,128)(2,1)S(1)} %broadcast_select_fusion), channel_id=1, source_target_pairs={{0,1},{1,0},{2,3},{3,2},{4,5},{5,4},{6,7},{7,6},{8,9},{9,8},{10,11... | collective-permute-start | bytes 196616 | tf_op jit(solution)/shard_map/ppermute | solution.py:20
  30.8 4.4 %collective-permute-start.6 = (bf16[256,128]{0,1:T(8,128)(2,1)S(1)}, bf16[256,128]{0,1:T(8,128)(2,1)S(1)}, u32[]{:S(2)}, u32[]{:S(2)}) collective-permute-start(bf16[256,128]{0,1:T(8,128)(2,1)S(1)} %add_convert_fusion.1), channel_id=1, source_target_pairs={{0,2},{1,3},{2,0},{3,1},{4,6},{5,7},{6,4},{7,5},{8,10},{9,11},{10,... | collective-permute-start | bytes 196616 | tf_op jit(solution)/shard_map/ppermute | solution.py:20
  35.2 4.3 %collective-permute-start.8 = (bf16[256,128]{0,1:T(8,128)(2,1)S(1)}, bf16[256,128]{0,1:T(8,128)(2,1)S(1)}, u32[]{:S(2)}, u32[]{:S(2)}) collective-permute-start(bf16[256,128]{0,1:T(8,128)(2,1)S(1)} %multiply_convert_fusion), channel_id=1, source_target_pairs={{0,4},{4,0},{8,12},{12,8},{1,5},{5,1},{9,13},{13,9},{2,6},{6,2},{1... | collective-permute-start | bytes 196616 | tf_op jit(solution)/shard_map/ppermute | solution.py:20
  35.3 4.3 %collective-permute-start.7 = (bf16[256,128]{0,1:T(8,128)(2,1)S(1)}, bf16[256,128]{0,1:T(8,128)(2,1)S(1)}, u32[]{:S(2)}, u32[]{:S(2)}) collective-permute-start(bf16[256,128]{0,1:T(8,128)(2,1)S(1)} %multiply_convert_fusion), channel_id=1, source_target_pairs={{0,1},{1,0},{2,3},{3,2},{4,5},{5,4},{6,7},{7,6},{8,9},{9,8},{10,11... | collective-permute-start | bytes 196616 | tf_op jit(solution)/shard_map/ppermute | solution.py:20
  39.6 1.3 %collective-permute-start.9 = (bf16[256,128]{0,1:T(8,128)(2,1)S(1)}, bf16[256,128]{0,1:T(8,128)(2,1)S(1)}, u32[]{:S(2)}, u32[]{:S(2)}) collective-permute-start(bf16[256,128]{0,1:T(8,128)(2,1)S(1)} %collective-permute-done.8), channel_id=1, source_target_pairs={{0,1},{1,0},{2,3},{3,2},{4,5},{5,4},{6,7},{7,6},{8,9},{9,8},{10,11... | collective-permute-start | bytes 196616 | tf_op jit(solution)/shard_map/ppermute | solution.py:20
  41.1 6.0 %collective-permute-start.10 = (bf16[256,128]{0,1:T(8,128)(2,1)S(1)}, bf16[256,128]{0,1:T(8,128)(2,1)S(1)}, u32[]{:S(2)}, u32[]{:S(2)}) collective-permute-start(bf16[256,128]{0,1:T(8,128)(2,1)S(1)} %slice_select_fusion), channel_id=1, source_target_pairs={{0,8},{4,12},{8,0},{12,4},{1,9},{5,13},{9,1},{13,5},{2,10},{6,14},... | collective-permute-start | bytes 196616 | tf_op jit(solution)/shard_map/ppermute | solution.py:20
  47.2 1.4 %collective-permute-start.11 = (f32[256,128]{0,1:T(8,128)S(1)}, f32[256,128]{0,1:T(8,128)S(1)}, u32[]{:S(2)}, u32[]{:S(2)}) collective-permute-start(f32[256,128]{0,1:T(8,128)S(1)} %convert_select_fusion), channel_id=1, source_target_pairs={{0,1},{1,0},{2,3},{3,2},{4,5},{5,4},{6,7},{7,6},{8,9},{9,8},{10,11... | collective-permute-start | bytes 393224 | tf_op jit(solution)/shard_map/ppermute | solution.py:20

commit v3 on v2

v3 whole, which is shorter than its diff:
```python
import functools
import math

import jax
import jax.numpy as jnp
from jax import lax
from jax.experimental import pallas as pl
from jax.experimental.pallas import tpu as pltpu
from jax.sharding import PartitionSpec as P

K = 256
BLOCK = 16
STEPS = 4
HALF = K // 2

coupling = 0.35


def swap(value, axis, bit):
    size = lax.axis_size(axis)
    return lax.ppermute(value, axis, [(i, i ^ bit) for i in range(size)])


def exchange_pairs(value, axis, first):
    size = lax.axis_size(axis)
    route = []
    for i in range(first, size - 1, 2):
        route += [(i, i + 1), (i + 1, i)]
    return lax.ppermute(value, axis, route)


ROWS = 144
TOP = 8
CHUNK = 16
FIELDS = 4
NEAR_LAYERS = (6, 4, 2)


def spread_coefs(columns, column, out, plane):
    def field(k):
        return jnp.broadcast_to(columns[:, column + k : column + k + 1], (columns.shape[0], HALF))

    diffusion = field(0)
    along_u = field(1)
    along_y = field(2)
    along_z = field(3)
    out[plane, 0] = 1.0 - 6.0 * diffusion
    out[plane, 1] = diffusion - along_u
    out[plane, 2] = diffusion + along_u
    out[plane, 3] = diffusion - along_y
    out[plane, 4] = diffusion + along_y
    out[plane, 5] = diffusion - along_z
    out[plane, 6] = diffusion + along_z


def coef_columns(fields, odd, backward, table):
    ys, layers, zs = fields.shape[1:]
    table[...] = jnp.zeros_like(table)
    sign = jnp.where(odd, 0.5, -0.5)
    for k in range(layers):
        flipped = layers - 1 - k
        x = jnp.where(odd, flipped, k) if backward else jnp.where(odd, k, flipped)
        for y in range(ys):
            for f in range(FIELDS):
                row = fields[f, y, pl.ds(x, 1), :]
                if f == 1:
                    row = row * sign
                elif f > 1:
                    row = row * 0.5
                at = (k * ys + y) * FIELDS + f
                table[at : at + 1, :] = row
    return table[...].T


def unpack_layer(source, index, dest, slot):
    ys, zs = source.shape[1], source.shape[2]
    for y in range(ys):
        for h in range(2):
            lanes = slice(h * HALF, (h + 1) * HALF)
            value = source[index, y, :, lanes].astype(jnp.float32)
            dest[slot, y, h, TOP : TOP + zs, :] = value
            dest[slot, y, h, TOP - 1 : TOP, :] = value[zs - 1 : zs]
            dest[slot, y, h, TOP + zs : TOP + zs + 1, :] = value[0:1]


def step_layer(source, index, coefs, layer, active, store):
    ys = source.shape[1]
    zs = coefs.shape[2]
    for z in range(0, zs, CHUNK):
        rows = slice(TOP + z, TOP + z + CHUNK)
        centers = [[source[index, y, h, rows, :] for h in range(2)] for y in range(ys)]
        for y in range(ys):
            factor = [coefs[layer * ys + y, k, z : z + CHUNK, :] for k in range(7)]
            for h in range(2):
                center = centers[y][h]
                new = factor[0] * center
                new += factor[1] * source[index + 1, y, h, rows, :]
                new += factor[2] * source[index - 1, y, h, rows, :]
                new += factor[3] * centers[(y + 1) % ys][h]
                new += factor[4] * centers[(y + ys - 1) % ys][h]
                new += factor[5] * source[index, y, h, TOP + z + 1 : TOP + z + CHUNK + 1, :]
                new += factor[6] * source[index, y, h, TOP + z - 1 : TOP + z + CHUNK - 1, :]
                if active is not None:
                    new = jnp.where(active, new, center)
                store(y, h, z, new.astype(jnp.bfloat16))


def into_level(dest, slot, zs):
    def store(y, h, z, rows):
        wide = rows.astype(jnp.float32)
        dest[slot, y, h, TOP + z : TOP + z + CHUNK, :] = wide
        if z == 0:
            dest[slot, y, h, TOP + zs : TOP + zs + 1, :] = wide[0:1]
        if z + CHUNK == zs:
            dest[slot, y, h, TOP - 1 : TOP, :] = wide[CHUNK - 1 : CHUNK]

    return store


def core_is_odd():
    return lax.axis_index("space") % 2 == 1


def near_kernel(
    counts, start, near, own_fields, near_fields, own_coefs, mid0, mid1, mid2, mid3,
    own, table, level0, level1, level2, level3, near_coefs, sem,
):
    odd = core_is_odd()
    fetch = pltpu.make_async_copy(start, own, sem)
    fetch.start()
    ys, zs = own.shape[1], own.shape[2]
    columns = coef_columns(own_fields, odd, False, table)
    for u in range(4):
        for y in range(ys):
            spread_coefs(columns, (u * ys + y) * FIELDS, own_coefs, u * ys + y)
    columns = coef_columns(near_fields, odd, True, table)
    for k in range(3):
        for y in range(ys):
            spread_coefs(columns, (k * ys + y) * FIELDS, near_coefs, (2 - k) * ys + y)

    def fill_near(k, _):
        unpack_layer(near, jnp.where(odd, 3 - k, k), level0, 3 - k)
        return 0

    def fill_own(k, _):
        unpack_layer(own, jnp.where(odd, k, 3 - k), level0, 4 + k)
        return 0

    lax.fori_loop(0, 4, fill_near, 0)
    fetch.wait()
    lax.fori_loop(0, 4, fill_own, 0)
    mid0[...] = level0[6:8]
    levels = (level0, level1, level2, level3)
    for t, layers in enumerate(NEAR_LAYERS):
        source, dest = levels[t], levels[t + 1]
        active = None if t < 2 else counts[0] > t
        half = layers // 2

        def near_one(j, _):
            step_layer(source, j + 1, near_coefs, j + t, active, into_level(dest, j, zs))
            return 0

        def own_one(j, _):
            step_layer(source, half + j + 1, own_coefs, j, active, into_level(dest, half + j, zs))
            return 0

        lax.fori_loop(0, half, near_one, 0)
        lax.fori_loop(0, half, own_one, 0)
    mid1[...] = level1[4:6]
    mid2[...] = level2[2:4]
    mid3[...] = level3[...]


def far_kernel(
    counts, far, far_fields, own_coefs, mid0, mid1, mid2, mid3,
    out, table, level0, level1, level2, level3, far_coefs,
):
    odd = core_is_odd()
    ys, zs = far.shape[1], far.shape[2]
    columns = coef_columns(far_fields, odd, True, table)
    for k in range(3):
        for y in range(ys):
            spread_coefs(columns, ((3 - k) * ys + y) * FIELDS, far_coefs, k * ys + y)

    def fill_far(k, _):
        unpack_layer(far, jnp.where(odd, k, 3 - k), level0, 2 + k)
        return 0

    lax.fori_loop(0, 4, fill_far, 0)
    level0[0:2] = mid0[...]
    level1[0:2] = mid1[...]
    level2[0:2] = mid2[...]
    level3[0:2] = mid3[...]
    levels = (level0, level1, level2, level3)
    for t in range(STEPS):
        source = levels[t]
        active = None if t < 2 else counts[0] > t

        def one(j, coefs, layer):
            if t < STEPS - 1:
                store = into_level(levels[t + 1], 2 + j, zs)
            else:
                place = jnp.where(odd, j, 3 - j)

                def store(y, h, z, rows):
                    out[place, y, z : z + CHUNK, h * HALF : (h + 1) * HALF] = rows

            step_layer(source, 1 + j, coefs, layer, active, store)

        def own_one(j, _):
            one(j, own_coefs, 3 - t + j)
            return 0

        def far_one(j, _):
            one(j, far_coefs, j - t - 1)
            return 0

        lax.fori_loop(0, t + 1, own_one, 0)
        if t < 3:
            lax.fori_loop(t + 1, 4, far_one, 0)


def mul(left, right):
    return jnp.dot(left, right, preferred_element_type=jnp.float32)


def to_bf16(value):
    return value.astype(jnp.bfloat16)


def to_f32(value):
    return value.astype(jnp.float32)


def product_kernel(order, ahead, state, image, out, rows, column_perm, sem):
    save = pltpu.make_async_copy(state, image, sem)
    save.start()
    here = lax.axis_index("seg")
    after = lax.rem(here + 1, lax.axis_size("seg"))
    blocks = K // BLOCK
    stored = lax.broadcasted_iota(jnp.int32, (BLOCK, K), 0)
    true = lax.broadcasted_iota(jnp.int32, (BLOCK, K), 1)
    for b in range(blocks):
        hit = (stored + order[here, b] * BLOCK) == true
        column_perm[b * BLOCK : (b + 1) * BLOCK, :] = jnp.where(hit, 1.0, 0.0).astype(jnp.bfloat16)
    left = ahead[...].reshape(-1, K)
    right = state[...].reshape(-1, K)
    raw = lax.dot_general(left, right, (((0,), (0,)), ((), ())), preferred_element_type=jnp.float32)
    raw = to_bf16(raw)
    for b in range(blocks):
        to = pl.multiple_of(order[after, b] * BLOCK, BLOCK)
        rows[pl.ds(to, BLOCK), :] = raw[b * BLOCK : (b + 1) * BLOCK]
    out[...] = to_bf16(mul(rows[...], column_perm[...]))
    save.wait()


def specs(kinds):
    spaces = {"s": pltpu.SMEM, "v": pltpu.VMEM, "a": pl.ANY}
    return [pl.BlockSpec(memory_space=spaces[kind]) for kind in kinds]


def params(megabytes):
    return pltpu.CompilerParams(vmem_limit_bytes=megabytes * 2**20)


def cost(flops, read):
    return pl.CostEstimate(flops=int(flops), bytes_accessed=int(read), transcendentals=0)


def near_steps(counts, start, near, own_fields, near_fields):
    ys, zs = start.shape[1], start.shape[2]

    def level(layers):
        return pltpu.VMEM((layers, ys, 2, ROWS, HALF), jnp.float32)

    mid = jax.ShapeDtypeStruct((2, ys, 2, ROWS, HALF), jnp.float32)
    return pl.pallas_call(
        near_kernel,
        out_shape=(jax.ShapeDtypeStruct((4 * ys, 7, zs, HALF), jnp.float32), mid, mid, mid, mid),
        in_specs=specs("savvv"),
        out_specs=tuple(specs("vvvvv")),
        scratch_shapes=[
            pltpu.VMEM(start.shape, start.dtype),
            pltpu.VMEM((128, zs), jnp.float32),
            level(8),
            level(6),
            level(4),
            level(2),
            pltpu.VMEM((3 * ys, 7, zs, HALF), jnp.float32),
            pltpu.SemaphoreType.DMA,
        ],
        compiler_params=params(36),
        cost_estimate=cost(0, 0),
    )(counts, start, near, own_fields, near_fields)


def far_steps(counts, far, far_fields, carried):
    ys, zs = far.shape[1], far.shape[2]
    level = pltpu.VMEM((6, ys, 2, ROWS, HALF), jnp.float32)
    return pl.pallas_call(
        far_kernel,
        out_shape=jax.ShapeDtypeStruct(far.shape, far.dtype),
        in_specs=specs("svvvvvvv"),
        out_specs=specs("v")[0],
        scratch_shapes=[pltpu.VMEM((128, zs), jnp.float32)]
        + [level] * 4
        + [pltpu.VMEM((3 * ys, 7, zs, HALF), jnp.float32)],
        compiler_params=params(36),
        cost_estimate=cost(0, 0),
    )(counts, far, far_fields, *carried)


def products(order, ahead, state):
    return pl.pallas_call(
        product_kernel,
        out_shape=(
            jax.ShapeDtypeStruct(state.shape, state.dtype),
            jax.ShapeDtypeStruct((K, K), jnp.bfloat16),
        ),
        in_specs=specs("svv"),
        out_specs=tuple(specs("av")),
        scratch_shapes=[
            pltpu.VMEM((K, K), jnp.bfloat16),
            pltpu.VMEM((K, K), jnp.bfloat16),
            pltpu.SemaphoreType.DMA,
        ],
        compiler_params=params(16),
        cost_estimate=cost(0, 0),
    )(order, ahead, state)


def merge_kernel(scale, straight, straight_other, diagonal, diagonal_other, own, tail, wide, block, half):
    odd = core_is_odd()
    upper = lax.axis_index("seg") % 2 == 1
    across = jnp.where(odd, straight_other[...], straight[...])
    along = jnp.where(odd, straight[...], straight_other[...])
    low = jnp.where(odd, diagonal_other[...], diagonal[...])
    high = jnp.where(odd, diagonal[...], diagonal_other[...])
    mine = (to_f32(own[...]) + to_f32(across)) * scale
    theirs = (to_f32(along) + to_f32(jnp.concatenate([low, high], axis=1))) * scale
    mine_low, theirs_low = to_bf16(mine), to_bf16(theirs)
    later = jnp.where(upper, mine_low, theirs_low)
    earlier = jnp.where(upper, theirs_low, mine_low)
    total = to_f32(mine_low) + to_f32(theirs_low) + mul(later, earlier)
    total_low = to_bf16(total)
    reach = jnp.where(upper, total, to_f32(mine_low))
    wide[...] = reach
    tail[...] = to_bf16(reach)
    block[...] = total_low
    half[...] = jnp.where(odd, total_low[:, HALF:], total_low[:, :HALF])


def merge(scale, straight, straight_other, diagonal, diagonal_other, own):
    full = jax.ShapeDtypeStruct((K, K), jnp.bfloat16)
    return pl.pallas_call(
        functools.partial(merge_kernel, scale),
        out_shape=(
            full,
            jax.ShapeDtypeStruct((K, K), jnp.float32),
            full,
            jax.ShapeDtypeStruct((K, HALF), jnp.bfloat16),
        ),
        in_specs=specs("vvvvv"),
        out_specs=tuple(specs("vvvv")),
        compiler_params=params(16),
        cost_estimate=cost(0, 0),
    )(straight, straight_other, diagonal, diagonal_other, own)


def last_kernel(bit, got, got_other, tail, wide, out):
    odd = core_is_odd()
    upper = lax.rem(lax.div(lax.axis_index("seg"), bit), 2) == 1
    low = jnp.where(odd, got_other[...], got[...])
    high = jnp.where(odd, got[...], got_other[...])
    before = jnp.concatenate([low, high], axis=1)
    more = to_f32(before) + mul(tail[...], before)
    row = lax.broadcasted_iota(jnp.int32, (K, K), 0)
    column = lax.broadcasted_iota(jnp.int32, (K, K), 1)
    reach = wide[...] + jnp.where(row == column, 1.0, 0.0)
    out[...] = jnp.where(upper, reach + more, reach)


def last(bit, got, got_other, tail, wide):
    return pl.pallas_call(
        functools.partial(last_kernel, bit),
        out_shape=jax.ShapeDtypeStruct((K, K), jnp.float32),
        in_specs=specs("vvvv"),
        out_specs=specs("v")[0],
        compiler_params=params(16),
        cost_estimate=cost(0, 0),
    )(got, got_other, tail, wide)


def mixed_swap(value, along, across, core_along):
    total, slabs = lax.axis_size("seg"), lax.axis_size("space")
    route = []
    for s in range(total):
        for x in range(slabs):
            if core_along:
                to = (s ^ along, x) if x % 2 else (s, x ^ across)
            else:
                to = (s ^ along, x ^ across)
            route.append((s * slabs + x, to[0] * slabs + to[1]))
    return lax.ppermute(value, ("seg", "space"), route)


def per_device(basis, diffusivity, velocity, step_counts, block_order):
    start = basis[0]
    total = lax.axis_size("seg")
    slabs = lax.axis_size("space")
    cells = start.shape[0] * slabs * start.shape[1] * start.shape[2]

    ahead = lax.ppermute(start, "seg", [((i + 1) % total, i) for i in range(total)])
    fields = jnp.concatenate([diffusivity, velocity[0]], axis=0).transpose(0, 2, 1, 3)
    far = exchange_pairs(start, "space", 1)
    near = exchange_pairs(start, "space", 0)
    far_fields = exchange_pairs(fields, "space", 1)
    near_fields = exchange_pairs(fields, "space", 0)
    carried = near_steps(step_counts, start, near, fields, near_fields)
    state = far_steps(step_counts, far, far_fields, carried)
    image, raw = products(block_order, ahead, state)

    bit = 1
    while 2 * bit < slabs:
        raw = to_bf16(to_f32(raw) + to_f32(swap(raw, "space", bit)))
        bit *= 2
    odd = lax.axis_index("space") % 2 == 1

    def my_half(full):
        return jnp.where(odd, full[:, HALF:], full[:, :HALF])

    straight = mixed_swap(raw, 1, bit, True)
    diagonal = mixed_swap(my_half(raw), 1, bit, False)
    straight_other = swap(straight, "space", 1)
    diagonal_other = swap(diagonal, "space", 1)
    scale = coupling / math.sqrt(K * cells)
    tail, wide, block, half = merge(scale, straight, straight_other, diagonal, diagonal_other, raw)

    bit = 2
    while 2 * bit < total:
        upper = (lax.axis_index("seg") // bit) % 2 == 1
        got = swap(half, "seg", bit)
        rest = swap(got, "space", 1)
        got = jnp.where(odd, jnp.concatenate([rest, got], 1), jnp.concatenate([got, rest], 1))
        later = jnp.where(upper, block, got)
        earlier = jnp.where(upper, got, block)
        wide = jnp.where(upper, wide + to_f32(got) + mul(tail, got), wide)
        tail = to_bf16(wide)
        block = to_bf16(to_f32(later) + to_f32(earlier) + mul(later, earlier))
        half = my_half(block)
        bit *= 2
    got = swap(half, "seg", bit)
    monodromy = last(bit, got, swap(got, "space", 1), tail, wide)
    return (image[None], monodromy[None])


def solution(mesh):
    in_specs = (
        P(("groups", "seg"), "space", None, None, None),
        P(("groups", "seg"), "space", None, None),
        P(("groups", "seg"), None, "space", None, None),
        P(("groups", "seg")),
        P("groups", None),
    )
    out_specs = (P(("groups", "seg"), "space", None, None, None), P(("groups", "seg"), None, None))
    return jax.shard_map(
        per_device, mesh=mesh, in_specs=in_specs, out_specs=out_specs, check_vma=False
    )
```

time: 49.9 us -> 44.2 us (0.89)
  waiting for transfers between devices: 16.6 us -> 12.5 us
  local copies, waits for them, and re-layouts: 3.99 us -> 1.13 us
  matrix products: 2.59 us -> 0 us
  starting transfers between devices: 12.8 us -> 15.3 us
  Pallas kernels: 11.7 us -> 12.9 us
    ppermute x7 -> x5, waiting for transfers between devices: 16.6 us -> 6.21 us  [swap(): return lax.ppermute(value, axis, [(i, i ^ bit) for i in range(size)])]
    ppermute x0 -> x2, waiting for transfers between devices: none -> 4.89 us  [mixed_swap(): return lax.ppermute(value, ('seg', 'space'), route)]
    unnamed x13 -> x4, local copies, waits for them, and re-layouts: 3.94 us -> 1.13 us
    dot_general x5 -> x0, matrix products: 2.59 us -> none  [the longest x1 1.55 us: per_device(): lax.dot_general(ahead.reshape(-1, K), state.reshape(-1, K), (((0,), (0,))...]
    ppermute x0 -> x2, starting transfers between devices: none -> 1.65 us  [mixed_swap(): return lax.ppermute(value, ('seg', 'space'), route)]
    ppermute x1, waiting for transfers between devices: 0.01 us -> 1.35 us  [per_device(): lax.ppermute(start, 'seg', [((i + 1) % total, i) for i in range(total)])]
    pallas_call x2 -> x5, Pallas kernels: 11.7 us -> 12.9 us  [the longest x1 4.75 us: near_steps(): pl.pallas_call(near_kernel, out_shape=(jax.ShapeDtypeStruct((4 * ys, 7, z...]
    ppermute x7 -> x5, starting transfers between devices: 3.67 us -> 4.54 us  [swap(): return lax.ppermute(value, axis, [(i, i ^ bit) for i in range(size)])]
  transfers between devices with their start and end apart: 12 -> 12, of which waited for: 6 -> 7; matrix products, arithmetic and copies ran while one was open for 1% -> 2% of each run, Pallas kernels for 24% -> 21%
where the time goes in v3:
time: 44.2 us; the launch traced here: 43.9 us
  starting transfers between devices  15.3 us (35%)
  Pallas kernels  12.9 us (29%)
  waiting for transfers between devices  12.5 us (28%)
  between operations  1.38 us (3%)
  local copies, waits for them, and re-layouts  1.13 us (3%)
  other arithmetic  0.77 us (2%)
    ppermute x5, waiting for transfers between devices, swap(): return lax.ppermute(value, axis, [(i, i ^ bit) for i in range(size)])  6.21 us
    ppermute x2, waiting for transfers between devices, mixed_swap(): return lax.ppermute(value, ('seg', 'space'), route)  4.89 us
    pallas_call x1, Pallas kernels, near_steps(): pl.pallas_call(near_kernel, out_shape=(jax.ShapeDtypeStruct((4 * ys, 7, z...  4.75 us
    ppermute x1, starting transfers between devices, per_device(): lax.ppermute(start, 'seg', [((i + 1) % total, i) for i in range(total)])  4.68 us
    ppermute x5, starting transfers between devices, swap(): return lax.ppermute(value, axis, [(i, i ^ bit) for i in range(size)])  4.54 us
    pallas_call x1, Pallas kernels, far_steps(): pl.pallas_call(far_kernel, out_shape=jax.ShapeDtypeStruct(far.shape, far....  4.48 us
    ppermute x4, starting transfers between devices, exchange_pairs(): return lax.ppermute(value, axis, route)  4.39 us
    pallas_call x1, Pallas kernels, products(): pl.pallas_call(product_kernel, out_shape=(jax.ShapeDtypeStruct(state.shap...  1.84 us
  transfers between devices with their start and end apart: 12, of which 7 were waited for; matrix products, arithmetic and copies ran while one was open for 2% of the time, Pallas kernels for 21%

profile of v3, /device:TPU:0, one launch (start us, length us, event | category | flops | bytes accessed | tf_op | source)
XLA Modules:
  0.0 43.9 jit_solution(15972495937475486760)
XLA Ops:
  0.6 0.5 %collective-permute-start.3 = (bf16[4,3,128,256]{3,2,1,0:T(8,128)(2,1)}, bf16[4,3,128,256]{3,2,1,0:T(8,128)(2,1)S(1)}, u32[]{:S(2)}, u32[]{:S(2)}) collective-permute-start(bf16[4,3,128,256]{3,2,1,0:T(8,128)(2,1)} %bitcast.6), channel_id=1, source_target_pairs={{0,1},{1,0},{2,3},{3,2},{4,5},{5,4},{6,7},{7,6},{8,9},{9,8},{10,11... | collective-permute-start | bytes 2359304 | tf_op jit(solution)/shard_map/ppermute | solution.py:29
  1.1 0.7 %collective-permute-start.1 = (bf16[4,3,128,256]{3,2,1,0:T(8,128)(2,1)}, bf16[4,3,128,256]{3,2,1,0:T(8,128)(2,1)S(1)}, u32[]{:S(2)}, u32[]{:S(2)}) collective-permute-start(bf16[4,3,128,256]{3,2,1,0:T(8,128)(2,1)} %bitcast.7), channel_id=1, source_target_pairs={{1,2},{2,1},{5,6},{6,5},{9,10},{10,9},{13,14},{14,13},{17,18},{18,... | collective-permute-start | bytes 2359304 | tf_op jit(solution)/shard_map/ppermute | solution.py:29
  1.9 4.7 %collective-permute-start = (bf16[4,3,128,256]{3,2,1,0:T(8,128)(2,1)}, bf16[4,3,128,256]{3,2,1,0:T(8,128)(2,1)S(1)}, u32[]{:S(2)}, u32[]{:S(2)}) collective-permute-start(bf16[4,3,128,256]{3,2,1,0:T(8,128)(2,1)} %bitcast.8), channel_id=1, source_target_pairs={{4,0},{8,4},{12,8},{0,12},{5,1},{9,5},{13,9},{1,13},{6,2},{10,6},{... | collective-permute-start | bytes 2359304 | tf_op jit(solution)/shard_map/ppermute | solution.py:413
  6.5 0.7 %maximum_bitcast_fusion.own_fields = f32[4,3,4,128]{3,2,1,0:T(4,128)S(1)} fusion(f32[3,4,3,128]{3,1,2,0:T(4,128)} %bitcast.11, f32[1,4,3,128]{3,1,2,0:T(4,128)} %param.6), kind=kLoop, calls=%fused_computation.2 | loop fusion | flops 6144 | bytes 49152 | tf_op jit(solution)/shard_map/transpose | solution.py:414
  7.3 2.5 %collective-permute-start.4 = (f32[4,3,4,128]{3,2,1,0:T(4,128)S(1)}, f32[4,3,4,128]{3,2,1,0:T(4,128)S(1)}, u32[]{:S(2)}, u32[]{:S(2)}) collective-permute-start(f32[4,3,4,128]{3,2,1,0:T(4,128)S(1)} %maximum_bitcast_fusion.own_fields), channel_id=1, source_target_pairs={{0,1},{1,0},{2,3},{3,2},{4,5},{5,4},{6,7},{7,6},{8,9},{9,8},{10,11... | collective-permute-start | bytes 73736 | tf_op jit(solution)/shard_map/ppermute | solution.py:29
  9.8 0.7 %collective-permute-start.2 = (f32[4,3,4,128]{3,2,1,0:T(4,128)S(1)}, f32[4,3,4,128]{3,2,1,0:T(4,128)S(1)}, u32[]{:S(2)}, u32[]{:S(2)}) collective-permute-start(f32[4,3,4,128]{3,2,1,0:T(4,128)S(1)} %maximum_bitcast_fusion.own_fields), channel_id=1, source_target_pairs={{1,2},{2,1},{5,6},{6,5},{9,10},{10,9},{13,14},{14,13},{17,18},{18,... | collective-permute-start | bytes 73736 | tf_op jit(solution)/shard_map/ppermute | solution.py:29
  11.1 0.0 collective-permute-done.4.near_fields
  11.1 0.0 collective-permute-done.3.near
  11.1 0.0 copy-start
  11.1 1.1 %copy-done = bf16[1,4,3,128,256]{4,3,2,1,0:T(8,128)(2,1)S(1)} copy-done((bf16[1,4,3,128,256]{4,3,2,1,0:T(8,128)(2,1)S(1)}, bf16[1,4,3,128,256]{4,3,2,1,0:T(8,128)(2,1)}, u32[]{:S(2)}) %copy-start) | copy-done | bytes 786456
  12.3 4.8 %shard_map.68 = (f32[12,7,128,128]{3,2,1,0:T(8,128)S(1)}, f32[2,3,2,144,128]{4,3,2,1,0:T(8,128)S(1)}, f32[2,3,2,144,128]{4,3,2,1,0:T(8,128)S(1)}, f32[2,3,2,144,...) custom-call(s32[1]{0:T(128)S(6)} %copy.7.counts, bf16[4,3,128,256]{3,2,1,0:T(8,128)(2,1)S(1)} %bitcast.9, ...), custom_call_target="tpu_custom_call" | custom-call | tf_op jit(solution)/shard_map/pallas_call | solution.py:277
  17.0 0.0 copy-start.1
  17.0 0.0 collective-permute-done.2.far_fields
  17.0 0.0 collective-permute-done.1.far
  17.0 4.5 %shard_map.69.state = bf16[4,3,128,256]{3,2,1,0:T(8,128)(2,1)S(1)} custom-call(s32[1]{0:T(128)S(6)} %copy.7.counts, bf16[4,3,128,256]{3,2,1,0:T(8,128)(2,1)S(1)} %collective-permute-done.1.far, f32[4,3,4,128]{3,2,1,0:T(4,128)S(1)} %collective-permute-done.2.far_fields, f32[12,7,128,128]{3,2,1,0:T(8,128)S(1)} %get-tuple-element.12.own_coefs, ...), custom_call_target="tpu_custom_call" | custom-call | tf_op jit(solution)/shard_map/pallas_call | solution.py:300
  21.5 1.3 %collective-permute-done.ahead = bf16[4,3,128,256]{3,2,1,0:T(8,128)(2,1)S(1)} collective-permute-done((bf16[4,3,128,256]{3,2,1,0:T(8,128)(2,1)}, bf16[4,3,128,256]{3,2,1,0:T(8,128)(2,1)S(1)}, u32[]{:S(2)}, u32[]{:S(2)}) %collective-permute-start) | collective-permute-done | bytes 786464 | tf_op jit(solution)/shard_map/ppermute | solution.py:413
  22.9 1.8 %shard_map.70 = (bf16[4,3,128,256]{3,2,1,0:T(8,128)(2,1)}, bf16[256,256]{1,0:T(8,128)(2,1)S(1)}) custom-call(s32[4,16]{1,0:T(4,128)S(1)} %copy-done.1, bf16[4,3,128,256]{3,2,1,0:T(8,128)(2,1)S(1)} %collective-permute-done.ahead, bf16[4,3,128,256]{3,2,1,0:T(8,128)(2,1)S(1)} %shard_map.69.state), custom_call_target="tpu_custom_call" | custom-call | tf_op jit(solution)/shard_map/pallas_call | solution.py:314
  24.7 2.1 %collective-permute-start.5 = (bf16[256,256]{1,0:T(8,128)(2,1)S(1)}, bf16[256,256]{1,0:T(8,128)(2,1)S(1)}, u32[]{:S(2)}, u32[]{:S(2)}) collective-permute-start(bf16[256,256]{1,0:T(8,128)(2,1)S(1)} %get-tuple-element.18), channel_id=1, source_target_pairs={{0,1},{1,0},{2,3},{3,2},{4,5},{5,4},{6,7},{7,6},{8,9},{9,8},{10,11... | collective-permute-start | bytes 393224 | tf_op jit(solution)/shard_map/ppermute | solution.py:21
  26.8 1.0 %collective-permute-done.5 = bf16[256,256]{1,0:T(8,128)(2,1)S(1)} collective-permute-done((bf16[256,256]{1,0:T(8,128)(2,1)S(1)}, bf16[256,256]{1,0:T(8,128)(2,1)S(1)}, u32[]{:S(2)}, u32[]{:S(2)}) %collective-permute-start.5) | collective-permute-done | bytes 131104 | tf_op jit(solution)/shard_map/ppermute | solution.py:21
  27.8 1.3 %collective-permute-start.6 = (bf16[256,256]{1,0:T(8,128)(2,1)S(1)}, bf16[256,256]{1,0:T(8,128)(2,1)S(1)}, u32[]{:S(2)}, u32[]{:S(2)}) collective-permute-start(bf16[256,256]{1,0:T(8,128)(2,1)S(1)} %add_convert_fusion.own), channel_id=1, source_target_pairs={{0,2},{1,5},{2,0},{3,7},{4,6},{5,1},{6,4},{7,3},{8,10},{9,13},{10,... | collective-permute-start | bytes 393224 | tf_op jit(solution)/shard_map/ppermute | solution.py:404
  29.2 0.3 collective-permute-start.8
  29.5 4.1 %collective-permute-done.6.straight = bf16[256,256]{1,0:T(8,128)(2,1)S(1)} collective-permute-done((bf16[256,256]{1,0:T(8,128)(2,1)S(1)}, bf16[256,256]{1,0:T(8,128)(2,1)S(1)}, u32[]{:S(2)}, u32[]{:S(2)}) %collective-permute-start.6) | collective-permute-done | bytes 131104 | tf_op jit(solution)/shard_map/ppermute | solution.py:404
  33.6 0.0 collective-permute-start.7
  33.6 0.8 %collective-permute-done.8.diagonal = bf16[256,128]{1,0:T(8,128)(2,1)S(1)} collective-permute-done((bf16[256,128]{1,0:T(8,128)(2,1)S(1)}, bf16[256,128]{1,0:T(8,128)(2,1)S(1)}, u32[]{:S(2)}, u32[]{:S(2)}) %collective-permute-start.8) | collective-permute-done | bytes 65568 | tf_op jit(solution)/shard_map/ppermute | solution.py:404
  34.4 0.0 collective-permute-start.9
  34.4 1.3 %collective-permute-done.9.diagonal_other = bf16[256,128]{1,0:T(8,128)(2,1)S(1)} collective-permute-done((bf16[256,128]{1,0:T(8,128)(2,1)S(1)}, bf16[256,128]{1,0:T(8,128)(2,1)S(1)}, u32[]{:S(2)}, u32[]{:S(2)}) %collective-permute-start.9) | collective-permute-done | bytes 65568 | tf_op jit(solution)/shard_map/ppermute | solution.py:21
  35.7 0.0 collective-permute-done.7.straight_other
  35.7 0.9 %shard_map.71 = (bf16[256,256]{1,0:T(8,128)(2,1)S(1)}, f32[256,256]{1,0:T(8,128)S(1)}, bf16[256,256]{1,0:T(8,128)(2,1)}, bf16[256,128]{1,0:T(8,128)(2,1)S(1)}) custom-call(bf16[256,256]{1,0:T(8,128)(2,1)S(1)} %collective-permute-done.6.straight, bf16[256,256]{1,0:T(8,128)(2,1)S(1)} %collective-permute-done.7.straight_other, ...), custom_call_target="tpu_custom_call" | custom-call | tf_op jit(solution)/shard_map/pallas_call | solution.py:355
  36.6 2.4 %collective-permute-start.10 = (bf16[256,128]{1,0:T(8,128)(2,1)S(1)}, bf16[256,128]{1,0:T(8,128)(2,1)S(1)}, u32[]{:S(2)}, u32[]{:S(2)}) collective-permute-start(bf16[256,128]{1,0:T(8,128)(2,1)S(1)} %get-tuple-element.19), channel_id=1, source_target_pairs={{0,8},{4,12},{8,0},{12,4},{1,9},{5,13},{9,1},{13,5},{2,10},{6,14},... | collective-permute-start | bytes 196616 | tf_op jit(solution)/shard_map/ppermute | solution.py:21
  39.0 2.7 %collective-permute-done.10.got = bf16[256,128]{1,0:T(8,128)(2,1)S(1)} collective-permute-done((bf16[256,128]{1,0:T(8,128)(2,1)S(1)}, bf16[256,128]{1,0:T(8,128)(2,1)S(1)}, u32[]{:S(2)}, u32[]{:S(2)}) %collective-permute-start.10) | collective-permute-done | bytes 65568 | tf_op jit(solution)/shard_map/ppermute | solution.py:21
  41.8 1.3 %collective-permute-done.11.got_other = bf16[256,128]{1,0:T(8,128)(2,1)S(1)} collective-permute-done((bf16[256,128]{1,0:T(8,128)(2,1)S(1)}, bf16[256,128]{1,0:T(8,128)(2,1)S(1)}, u32[]{:S(2)}, u32[]{:S(2)}) %collective-permute-start.11) | collective-permute-done | bytes 65568 | tf_op jit(solution)/shard_map/ppermute | solution.py:21
  43.0 0.9 %shard_map.72 = f32[256,256]{1,0:T(8,128)} custom-call(bf16[256,128]{1,0:T(8,128)(2,1)S(1)} %collective-permute-done.10.got, bf16[256,128]{1,0:T(8,128)(2,1)S(1)} %collective-permute-done.11.got_other, bf16[256,256]{1,0:T(8,128)(2,1)S(1)} %get-tuple-element.20.tail, f32[256,256]{1,0:T(8,128)S(1)} %get-tuple-element.21.wide), custom_call_target="tpu_custom_call" | custom-call | tf_op jit(solution)/shard_map/pallas_call | solution.py:384
  (4 shorter events, 0.0 us)
Async XLA Ops:
  0.6 10.5 %collective-permute-start.3 = (bf16[4,3,128,256]{3,2,1,0:T(8,128)(2,1)}, bf16[4,3,128,256]{3,2,1,0:T(8,128)(2,1)S(1)}, u32[]{:S(2)}, u32[]{:S(2)}) collective-permute-start(bf16[4,3,128,256]{3,2,1,0:T(8,128)(2,1)} %bitcast.6), channel_id=1, source_target_pairs={{0,1},{1,0},{2,3},{3,2},{4,5},{5,4},{6,7},{7,6},{8,9},{9,8},{10,11... | collective-permute-start | bytes 2359304 | tf_op jit(solution)/shard_map/ppermute | solution.py:29
  1.1 15.9 %collective-permute-start.1 = (bf16[4,3,128,256]{3,2,1,0:T(8,128)(2,1)}, bf16[4,3,128,256]{3,2,1,0:T(8,128)(2,1)S(1)}, u32[]{:S(2)}, u32[]{:S(2)}) collective-permute-start(bf16[4,3,128,256]{3,2,1,0:T(8,128)(2,1)} %bitcast.7), channel_id=1, source_target_pairs={{1,2},{2,1},{5,6},{6,5},{9,10},{10,9},{13,14},{14,13},{17,18},{18,... | collective-permute-start | bytes 2359304 | tf_op jit(solution)/shard_map/ppermute | solution.py:29
  1.9 21.0 %collective-permute-start = (bf16[4,3,128,256]{3,2,1,0:T(8,128)(2,1)}, bf16[4,3,128,256]{3,2,1,0:T(8,128)(2,1)S(1)}, u32[]{:S(2)}, u32[]{:S(2)}) collective-permute-start(bf16[4,3,128,256]{3,2,1,0:T(8,128)(2,1)} %bitcast.8), channel_id=1, source_target_pairs={{4,0},{8,4},{12,8},{0,12},{5,1},{9,5},{13,9},{1,13},{6,2},{10,6},{... | collective-permute-start | bytes 2359304 | tf_op jit(solution)/shard_map/ppermute | solution.py:413
  7.3 3.8 %collective-permute-start.4 = (f32[4,3,4,128]{3,2,1,0:T(4,128)S(1)}, f32[4,3,4,128]{3,2,1,0:T(4,128)S(1)}, u32[]{:S(2)}, u32[]{:S(2)}) collective-permute-start(f32[4,3,4,128]{3,2,1,0:T(4,128)S(1)} %maximum_bitcast_fusion.own_fields), channel_id=1, source_target_pairs={{0,1},{1,0},{2,3},{3,2},{4,5},{5,4},{6,7},{7,6},{8,9},{9,8},{10,11... | collective-permute-start | bytes 73736 | tf_op jit(solution)/shard_map/ppermute | solution.py:29
  9.8 7.2 %collective-permute-start.2 = (f32[4,3,4,128]{3,2,1,0:T(4,128)S(1)}, f32[4,3,4,128]{3,2,1,0:T(4,128)S(1)}, u32[]{:S(2)}, u32[]{:S(2)}) collective-permute-start(f32[4,3,4,128]{3,2,1,0:T(4,128)S(1)} %maximum_bitcast_fusion.own_fields), channel_id=1, source_target_pairs={{1,2},{2,1},{5,6},{6,5},{9,10},{10,9},{13,14},{14,13},{17,18},{18,... | collective-permute-start | bytes 73736 | tf_op jit(solution)/shard_map/ppermute | solution.py:29
  11.1 1.1 %copy-start = (bf16[1,4,3,128,256]{4,3,2,1,0:T(8,128)(2,1)S(1)}, bf16[1,4,3,128,256]{4,3,2,1,0:T(8,128)(2,1)}, u32[]{:S(2)}) copy-start(bf16[1,4,3,128,256]{4,3,2,1,0:T(8,128)(2,1)} %param.5) | copy-start | bytes 2359300
  17.0 5.9 %copy-start.1 = (s32[4,16]{1,0:T(4,128)S(1)}, s32[4,16]{1,0:T(4,128)}, u32[]{:S(2)}) copy-start(s32[4,16]{1,0:T(4,128)} %order.1) | copy-start | bytes 772
  24.7 3.1 %collective-permute-start.5 = (bf16[256,256]{1,0:T(8,128)(2,1)S(1)}, bf16[256,256]{1,0:T(8,128)(2,1)S(1)}, u32[]{:S(2)}, u32[]{:S(2)}) collective-permute-start(bf16[256,256]{1,0:T(8,128)(2,1)S(1)} %get-tuple-element.18), channel_id=1, source_target_pairs={{0,1},{1,0},{2,3},{3,2},{4,5},{5,4},{6,7},{7,6},{8,9},{9,8},{10,11... | collective-permute-start | bytes 393224 | tf_op jit(solution)/shard_map/ppermute | solution.py:21
  27.8 5.7 %collective-permute-start.6 = (bf16[256,256]{1,0:T(8,128)(2,1)S(1)}, bf16[256,256]{1,0:T(8,128)(2,1)S(1)}, u32[]{:S(2)}, u32[]{:S(2)}) collective-permute-start(bf16[256,256]{1,0:T(8,128)(2,1)S(1)} %add_convert_fusion.own), channel_id=1, source_target_pairs={{0,2},{1,5},{2,0},{3,7},{4,6},{5,1},{6,4},{7,3},{8,10},{9,13},{10,... | collective-permute-start | bytes 393224 | tf_op jit(solution)/shard_map/ppermute | solution.py:404
  29.2 5.2 %collective-permute-start.8 = (bf16[256,128]{1,0:T(8,128)(2,1)S(1)}, bf16[256,128]{1,0:T(8,128)(2,1)S(1)}, u32[]{:S(2)}, u32[]{:S(2)}) collective-permute-start(bf16[256,128]{1,0:T(8,128)(2,1)S(1)} %slice_select_fusion), channel_id=1, source_target_pairs={{0,6},{1,7},{2,4},{3,5},{4,2},{5,3},{6,0},{7,1},{8,14},{9,15},{10,... | collective-permute-start | bytes 196616 | tf_op jit(solution)/shard_map/ppermute | solution.py:404
  33.6 2.1 %collective-permute-start.7 = (bf16[256,256]{1,0:T(8,128)(2,1)S(1)}, bf16[256,256]{1,0:T(8,128)(2,1)S(1)}, u32[]{:S(2)}, u32[]{:S(2)}) collective-permute-start(bf16[256,256]{1,0:T(8,128)(2,1)S(1)} %collective-permute-done.6.straight), channel_id=1, source_target_pairs={{0,1},{1,0},{2,3},{3,2},{4,5},{5,4},{6,7},{7,6},{8,9},{9,8},{10,11... | collective-permute-start | bytes 393224 | tf_op jit(solution)/shard_map/ppermute | solution.py:21
  34.4 1.3 %collective-permute-start.9 = (bf16[256,128]{1,0:T(8,128)(2,1)S(1)}, bf16[256,128]{1,0:T(8,128)(2,1)S(1)}, u32[]{:S(2)}, u32[]{:S(2)}) collective-permute-start(bf16[256,128]{1,0:T(8,128)(2,1)S(1)} %collective-permute-done.8.diagonal), channel_id=1, source_target_pairs={{0,1},{1,0},{2,3},{3,2},{4,5},{5,4},{6,7},{7,6},{8,9},{9,8},{10,11... | collective-permute-start | bytes 196616 | tf_op jit(solution)/shard_map/ppermute | solution.py:21
  36.6 5.2 %collective-permute-start.10 = (bf16[256,128]{1,0:T(8,128)(2,1)S(1)}, bf16[256,128]{1,0:T(8,128)(2,1)S(1)}, u32[]{:S(2)}, u32[]{:S(2)}) collective-permute-start(bf16[256,128]{1,0:T(8,128)(2,1)S(1)} %get-tuple-element.19), channel_id=1, source_target_pairs={{0,8},{4,12},{8,0},{12,4},{1,9},{5,13},{9,1},{13,5},{2,10},{6,14},... | collective-permute-start | bytes 196616 | tf_op jit(solution)/shard_map/ppermute | solution.py:21
  41.8 1.3 %collective-permute-start.11 = (bf16[256,128]{1,0:T(8,128)(2,1)S(1)}, bf16[256,128]{1,0:T(8,128)(2,1)S(1)}, u32[]{:S(2)}, u32[]{:S(2)}) collective-permute-start(bf16[256,128]{1,0:T(8,128)(2,1)S(1)} %collective-permute-done.10.got), channel_id=1, source_target_pairs={{0,1},{1,0},{2,3},{3,2},{4,5},{5,4},{6,7},{7,6},{8,9},{9,8},{10,11... | collective-permute-start | bytes 196616 | tf_op jit(solution)/shard_map/ppermute | solution.py:21

commit v4 on v3

v4 whole, which is shorter than its diff:
```python
import math

import jax
import jax.numpy as jnp
from jax import lax
from jax.experimental import pallas as pl
from jax.experimental.pallas import tpu as pltpu
from jax.sharding import PartitionSpec as P

K = 256
BLOCK = 16
STEPS = 4
HALF = K // 2

coupling = 0.35


def swap(value, axis, bit):
    size = lax.axis_size(axis)
    return lax.ppermute(value, axis, [(i, i ^ bit) for i in range(size)])


def exchange_pairs(value, axis, first):
    size = lax.axis_size(axis)
    route = []
    for i in range(first, size - 1, 2):
        route += [(i, i + 1), (i + 1, i)]
    return lax.ppermute(value, axis, route)


ROWS = 144
TOP = 8
CHUNK = 16
FIELDS = 4
NEAR_LAYERS = (6, 4, 2)


def spread_coefs(columns, column, out, plane):
    def field(k):
        return jnp.broadcast_to(columns[:, column + k : column + k + 1], (columns.shape[0], HALF))

    diffusion = field(0)
    along_u = field(1)
    along_y = field(2)
    along_z = field(3)
    out[plane, 0] = 1.0 - 6.0 * diffusion
    out[plane, 1] = diffusion - along_u
    out[plane, 2] = diffusion + along_u
    out[plane, 3] = diffusion - along_y
    out[plane, 4] = diffusion + along_y
    out[plane, 5] = diffusion - along_z
    out[plane, 6] = diffusion + along_z


def coef_columns(fields, odd, backward, table):
    ys, layers, zs = fields.shape[1:]
    table[...] = jnp.zeros_like(table)
    sign = jnp.where(odd, 0.5, -0.5)
    for k in range(layers):
        flipped = layers - 1 - k
        x = jnp.where(odd, flipped, k) if backward else jnp.where(odd, k, flipped)
        for y in range(ys):
            for f in range(FIELDS):
                row = fields[f, y, pl.ds(x, 1), :]
                if f == 1:
                    row = row * sign
                elif f > 1:
                    row = row * 0.5
                at = (k * ys + y) * FIELDS + f
                table[at : at + 1, :] = row
    return table[...].T


def unpack_layer(source, index, dest, slot):
    ys, zs = source.shape[1], source.shape[2]
    for y in range(ys):
        for h in range(2):
            lanes = slice(h * HALF, (h + 1) * HALF)
            value = source[index, y, :, lanes].astype(jnp.float32)
            dest[slot, y, h, TOP : TOP + zs, :] = value
            dest[slot, y, h, TOP - 1 : TOP, :] = value[zs - 1 : zs]
            dest[slot, y, h, TOP + zs : TOP + zs + 1, :] = value[0:1]


def step_layer(minus, here, plus, coefs, layer, active, store):
    level, slot = here
    ys = level.shape[1]
    zs = coefs.shape[2]
    for z in range(0, zs, CHUNK):
        rows = slice(TOP + z, TOP + z + CHUNK)
        centers = [[level[slot, y, h, rows, :] for h in range(2)] for y in range(ys)]
        for y in range(ys):
            factor = [coefs[layer * ys + y, k, z : z + CHUNK, :] for k in range(7)]
            for h in range(2):
                center = centers[y][h]
                new = factor[0] * center
                new += factor[1] * plus[0][plus[1], y, h, rows, :]
                new += factor[2] * minus[0][minus[1], y, h, rows, :]
                new += factor[3] * centers[(y + 1) % ys][h]
                new += factor[4] * centers[(y + ys - 1) % ys][h]
                new += factor[5] * level[slot, y, h, TOP + z + 1 : TOP + z + CHUNK + 1, :]
                new += factor[6] * level[slot, y, h, TOP + z - 1 : TOP + z + CHUNK - 1, :]
                if active is not None:
                    new = jnp.where(active, new, center)
                store(y, h, z, new.astype(jnp.bfloat16))


def into_level(dest, slot, zs):
    def store(y, h, z, rows):
        wide = rows.astype(jnp.float32)
        dest[slot, y, h, TOP + z : TOP + z + CHUNK, :] = wide
        if z == 0:
            dest[slot, y, h, TOP + zs : TOP + zs + 1, :] = wide[0:1]
        if z + CHUNK == zs:
            dest[slot, y, h, TOP - 1 : TOP, :] = wide[CHUNK - 1 : CHUNK]

    return store


def core_is_odd():
    return lax.axis_index("space") % 2 == 1


def coefs_kernel(
    own_fields, near_fields, start, order_home, own_coefs, near_coefs, order_here, order_next, own,
    table, order, columns, sems,
):
    fetch = pltpu.make_async_copy(start, own, sems.at[0])
    fetch_order = pltpu.make_async_copy(order_home, order, sems.at[1])
    fetch_order.start()
    fetch.start()
    odd = core_is_odd()
    ys = own_fields.shape[1]
    turned = coef_columns(own_fields, odd, False, table)
    for u in range(4):
        for y in range(ys):
            spread_coefs(turned, (u * ys + y) * FIELDS, own_coefs, u * ys + y)
    turned = coef_columns(near_fields, odd, True, table)
    for k in range(3):
        for y in range(ys):
            spread_coefs(turned, (k * ys + y) * FIELDS, near_coefs, (2 - k) * ys + y)

    fetch_order.wait()
    segments, blocks = order.shape
    block = lax.broadcasted_iota(jnp.int32, (blocks, K), 0)
    stored = lax.broadcasted_iota(jnp.int32, (blocks, K), 1)
    inside = jnp.where(lax.div(stored, BLOCK) == block, float(BLOCK), 0.0).astype(jnp.bfloat16)
    first = mul(order[...].astype(jnp.float32).astype(jnp.bfloat16), inside)
    offset = lax.rem(lax.broadcasted_iota(jnp.int32, first.shape, 1), BLOCK)
    columns[...] = first.astype(jnp.int32) + offset
    here = lax.axis_index("seg")
    after = lax.rem(here + 1, lax.axis_size("seg"))
    row = lax.broadcasted_iota(jnp.int32, (K, K), 0)
    for segment, out in ((here, order_here), (after, order_next)):
        out[...] = jnp.where(row == columns[pl.ds(segment, 1), :], 1.0, 0.0).astype(jnp.bfloat16)
    fetch.wait()


def near_kernel(counts, own, near, own_coefs, near_coefs, level0, level1, level2, level3):
    odd = core_is_odd()
    zs = own.shape[2]

    def fill(k, _):
        unpack_layer(near, jnp.where(odd, 3 - k, k), level0, 3 - k)
        unpack_layer(own, jnp.where(odd, k, 3 - k), level0, 4 + k)
        return 0

    lax.fori_loop(0, 4, fill, 0)
    levels = (level0, level1, level2, level3)
    for t, layers in enumerate(NEAR_LAYERS):
        source, dest = levels[t], levels[t + 1]
        active = None if t < 2 else counts[0] > t
        half = layers // 2

        def one(j, coefs, layer):
            refs = [(source, j + k) for k in range(3)]
            step_layer(*refs, coefs, layer, active, into_level(dest, j, zs))

        def near_one(j, _):
            one(j, near_coefs, j + t)
            return 0

        def own_one(j, _):
            one(half + j, own_coefs, j)
            return 0

        lax.fori_loop(0, half, near_one, 0)
        lax.fori_loop(0, half, own_one, 0)


def far_kernel(
    counts, far, far_fields, own_coefs, near0, near1, near2, near3,
    out, table, level0, level1, level2, level3, far_coefs,
):
    odd = core_is_odd()
    ys, zs = far.shape[1], far.shape[2]
    columns = coef_columns(far_fields, odd, True, table)
    for k in range(3):
        for y in range(ys):
            spread_coefs(columns, ((3 - k) * ys + y) * FIELDS, far_coefs, k * ys + y)

    def fill_far(k, _):
        unpack_layer(far, jnp.where(odd, k, 3 - k), level0, k)
        return 0

    lax.fori_loop(0, 4, fill_far, 0)
    nears = (near0, near1, near2, near3)
    levels = (level0, level1, level2, level3)
    for t in range(STEPS):
        near, source = nears[t], levels[t]
        end = near.shape[0]
        active = None if t < 2 else counts[0] > t

        def one(j, refs, is_far):
            if t < STEPS - 1:
                store = into_level(levels[t + 1], j, zs)
            else:
                place = jnp.where(odd, j, 3 - j)

                def store(y, h, z, rows):
                    out[place, y, z : z + CHUNK, h * HALF : (h + 1) * HALF] = rows

            if is_far:
                step_layer(*refs, far_coefs, j - t - 1, active, store)
            else:
                step_layer(*refs, own_coefs, 3 - t + j, active, store)

        one(0, ((near, end - 2), (near, end - 1), (source, 0)), False)
        one(1, ((near, end - 1), (source, 0), (source, 1)), t < 1)

        def own_one(j, _):
            one(j, [(source, j - 2 + k) for k in range(3)], False)
            return 0

        def far_one(j, _):
            one(j, [(source, j - 2 + k) for k in range(3)], True)
            return 0

        split = max(t + 1, 2)
        if split > 2:
            lax.fori_loop(2, split, own_one, 0)
        if split < 4:
            lax.fori_loop(split, 4, far_one, 0)


def mul(left, right):
    return jnp.dot(left, right, preferred_element_type=jnp.float32)


def to_bf16(value):
    return value.astype(jnp.bfloat16)


def to_f32(value):
    return value.astype(jnp.float32)


def product_kernel(ahead, state, order_next, order_here, image, out, sem):
    save = pltpu.make_async_copy(state, image, sem)
    save.start()
    left = ahead[...].reshape(-1, K)
    right = state[...].reshape(-1, K)
    raw = lax.dot_general(left, right, (((0,), (0,)), ((), ())), preferred_element_type=jnp.float32)
    raw = to_bf16(mul(order_next[...], to_bf16(raw)))
    turned = (((1,), (1,)), ((), ()))
    out[...] = to_bf16(lax.dot_general(raw, order_here[...], turned, preferred_element_type=jnp.float32))
    save.wait()


def specs(kinds):
    spaces = {"s": pltpu.SMEM, "v": pltpu.VMEM, "a": pl.ANY, "h": pltpu.HBM}
    return [pl.BlockSpec(memory_space=spaces[kind]) for kind in kinds]


def params(megabytes):
    return pltpu.CompilerParams(vmem_limit_bytes=megabytes * 2**20)


def cost(flops, read):
    return pl.CostEstimate(flops=int(flops), bytes_accessed=int(read), transcendentals=0)


def pinned(value):
    return pltpu.with_memory_space_constraint(value, pltpu.HBM)


def spread(fields, near_fields, start, order):
    zs = fields.shape[3]
    ys = fields.shape[1]

    def factors(layers):
        return jax.ShapeDtypeStruct((layers * ys, 7, zs, HALF), jnp.float32)

    perm = jax.ShapeDtypeStruct((K, K), jnp.bfloat16)
    return pl.pallas_call(
        coefs_kernel,
        out_shape=(factors(4), factors(3), perm, perm, jax.ShapeDtypeStruct(start.shape, start.dtype)),
        in_specs=specs("vvhh"),
        out_specs=tuple(specs("vvvvv")),
        scratch_shapes=[
            pltpu.VMEM((128, zs), jnp.float32),
            pltpu.VMEM(order.shape, jnp.int32),
            pltpu.VMEM((order.shape[0], K), jnp.int32),
            pltpu.SemaphoreType.DMA((2,)),
        ],
        compiler_params=params(8),
        cost_estimate=cost(0, 6 * 2**20),
    )(fields, near_fields, pinned(start), pinned(order))


def near_steps(counts, start, near, own_coefs, near_coefs):
    ys = start.shape[1]
    return pl.pallas_call(
        near_kernel,
        out_shape=tuple(
            jax.ShapeDtypeStruct((layers, ys, 2, ROWS, HALF), jnp.float32) for layers in (8, *NEAR_LAYERS)
        ),
        in_specs=specs("svvvv"),
        out_specs=tuple(specs("vvvv")),
        compiler_params=params(8),
        cost_estimate=cost(0, 0),
    )(counts, start, near, own_coefs, near_coefs)


def far_steps(counts, far, far_fields, own_coefs, levels):
    ys, zs = far.shape[1], far.shape[2]
    level = pltpu.VMEM((4, ys, 2, ROWS, HALF), jnp.float32)
    return pl.pallas_call(
        far_kernel,
        out_shape=jax.ShapeDtypeStruct(far.shape, far.dtype),
        in_specs=specs("svvvvvvv"),
        out_specs=specs("v")[0],
        scratch_shapes=[pltpu.VMEM((128, zs), jnp.float32)]
        + [level] * 4
        + [pltpu.VMEM((3 * ys, 7, zs, HALF), jnp.float32)],
        compiler_params=params(24),
        cost_estimate=cost(0, 0),
    )(counts, far, far_fields, own_coefs, *levels)


def products(ahead, state, order_next, order_here):
    return pl.pallas_call(
        product_kernel,
        out_shape=(
            jax.ShapeDtypeStruct(state.shape, state.dtype),
            jax.ShapeDtypeStruct((K, K), jnp.bfloat16),
        ),
        in_specs=specs("vvvv"),
        out_specs=tuple(specs("av")),
        scratch_shapes=[pltpu.SemaphoreType.DMA],
        compiler_params=params(16),
        cost_estimate=cost(0, 0),
    )(ahead, state, order_next, order_here)


def mixed_swap(value, along, across, core_along):
    total, slabs = lax.axis_size("seg"), lax.axis_size("space")
    route = []
    for s in range(total):
        for x in range(slabs):
            if core_along:
                to = (s ^ along, x) if x % 2 else (s, x ^ across)
            else:
                to = (s ^ along, x ^ across)
            route.append((s * slabs + x, to[0] * slabs + to[1]))
    return lax.ppermute(value, ("seg", "space"), route)


def per_device(basis, diffusivity, velocity, step_counts, block_order):
    start = basis[0]
    total = lax.axis_size("seg")
    slabs = lax.axis_size("space")
    cells = start.shape[0] * slabs * start.shape[1] * start.shape[2]

    ahead = lax.ppermute(start, "seg", [((i + 1) % total, i) for i in range(total)])
    fields = jnp.concatenate([diffusivity, velocity[0]], axis=0).transpose(0, 2, 1, 3)
    far = exchange_pairs(start, "space", 1)
    near = exchange_pairs(start, "space", 0)
    far_fields = exchange_pairs(fields, "space", 1)
    near_fields = exchange_pairs(fields, "space", 0)
    own_coefs, near_coefs, order_here, order_next, own = spread(fields, near_fields, start, block_order)
    levels = near_steps(step_counts, own, near, own_coefs, near_coefs)
    state = far_steps(step_counts, far, far_fields, own_coefs, levels)
    image, raw = products(ahead, state, order_next, order_here)

    bit = 1
    while 2 * bit < slabs:
        raw = to_bf16(to_f32(raw) + to_f32(swap(raw, "space", bit)))
        bit *= 2
    odd = lax.axis_index("space") % 2 == 1

    def my_half(full):
        return jnp.where(odd, full[:, HALF:], full[:, :HALF])

    def both_halves(part):
        rest = swap(part, "space", 1)
        return jnp.where(odd, jnp.concatenate([rest, part], 1), jnp.concatenate([part, rest], 1))

    straight = mixed_swap(raw, 1, bit, True)
    diagonal = mixed_swap(my_half(raw), 1, bit, False)
    straight_other = swap(straight, "space", 1)
    diagonal_other = swap(diagonal, "space", 1)
    scale = coupling / math.sqrt(K * cells)
    across = jnp.where(odd, straight_other, straight)
    along = jnp.where(odd, straight, straight_other)
    diagonal = jnp.where(odd, jnp.concatenate([diagonal_other, diagonal], 1), jnp.concatenate([diagonal, diagonal_other], 1))
    mine = to_bf16((to_f32(raw) + to_f32(across)) * scale)
    theirs = to_bf16((to_f32(along) + to_f32(diagonal)) * scale)
    def chained(later, earlier):
        return to_f32(later) + to_f32(earlier) + mul(later, earlier)

    upper = lax.axis_index("seg") % 2 == 1
    later = jnp.where(upper, mine, theirs)
    earlier = jnp.where(upper, theirs, mine)
    half = to_bf16(to_f32(my_half(later)) + to_f32(my_half(earlier)) + mul(later, my_half(earlier)))
    block = chained(later, earlier)
    wide = jnp.where(upper, block, to_f32(mine))
    bit = 2
    while bit < total:
        upper = (lax.axis_index("seg") // bit) % 2 == 1
        got = both_halves(swap(half, "seg", bit))
        wide = jnp.where(upper, wide + to_f32(got) + mul(to_bf16(wide), got), wide)
        block = to_bf16(block)
        later = jnp.where(upper, block, got)
        earlier = jnp.where(upper, got, block)
        block = chained(later, earlier)
        half = to_bf16(my_half(block))
        bit *= 2
    monodromy = wide + jnp.eye(K, dtype=jnp.float32)
    return (image[None], monodromy[None])


def solution(mesh):
    in_specs = (
        P(("groups", "seg"), "space", None, None, None),
        P(("groups", "seg"), "space", None, None),
        P(("groups", "seg"), None, "space", None, None),
        P(("groups", "seg")),
        P("groups", None),
    )
    out_specs = (P(("groups", "seg"), "space", None, None, None), P(("groups", "seg"), None, None))
    return jax.shard_map(
        per_device, mesh=mesh, in_specs=in_specs, out_specs=out_specs, check_vma=False
    )
```

time: 44.2 us -> 42.7 us (0.966)
  Pallas kernels: 12.9 us -> 11.6 us
  matrix products: 0 us -> 1.28 us
  local copies, waits for them, and re-layouts: 1.13 us -> 0 us
  waiting for transfers between devices: 12.5 us -> 11.9 us
    dot_general x0 -> x3, matrix products: none -> 1.28 us  [mul(): return jnp.dot(left, right, preferred_element_type=jnp.float32)]
    unnamed x4 -> x0, local copies, waits for them, and re-layouts: 1.13 us -> none
    pallas_call x1, Pallas kernels: 1.84 us -> 0.91 us  [products(): pl.pallas_call(product_kernel, out_shape=(jax.ShapeDtypeStruct(state.shap...]
    pallas_call x3 -> x2, Pallas kernels: 6.6 us -> 5.79 us  [the longest x1 3.13 us: near_steps(): pl.pallas_call(near_kernel, out_shape=tuple((jax.ShapeDtypeStruct((layers...]
    pallas_call x1, Pallas kernels: 4.48 us -> 4.93 us  [far_steps(): pl.pallas_call(far_kernel, out_shape=jax.ShapeDtypeStruct(far.shape, far....]
  transfers between devices with their start and end apart: 12 -> 12, of which waited for: 7 -> 7; matrix products, arithmetic and copies ran while one was open for 2% -> 2% of each run, Pallas kernels for 21% -> 25%
where the time goes in v4:
time: 42.7 us; the launch traced here: 42.5 us
  starting transfers between devices  15.3 us (36%)
  waiting for transfers between devices  11.9 us (28%)
  Pallas kernels  11.6 us (27%)
  between operations  1.39 us (3%)
  matrix products  1.28 us (3%)
  other arithmetic  0.93 us (2%)
    ppermute x5, waiting for transfers between devices, swap(): return lax.ppermute(value, axis, [(i, i ^ bit) for i in range(size)])  6.01 us
    pallas_call x1, Pallas kernels, far_steps(): pl.pallas_call(far_kernel, out_shape=jax.ShapeDtypeStruct(far.shape, far....  4.93 us
    ppermute x2, waiting for transfers between devices, mixed_swap(): return lax.ppermute(value, ('seg', 'space'), route)  4.89 us
    ppermute x1, starting transfers between devices, per_device(): lax.ppermute(start, 'seg', [((i + 1) % total, i) for i in range(total)])  4.68 us
    ppermute x5, starting transfers between devices, swap(): return lax.ppermute(value, axis, [(i, i ^ bit) for i in range(size)])  4.6 us
    ppermute x4, starting transfers between devices, exchange_pairs(): return lax.ppermute(value, axis, route)  4.39 us
    pallas_call x1, Pallas kernels, near_steps(): pl.pallas_call(near_kernel, out_shape=tuple((jax.ShapeDtypeStruct((layers...  3.13 us
    pallas_call x1, Pallas kernels, spread(): pl.pallas_call(coefs_kernel, out_shape=(factors(4), factors(3), perm, per...  2.67 us
  transfers between devices with their start and end apart: 12, of which 7 were waited for; matrix products, arithmetic and copies ran while one was open for 2% of the time, Pallas kernels for 25%

profile of v4, /device:TPU:0, one launch (start us, length us, event | category | flops | bytes accessed | tf_op | source)
XLA Modules:
  0.0 42.5 jit_solution(16856880336431650081)
XLA Ops:
  0.6 0.5 %collective-permute-start.4 = (bf16[4,3,128,256]{3,2,1,0:T(8,128)(2,1)}, bf16[4,3,128,256]{3,2,1,0:T(8,128)(2,1)S(1)}, u32[]{:S(2)}, u32[]{:S(2)}) collective-permute-start(bf16[4,3,128,256]{3,2,1,0:T(8,128)(2,1)} %bitcast.8), channel_id=1, source_target_pairs={{0,1},{1,0},{2,3},{3,2},{4,5},{5,4},{6,7},{7,6},{8,9},{9,8},{10,11... | collective-permute-start | bytes 2359304 | tf_op jit(solution)/shard_map/ppermute | solution.py:28
  1.1 0.7 %collective-permute-start.1 = (bf16[4,3,128,256]{3,2,1,0:T(8,128)(2,1)}, bf16[4,3,128,256]{3,2,1,0:T(8,128)(2,1)S(1)}, u32[]{:S(2)}, u32[]{:S(2)}) collective-permute-start(bf16[4,3,128,256]{3,2,1,0:T(8,128)(2,1)} %bitcast.9), channel_id=1, source_target_pairs={{1,2},{2,1},{5,6},{6,5},{9,10},{10,9},{13,14},{14,13},{17,18},{18,... | collective-permute-start | bytes 2359304 | tf_op jit(solution)/shard_map/ppermute | solution.py:28
  1.9 4.7 %collective-permute-start = (bf16[4,3,128,256]{3,2,1,0:T(8,128)(2,1)}, bf16[4,3,128,256]{3,2,1,0:T(8,128)(2,1)S(1)}, u32[]{:S(2)}, u32[]{:S(2)}) collective-permute-start(bf16[4,3,128,256]{3,2,1,0:T(8,128)(2,1)} %bitcast.10), channel_id=1, source_target_pairs={{4,0},{8,4},{12,8},{0,12},{5,1},{9,5},{13,9},{1,13},{6,2},{10,6},{... | collective-permute-start | bytes 2359304 | tf_op jit(solution)/shard_map/ppermute | solution.py:375
  6.5 0.7 %maximum_bitcast_fusion.own_fields = f32[4,3,4,128]{3,2,1,0:T(4,128)S(1)} fusion(f32[3,4,3,128]{3,1,2,0:T(4,128)} %bitcast.12, f32[1,4,3,128]{3,1,2,0:T(4,128)} %param.6), kind=kLoop, calls=%fused_computation.21 | loop fusion | flops 6144 | bytes 49152 | tf_op jit(solution)/shard_map/transpose | solution.py:376
  7.3 2.5 %collective-permute-start.3 = (f32[4,3,4,128]{3,2,1,0:T(4,128)S(1)}, f32[4,3,4,128]{3,2,1,0:T(4,128)S(1)}, u32[]{:S(2)}, u32[]{:S(2)}) collective-permute-start(f32[4,3,4,128]{3,2,1,0:T(4,128)S(1)} %maximum_bitcast_fusion.own_fields), channel_id=1, source_target_pairs={{0,1},{1,0},{2,3},{3,2},{4,5},{5,4},{6,7},{7,6},{8,9},{9,8},{10,11... | collective-permute-start | bytes 73736 | tf_op jit(solution)/shard_map/ppermute | solution.py:28
  9.8 0.7 %collective-permute-start.2 = (f32[4,3,4,128]{3,2,1,0:T(4,128)S(1)}, f32[4,3,4,128]{3,2,1,0:T(4,128)S(1)}, u32[]{:S(2)}, u32[]{:S(2)}) collective-permute-start(f32[4,3,4,128]{3,2,1,0:T(4,128)S(1)} %maximum_bitcast_fusion.own_fields), channel_id=1, source_target_pairs={{1,2},{2,1},{5,6},{6,5},{9,10},{10,9},{13,14},{14,13},{17,18},{18,... | collective-permute-start | bytes 73736 | tf_op jit(solution)/shard_map/ppermute | solution.py:28
  11.1 0.0 collective-permute-done.3.near_fields
  11.1 2.7 %shard_map.68 = (f32[12,7,128,128]{3,2,1,0:T(8,128)S(1)}, f32[9,7,128,128]{3,2,1,0:T(8,128)S(1)}, bf16[256,256]{1,0:T(8,128)(2,1)S(1)}, bf16[256,256]{1,0:T(8,128)(2,1)S(1)}, bf16[4,3,128,256]{3,2,1,0:T(8,128)(2,1)S(1)}) custom-call(f32[4,3,4,128]{3,2,1,0:T(4,128)S(1)} %maximum_bitcast_fusion.own_fields, ...), custom_call_target="tpu_custom_call" | custom-call | bytes 6291456 | tf_op jit(solution)/shard_map/pallas_call | solution.py:295
  13.8 0.0 collective-permute-done.4.near
  13.8 3.1 %shard_map.69 = (f32[8,3,2,144,128]{4,3,2,1,0:T(8,128)S(1)}, f32[6,3,2,144,128]{4,3,2,1,0:T(8,128)S(1)}, f32[4,3,2,144,128]{4,3,2,1,0:T(8,128)S(1)}, f32[2,3,2,144,128]{4,3,2,1,0:T(8,128)S(1)}) custom-call(s32[1]{0:T(128)S(6)} %copy.7.counts, bf16[4,3,128,256]{3,2,1,0:T(8,128)(2,1)S(1)} %get-tuple-element.14.own, ...), custom_call_target="tpu_custom_call" | custom-call | tf_op jit(solution)/shard_map/pallas_call | solution.py:313
  16.9 0.0 collective-permute-done.2.far_fields
  16.9 0.0 collective-permute-done.1.far
  16.9 4.9 %shard_map.70.state = bf16[4,3,128,256]{3,2,1,0:T(8,128)(2,1)S(1)} custom-call(s32[1]{0:T(128)S(6)} %copy.7.counts, bf16[4,3,128,256]{3,2,1,0:T(8,128)(2,1)S(1)} %collective-permute-done.1.far, f32[4,3,4,128]{3,2,1,0:T(4,128)S(1)} %collective-permute-done.2.far_fields, f32[12,7,128,128]{3,2,1,0:T(8,128)S(1)} %get-tuple-element.13.own_coefs, ...), custom_call_target="tpu_custom_call" | custom-call | tf_op jit(solution)/shard_map/pallas_call | solution.py:328
  21.9 1.0 %collective-permute-done.ahead = bf16[4,3,128,256]{3,2,1,0:T(8,128)(2,1)S(1)} collective-permute-done((bf16[4,3,128,256]{3,2,1,0:T(8,128)(2,1)}, bf16[4,3,128,256]{3,2,1,0:T(8,128)(2,1)S(1)}, u32[]{:S(2)}, u32[]{:S(2)}) %collective-permute-start) | collective-permute-done | bytes 786464 | tf_op jit(solution)/shard_map/ppermute | solution.py:375
  22.9 0.9 %shard_map.71 = (bf16[4,3,128,256]{3,2,1,0:T(8,128)(2,1)}, bf16[256,256]{1,0:T(8,128)(2,1)S(1)}) custom-call(bf16[4,3,128,256]{3,2,1,0:T(8,128)(2,1)S(1)} %collective-permute-done.ahead, bf16[4,3,128,256]{3,2,1,0:T(8,128)(2,1)S(1)} %shard_map.70.state, bf16[256,256]{1,0:T(8,128)(2,1)S(1)} %get-tuple-element.20.order_next, ...), custom_call_target="tpu_custom_call" | custom-call | tf_op jit(solution)/shard_map/pallas_call | solution.py:342
  23.8 2.1 %collective-permute-start.5 = (bf16[256,256]{1,0:T(8,128)(2,1)S(1)}, bf16[256,256]{1,0:T(8,128)(2,1)S(1)}, u32[]{:S(2)}, u32[]{:S(2)}) collective-permute-start(bf16[256,256]{1,0:T(8,128)(2,1)S(1)} %get-tuple-element.23), channel_id=1, source_target_pairs={{0,1},{1,0},{2,3},{3,2},{4,5},{5,4},{6,7},{7,6},{8,9},{9,8},{10,11... | collective-permute-start | bytes 393224 | tf_op jit(solution)/shard_map/ppermute | solution.py:20
  25.9 1.0 %collective-permute-done.5 = bf16[256,256]{1,0:T(8,128)(2,1)S(1)} collective-permute-done((bf16[256,256]{1,0:T(8,128)(2,1)S(1)}, bf16[256,256]{1,0:T(8,128)(2,1)S(1)}, u32[]{:S(2)}, u32[]{:S(2)}) %collective-permute-start.5) | collective-permute-done | bytes 131104 | tf_op jit(solution)/shard_map/ppermute | solution.py:20
  26.9 1.3 %collective-permute-start.6 = (bf16[256,256]{1,0:T(8,128)(2,1)S(1)}, bf16[256,256]{1,0:T(8,128)(2,1)S(1)}, u32[]{:S(2)}, u32[]{:S(2)}) collective-permute-start(bf16[256,256]{1,0:T(8,128)(2,1)S(1)} %add_convert_fusion), channel_id=1, source_target_pairs={{0,2},{1,5},{2,0},{3,7},{4,6},{5,1},{6,4},{7,3},{8,10},{9,13},{10,... | collective-permute-start | bytes 393224 | tf_op jit(solution)/shard_map/ppermute | solution.py:366
  28.2 0.3 collective-permute-start.8
  28.6 4.1 %collective-permute-done.6 = bf16[256,256]{1,0:T(8,128)(2,1)S(1)} collective-permute-done((bf16[256,256]{1,0:T(8,128)(2,1)S(1)}, bf16[256,256]{1,0:T(8,128)(2,1)S(1)}, u32[]{:S(2)}, u32[]{:S(2)}) %collective-permute-start.6) | collective-permute-done | bytes 131104 | tf_op jit(solution)/shard_map/ppermute | solution.py:366
  32.6 0.0 collective-permute-start.7
  32.6 0.8 %collective-permute-done.8 = bf16[256,128]{1,0:T(8,128)(2,1)S(1)} collective-permute-done((bf16[256,128]{1,0:T(8,128)(2,1)S(1)}, bf16[256,128]{1,0:T(8,128)(2,1)S(1)}, u32[]{:S(2)}, u32[]{:S(2)}) %collective-permute-start.8) | collective-permute-done | bytes 65568 | tf_op jit(solution)/shard_map/ppermute | solution.py:366
  33.5 0.0 collective-permute-start.9
  33.5 1.3 %collective-permute-done.9 = bf16[256,128]{1,0:T(8,128)(2,1)S(1)} collective-permute-done((bf16[256,128]{1,0:T(8,128)(2,1)S(1)}, bf16[256,128]{1,0:T(8,128)(2,1)S(1)}, u32[]{:S(2)}, u32[]{:S(2)}) %collective-permute-start.9) | collective-permute-done | bytes 65568 | tf_op jit(solution)/shard_map/ppermute | solution.py:20
  34.7 0.0 collective-permute-done.7
  34.7 0.1 broadcast_select_fusion
  34.9 0.2 fusion.1
  35.1 2.5 %collective-permute-start.10 = (bf16[256,128]{1,0:T(8,128)(2,1)S(1)}, bf16[256,128]{1,0:T(8,128)(2,1)S(1)}, u32[]{:S(2)}, u32[]{:S(2)}) collective-permute-start(bf16[256,128]{1,0:T(8,128)(2,1)S(1)} %fusion.1), channel_id=1, source_target_pairs={{0,8},{4,12},{8,0},{12,4},{1,9},{5,13},{9,1},{13,5},{2,10},{6,14},... | collective-permute-start | bytes 196616 | tf_op jit(solution)/shard_map/ppermute | solution.py:20
  37.6 2.7 %collective-permute-done.10 = bf16[256,128]{1,0:T(8,128)(2,1)S(1)} collective-permute-done((bf16[256,128]{1,0:T(8,128)(2,1)S(1)}, bf16[256,128]{1,0:T(8,128)(2,1)S(1)}, u32[]{:S(2)}, u32[]{:S(2)}) %collective-permute-start.10) | collective-permute-done | bytes 65568 | tf_op jit(solution)/shard_map/ppermute | solution.py:20
  40.3 0.2 fusion
  40.5 1.1 %collective-permute-done.11 = bf16[256,128]{1,0:T(8,128)(2,1)S(1)} collective-permute-done((bf16[256,128]{1,0:T(8,128)(2,1)S(1)}, bf16[256,128]{1,0:T(8,128)(2,1)S(1)}, u32[]{:S(2)}, u32[]{:S(2)}) %collective-permute-start.11) | collective-permute-done | bytes 65568 | tf_op jit(solution)/shard_map/ppermute | solution.py:20
  41.6 0.9 %add_bitcast_fusion = f32[1,256,256]{2,1,0:T(8,128)} fusion(f32[256,256]{1,0:T(8,128)S(1)} %fusion, bf16[256,128]{1,0:T(8,128)(2,1)S(1)} %collective-permute-done.11, bf16[256,128]{1,0:T(8,128)(2,1)S(1)} %collective-permute-done.10, pred[]{:T(512)S(6)} %eq.18, pred[]{:T(512)S(6)} %eq.16), kind=kOutput, calls=%fused_computation.4 | convolution fusion | flops 35258368 | bytes 655362 | tf_op jit(solution)/shard_map/dot_general | solution.py:247
  (4 shorter events, 0.1 us)
Async XLA Ops:
  0.6 13.2 %collective-permute-start.4 = (bf16[4,3,128,256]{3,2,1,0:T(8,128)(2,1)}, bf16[4,3,128,256]{3,2,1,0:T(8,128)(2,1)S(1)}, u32[]{:S(2)}, u32[]{:S(2)}) collective-permute-start(bf16[4,3,128,256]{3,2,1,0:T(8,128)(2,1)} %bitcast.8), channel_id=1, source_target_pairs={{0,1},{1,0},{2,3},{3,2},{4,5},{5,4},{6,7},{7,6},{8,9},{9,8},{10,11... | collective-permute-start | bytes 2359304 | tf_op jit(solution)/shard_map/ppermute | solution.py:28
  1.1 15.8 %collective-permute-start.1 = (bf16[4,3,128,256]{3,2,1,0:T(8,128)(2,1)}, bf16[4,3,128,256]{3,2,1,0:T(8,128)(2,1)S(1)}, u32[]{:S(2)}, u32[]{:S(2)}) collective-permute-start(bf16[4,3,128,256]{3,2,1,0:T(8,128)(2,1)} %bitcast.9), channel_id=1, source_target_pairs={{1,2},{2,1},{5,6},{6,5},{9,10},{10,9},{13,14},{14,13},{17,18},{18,... | collective-permute-start | bytes 2359304 | tf_op jit(solution)/shard_map/ppermute | solution.py:28
  1.9 21.0 %collective-permute-start = (bf16[4,3,128,256]{3,2,1,0:T(8,128)(2,1)}, bf16[4,3,128,256]{3,2,1,0:T(8,128)(2,1)S(1)}, u32[]{:S(2)}, u32[]{:S(2)}) collective-permute-start(bf16[4,3,128,256]{3,2,1,0:T(8,128)(2,1)} %bitcast.10), channel_id=1, source_target_pairs={{4,0},{8,4},{12,8},{0,12},{5,1},{9,5},{13,9},{1,13},{6,2},{10,6},{... | collective-permute-start | bytes 2359304 | tf_op jit(solution)/shard_map/ppermute | solution.py:375
  7.3 3.8 %collective-permute-start.3 = (f32[4,3,4,128]{3,2,1,0:T(4,128)S(1)}, f32[4,3,4,128]{3,2,1,0:T(4,128)S(1)}, u32[]{:S(2)}, u32[]{:S(2)}) collective-permute-start(f32[4,3,4,128]{3,2,1,0:T(4,128)S(1)} %maximum_bitcast_fusion.own_fields), channel_id=1, source_target_pairs={{0,1},{1,0},{2,3},{3,2},{4,5},{5,4},{6,7},{7,6},{8,9},{9,8},{10,11... | collective-permute-start | bytes 73736 | tf_op jit(solution)/shard_map/ppermute | solution.py:28
  9.8 7.1 %collective-permute-start.2 = (f32[4,3,4,128]{3,2,1,0:T(4,128)S(1)}, f32[4,3,4,128]{3,2,1,0:T(4,128)S(1)}, u32[]{:S(2)}, u32[]{:S(2)}) collective-permute-start(f32[4,3,4,128]{3,2,1,0:T(4,128)S(1)} %maximum_bitcast_fusion.own_fields), channel_id=1, source_target_pairs={{1,2},{2,1},{5,6},{6,5},{9,10},{10,9},{13,14},{14,13},{17,18},{18,... | collective-permute-start | bytes 73736 | tf_op jit(solution)/shard_map/ppermute | solution.py:28
  23.8 3.1 %collective-permute-start.5 = (bf16[256,256]{1,0:T(8,128)(2,1)S(1)}, bf16[256,256]{1,0:T(8,128)(2,1)S(1)}, u32[]{:S(2)}, u32[]{:S(2)}) collective-permute-start(bf16[256,256]{1,0:T(8,128)(2,1)S(1)} %get-tuple-element.23), channel_id=1, source_target_pairs={{0,1},{1,0},{2,3},{3,2},{4,5},{5,4},{6,7},{7,6},{8,9},{9,8},{10,11... | collective-permute-start | bytes 393224 | tf_op jit(solution)/shard_map/ppermute | solution.py:20
  26.9 5.7 %collective-permute-start.6 = (bf16[256,256]{1,0:T(8,128)(2,1)S(1)}, bf16[256,256]{1,0:T(8,128)(2,1)S(1)}, u32[]{:S(2)}, u32[]{:S(2)}) collective-permute-start(bf16[256,256]{1,0:T(8,128)(2,1)S(1)} %add_convert_fusion), channel_id=1, source_target_pairs={{0,2},{1,5},{2,0},{3,7},{4,6},{5,1},{6,4},{7,3},{8,10},{9,13},{10,... | collective-permute-start | bytes 393224 | tf_op jit(solution)/shard_map/ppermute | solution.py:366
  28.2 5.2 %collective-permute-start.8 = (bf16[256,128]{1,0:T(8,128)(2,1)S(1)}, bf16[256,128]{1,0:T(8,128)(2,1)S(1)}, u32[]{:S(2)}, u32[]{:S(2)}) collective-permute-start(bf16[256,128]{1,0:T(8,128)(2,1)S(1)} %slice_select_fusion.3), channel_id=1, source_target_pairs={{0,6},{1,7},{2,4},{3,5},{4,2},{5,3},{6,0},{7,1},{8,14},{9,15},{10,... | collective-permute-start | bytes 196616 | tf_op jit(solution)/shard_map/ppermute | solution.py:366
  32.6 2.1 %collective-permute-start.7 = (bf16[256,256]{1,0:T(8,128)(2,1)S(1)}, bf16[256,256]{1,0:T(8,128)(2,1)S(1)}, u32[]{:S(2)}, u32[]{:S(2)}) collective-permute-start(bf16[256,256]{1,0:T(8,128)(2,1)S(1)} %collective-permute-done.6), channel_id=1, source_target_pairs={{0,1},{1,0},{2,3},{3,2},{4,5},{5,4},{6,7},{7,6},{8,9},{9,8},{10,11... | collective-permute-start | bytes 393224 | tf_op jit(solution)/shard_map/ppermute | solution.py:20
  33.5 1.3 %collective-permute-start.9 = (bf16[256,128]{1,0:T(8,128)(2,1)S(1)}, bf16[256,128]{1,0:T(8,128)(2,1)S(1)}, u32[]{:S(2)}, u32[]{:S(2)}) collective-permute-start(bf16[256,128]{1,0:T(8,128)(2,1)S(1)} %collective-permute-done.8), channel_id=1, source_target_pairs={{0,1},{1,0},{2,3},{3,2},{4,5},{5,4},{6,7},{7,6},{8,9},{9,8},{10,11... | collective-permute-start | bytes 196616 | tf_op jit(solution)/shard_map/ppermute | solution.py:20
  35.1 5.2 %collective-permute-start.10 = (bf16[256,128]{1,0:T(8,128)(2,1)S(1)}, bf16[256,128]{1,0:T(8,128)(2,1)S(1)}, u32[]{:S(2)}, u32[]{:S(2)}) collective-permute-start(bf16[256,128]{1,0:T(8,128)(2,1)S(1)} %fusion.1), channel_id=1, source_target_pairs={{0,8},{4,12},{8,0},{12,4},{1,9},{5,13},{9,1},{13,5},{2,10},{6,14},... | collective-permute-start | bytes 196616 | tf_op jit(solution)/shard_map/ppermute | solution.py:20
  40.3 1.3 %collective-permute-start.11 = (bf16[256,128]{1,0:T(8,128)(2,1)S(1)}, bf16[256,128]{1,0:T(8,128)(2,1)S(1)}, u32[]{:S(2)}, u32[]{:S(2)}) collective-permute-start(bf16[256,128]{1,0:T(8,128)(2,1)S(1)} %collective-permute-done.10), channel_id=1, source_target_pairs={{0,1},{1,0},{2,3},{3,2},{4,5},{5,4},{6,7},{7,6},{8,9},{9,8},{10,11... | collective-permute-start | bytes 196616 | tf_op jit(solution)/shard_map/ppermute | solution.py:20

commit v5 on v4

--- a/solution.py
+++ b/solution.py
@@ -52,8 +52,8 @@
     out[plane, 6] = diffusion + along_z
 
 
-def coef_columns(fields, odd, backward, table):
-    ys, layers, zs = fields.shape[1:]
+def coef_columns(fields, ys, odd, backward, table):
+    layers = fields.shape[0] // (ys * FIELDS)
     table[...] = jnp.zeros_like(table)
     sign = jnp.where(odd, 0.5, -0.5)
     for k in range(layers):
@@ -61,7 +61,7 @@
         x = jnp.where(odd, flipped, k) if backward else jnp.where(odd, k, flipped)
         for y in range(ys):
             for f in range(FIELDS):
-                row = fields[f, y, pl.ds(x, 1), :]
+                row = fields[pl.ds((f * ys + y) * layers + x, 1), :]
                 if f == 1:
                     row = row * sign
                 elif f > 1:
@@ -71,12 +71,11 @@
     return table[...].T
 
 
-def unpack_layer(source, index, dest, slot):
-    ys, zs = source.shape[1], source.shape[2]
+def unpack_layer(source, index, ys, dest, slot):
+    zs = source.shape[1]
     for y in range(ys):
         for h in range(2):
-            lanes = slice(h * HALF, (h + 1) * HALF)
-            value = source[index, y, :, lanes].astype(jnp.float32)
+            value = source[index * ys + y, :, h * HALF : (h + 1) * HALF].astype(jnp.float32)
             dest[slot, y, h, TOP : TOP + zs, :] = value
             dest[slot, y, h, TOP - 1 : TOP, :] = value[zs - 1 : zs]
             dest[slot, y, h, TOP + zs : TOP + zs + 1, :] = value[0:1]
@@ -121,26 +120,72 @@
     return lax.axis_index("space") % 2 == 1
 
 
+def pack_kernel(start, diffusivity, velocity, first, second, fields, spread_home, drift_home, sems):
+    odd = core_is_odd()
+    half = second.shape[0]
+    here = jnp.where(odd, half, 0)
+    there = jnp.where(odd, 0, half)
+    small = (
+        pltpu.make_async_copy(diffusivity, spread_home, sems.at[0]),
+        pltpu.make_async_copy(velocity, drift_home, sems.at[1]),
+    )
+    copies = (
+        pltpu.make_async_copy(start.at[pl.ds(here, half)], first.at[pl.ds(0, half)], sems.at[2]),
+        pltpu.make_async_copy(start.at[pl.ds(there, half)], second, sems.at[3]),
+    )
+    for copy in small + copies:
+        copy.start()
+    for copy in small:
+        copy.wait()
+    ys, layers = spread_home.shape[0], spread_home.shape[1]
+    for y in range(ys):
+        for f in range(FIELDS):
+            at = (f * ys + y) * layers
+            fields[at : at + layers, :] = spread_home[y] if f == 0 else drift_home[f - 1, y]
+    value = fields[...]
+    high = to_bf16(value)
+    rest = value - to_f32(high)
+    middle = to_bf16(rest)
+    low = to_bf16(rest - to_f32(middle))
+    rows = value.shape[0]
+    first[half, :rows, :HALF] = high
+    first[half, :rows, HALF:] = middle
+    first[half, rows : 2 * rows, :HALF] = low
+    first[half, rows : 2 * rows, HALF:] = jnp.zeros_like(low)
+    if first.shape[1] > 2 * rows:
+        first[half, 2 * rows :, :] = jnp.zeros((first.shape[1] - 2 * rows, K), jnp.bfloat16)
+    for copy in copies:
+        copy.wait()
+
+
+def unpack_fields(packed, fields):
+    rows = fields.shape[0]
+    at = packed.shape[0] - 1
+    high = to_f32(packed[at, :rows, :HALF])
+    middle = to_f32(packed[at, :rows, HALF:])
+    low = to_f32(packed[at, rows : 2 * rows, :HALF])
+    fields[...] = high + (middle + low)
+
+
 def coefs_kernel(
-    own_fields, near_fields, start, order_home, own_coefs, near_coefs, order_here, order_next, own,
-    table, order, columns, sems,
+    own_fields, near_first, order_home, own_coefs, near_coefs, order_here, order_next,
+    near_fields, table, order, columns, sem,
 ):
-    fetch = pltpu.make_async_copy(start, own, sems.at[0])
-    fetch_order = pltpu.make_async_copy(order_home, order, sems.at[1])
-    fetch_order.start()
+    fetch = pltpu.make_async_copy(order_home, order, sem)
     fetch.start()
     odd = core_is_odd()
-    ys = own_fields.shape[1]
-    turned = coef_columns(own_fields, odd, False, table)
+    ys = own_coefs.shape[0] // 4
+    unpack_fields(near_first, near_fields)
+    turned = coef_columns(own_fields, ys, odd, False, table)
     for u in range(4):
         for y in range(ys):
             spread_coefs(turned, (u * ys + y) * FIELDS, own_coefs, u * ys + y)
-    turned = coef_columns(near_fields, odd, True, table)
+    turned = coef_columns(near_fields, ys, odd, True, table)
     for k in range(3):
         for y in range(ys):
             spread_coefs(turned, (k * ys + y) * FIELDS, near_coefs, (2 - k) * ys + y)
 
-    fetch_order.wait()
+    fetch.wait()
     segments, blocks = order.shape
     block = lax.broadcasted_iota(jnp.int32, (blocks, K), 0)
     stored = lax.broadcasted_iota(jnp.int32, (blocks, K), 1)
@@ -153,19 +198,25 @@
     row = lax.broadcasted_iota(jnp.int32, (K, K), 0)
     for segment, out in ((here, order_here), (after, order_next)):
         out[...] = jnp.where(row == columns[pl.ds(segment, 1), :], 1.0, 0.0).astype(jnp.bfloat16)
-    fetch.wait()
-
-
-def near_kernel(counts, own, near, own_coefs, near_coefs, level0, level1, level2, level3):
+
+
+def near_kernel(
+    counts, own_first, own_second, first, second, own_coefs, near_coefs, level0, level1, level2, level3
+):
     odd = core_is_odd()
-    zs = own.shape[2]
+    zs = own_coefs.shape[2]
+    ys = own_coefs.shape[0] // 4
 
     def fill(k, _):
-        unpack_layer(near, jnp.where(odd, 3 - k, k), level0, 3 - k)
-        unpack_layer(own, jnp.where(odd, k, 3 - k), level0, 4 + k)
+        backward = jnp.where(odd, 1 - k, k)
+        unpack_layer(second, backward, ys, level0, 3 - k)
+        unpack_layer(first, backward, ys, level0, 1 - k)
+        forward = jnp.where(odd, k, 1 - k)
+        unpack_layer(own_second, forward, ys, level0, 4 + k)
+        unpack_layer(own_first, forward, ys, level0, 6 + k)
         return 0
 
-    lax.fori_loop(0, 4, fill, 0)
+    lax.fori_loop(0, 2, fill, 0)
     levels = (level0, level1, level2, level3)
     for t, layers in enumerate(NEAR_LAYERS):
         source, dest = levels[t], levels[t + 1]
@@ -188,59 +239,72 @@
         lax.fori_loop(0, half, own_one, 0)
 
 
-def far_kernel(
-    counts, far, far_fields, own_coefs, near0, near1, near2, near3,
-    out, table, level0, level1, level2, level3, far_coefs,
+def two_layers(counts, befores, news, coefs_of, image, places):
+    zs = image.shape[2]
+    for t in range(STEPS):
+        before, new = befores[t], news[t]
+        end = before.shape[0]
+        active = None if t < 2 else counts[0] > t
+        window = ((before, end - 2), (before, end - 1), (new, 0), (new, 1))
+        for j in range(2):
+            if t < STEPS - 1:
+                store = into_level(news[t + 1], j, zs)
+            else:
+                place = places[j]
+
+                def store(y, h, z, rows):
+                    image[place, y, z : z + CHUNK, h * HALF : (h + 1) * HALF] = rows
+
+            step_layer(*window[j : j + 3], *coefs_of(t, j), active, store)
+
+
+def fill_pair(source, dest, ys):
+    odd = core_is_odd()
+
+    def fill(k, _):
+        unpack_layer(source, jnp.where(odd, k, 1 - k), ys, dest, k)
+        return 0
+
+    lax.fori_loop(0, 2, fill, 0)
+
+
+def first_kernel(
+    counts, first, own_coefs, near0, near1, near2, near3,
+    image, far_coefs, level0, level1, level2, level3, far_fields, table,
 ):
-    odd = core_is_odd()
-    ys, zs = far.shape[1], far.shape[2]
-    columns = coef_columns(far_fields, odd, True, table)
+    ys = image.shape[1]
+    unpack_fields(first, far_fields)
+    columns = coef_columns(far_fields, ys, core_is_odd(), True, table)
     for k in range(3):
         for y in range(ys):
             spread_coefs(columns, ((3 - k) * ys + y) * FIELDS, far_coefs, k * ys + y)
-
-    def fill_far(k, _):
-        unpack_layer(far, jnp.where(odd, k, 3 - k), level0, k)
-        return 0
-
-    lax.fori_loop(0, 4, fill_far, 0)
-    nears = (near0, near1, near2, near3)
-    levels = (level0, level1, level2, level3)
-    for t in range(STEPS):
-        near, source = nears[t], levels[t]
-        end = near.shape[0]
-        active = None if t < 2 else counts[0] > t
-
-        def one(j, refs, is_far):
-            if t < STEPS - 1:
-                store = into_level(levels[t + 1], j, zs)
-            else:
-                place = jnp.where(odd, j, 3 - j)
-
-                def store(y, h, z, rows):
-                    out[place, y, z : z + CHUNK, h * HALF : (h + 1) * HALF] = rows
-
-            if is_far:
-                step_layer(*refs, far_coefs, j - t - 1, active, store)
-            else:
-                step_layer(*refs, own_coefs, 3 - t + j, active, store)
-
-        one(0, ((near, end - 2), (near, end - 1), (source, 0)), False)
-        one(1, ((near, end - 1), (source, 0), (source, 1)), t < 1)
-
-        def own_one(j, _):
-            one(j, [(source, j - 2 + k) for k in range(3)], False)
-            return 0
-
-        def far_one(j, _):
-            one(j, [(source, j - 2 + k) for k in range(3)], True)
-            return 0
-
-        split = max(t + 1, 2)
-        if split > 2:
-            lax.fori_loop(2, split, own_one, 0)
-        if split < 4:
-            lax.fori_loop(split, 4, far_one, 0)
+    fill_pair(first, level0, ys)
+
+    def coefs_of(t, j):
+        u = 3 - t + j
+        return (own_coefs, u) if u < 4 else (far_coefs, u - 4)
+
+    odd = core_is_odd()
+    places = [jnp.where(odd, j, 1 - j) for j in range(2)]
+    two_layers(counts, (near0, near1, near2, near3), (level0, level1, level2, level3), coefs_of, image, places)
+
+
+def second_kernel(
+    counts, second, done, own_coefs, far_coefs, near0, near1, near2, near3, image, level0, level1, level2, level3
+):
+    ys = image.shape[1]
+    start = jnp.where(core_is_odd(), 0, 2)
+    for k in range(2):
+        image[start + k] = done[k]
+    fill_pair(second, level0, ys)
+
+    def coefs_of(t, j):
+        u = 5 - t + j
+        return (own_coefs, u) if u < 4 else (far_coefs, u - 4)
+
+    odd = core_is_odd()
+    places = [jnp.where(odd, 2 + j, 1 - j) for j in range(2)]
+    two_layers(counts, (near0, near1, near2, near3), (level0, level1, level2, level3), coefs_of, image, places)
 
 
 def mul(left, right):
@@ -284,58 +348,95 @@
     return pltpu.with_memory_space_constraint(value, pltpu.HBM)
 
 
-def spread(fields, near_fields, start, order):
-    zs = fields.shape[3]
-    ys = fields.shape[1]
-
-    def factors(layers):
-        return jax.ShapeDtypeStruct((layers * ys, 7, zs, HALF), jnp.float32)
-
+def pack(start, diffusivity, velocity):
+    planes, zs = start.shape[0], start.shape[1]
+    rows = diffusivity.shape[0] * diffusivity.shape[1] * FIELDS
+    return pl.pallas_call(
+        pack_kernel,
+        out_shape=(
+            jax.ShapeDtypeStruct((planes // 2 + 1, zs, K), jnp.bfloat16),
+            jax.ShapeDtypeStruct((planes // 2, zs, K), jnp.bfloat16),
+            jax.ShapeDtypeStruct((rows, zs), jnp.float32),
+        ),
+        in_specs=specs("hhh"),
+        out_specs=tuple(specs("vvv")),
+        scratch_shapes=[
+            pltpu.VMEM(diffusivity.shape, jnp.float32),
+            pltpu.VMEM(velocity.shape, jnp.float32),
+            pltpu.SemaphoreType.DMA((4,)),
+        ],
+        compiler_params=params(8),
+        cost_estimate=cost(0, 0),
+    )(pinned(start), pinned(diffusivity), pinned(velocity))
+
+
+def factors(layers, ys, zs):
+    return jax.ShapeDtypeStruct((layers * ys, 7, zs, HALF), jnp.float32)
+
+
+def level_shape(layers, ys):
+    return jax.ShapeDtypeStruct((layers, ys, 2, ROWS, HALF), jnp.float32)
+
+
+def spread(fields, near_first, order, ys):
+    zs = fields.shape[1]
     perm = jax.ShapeDtypeStruct((K, K), jnp.bfloat16)
     return pl.pallas_call(
         coefs_kernel,
-        out_shape=(factors(4), factors(3), perm, perm, jax.ShapeDtypeStruct(start.shape, start.dtype)),
-        in_specs=specs("vvhh"),
-        out_specs=tuple(specs("vvvvv")),
+        out_shape=(factors(4, ys, zs), factors(3, ys, zs), perm, perm),
+        in_specs=specs("vvh"),
+        out_specs=tuple(specs("vvvv")),
         scratch_shapes=[
+            pltpu.VMEM(fields.shape, jnp.float32),
             pltpu.VMEM((128, zs), jnp.float32),
             pltpu.VMEM(order.shape, jnp.int32),
             pltpu.VMEM((order.shape[0], K), jnp.int32),
-            pltpu.SemaphoreType.DMA((2,)),
+            pltpu.SemaphoreType.DMA,
         ],
         compiler_params=params(8),
-        cost_estimate=cost(0, 6 * 2**20),
-    )(fields, near_fields, pinned(start), pinned(order))
-
-
-def near_steps(counts, start, near, own_coefs, near_coefs):
-    ys = start.shape[1]
+        cost_estimate=cost(0, 0),
+    )(fields, near_first, pinned(order))
+
+
+def near_steps(counts, own_first, own_second, first, second, own_coefs, near_coefs, ys):
     return pl.pallas_call(
         near_kernel,
-        out_shape=tuple(
-            jax.ShapeDtypeStruct((layers, ys, 2, ROWS, HALF), jnp.float32) for layers in (8, *NEAR_LAYERS)
-        ),
-        in_specs=specs("svvvv"),
+        out_shape=tuple(level_shape(layers, ys) for layers in (8, *NEAR_LAYERS)),
+        in_specs=specs("svvvvvv"),
         out_specs=tuple(specs("vvvv")),
         compiler_params=params(8),
         cost_estimate=cost(0, 0),
-    )(counts, start, near, own_coefs, near_coefs)
-
-
-def far_steps(counts, far, far_fields, own_coefs, levels):
-    ys, zs = far.shape[1], far.shape[2]
-    level = pltpu.VMEM((4, ys, 2, ROWS, HALF), jnp.float32)
+    )(counts, own_first, own_second, first, second, own_coefs, near_coefs)
+
+
+def first_steps(counts, first, own_coefs, levels, shape, rows):
+    ys, zs = shape[1], shape[2]
     return pl.pallas_call(
-        far_kernel,
-        out_shape=jax.ShapeDtypeStruct(far.shape, far.dtype),
-        in_specs=specs("svvvvvvv"),
+        first_kernel,
+        out_shape=(
+            jax.ShapeDtypeStruct((2, *shape[1:]), jnp.bfloat16),
+            factors(3, ys, zs),
+            *[level_shape(2, ys)] * 4,
+        ),
+        in_specs=specs("svvvvvv"),
+        out_specs=tuple(specs("vvvvvv")),
+        scratch_shapes=[pltpu.VMEM((rows, zs), jnp.float32), pltpu.VMEM((128, zs), jnp.float32)],
+        compiler_params=params(8),
+        cost_estimate=cost(0, 0),
+    )(counts, first, own_coefs, *levels)
+
+
+def second_steps(counts, second, done, own_coefs, far_coefs, levels, shape):
+    ys = shape[1]
+    return pl.pallas_call(
+        second_kernel,
+        out_shape=jax.ShapeDtypeStruct(shape, jnp.bfloat16),
+        in_specs=specs("svvvvvvvv"),
         out_specs=specs("v")[0],
-        scratch_shapes=[pltpu.VMEM((128, zs), jnp.float32)]
-        + [level] * 4
-        + [pltpu.VMEM((3 * ys, 7, zs, HALF), jnp.float32)],
-        compiler_params=params(24),
+        scratch_shapes=[pltpu.VMEM((2, ys, 2, ROWS, HALF), jnp.float32)] * 4,
+        compiler_params=params(8),
         cost_estimate=cost(0, 0),
-    )(counts, far, far_fields, own_coefs, *levels)
+    )(counts, second, done, own_coefs, far_coefs, *levels)
 
 
 def products(ahead, state, order_next, order_here):
@@ -373,14 +474,19 @@
     cells = start.shape[0] * slabs * start.shape[1] * start.shape[2]
 
     ahead = lax.ppermute(start, "seg", [((i + 1) % total, i) for i in range(total)])
-    fields = jnp.concatenate([diffusivity, velocity[0]], axis=0).transpose(0, 2, 1, 3)
-    far = exchange_pairs(start, "space", 1)
-    near = exchange_pairs(start, "space", 0)
-    far_fields = exchange_pairs(fields, "space", 1)
-    near_fields = exchange_pairs(fields, "space", 0)
-    own_coefs, near_coefs, order_here, order_next, own = spread(fields, near_fields, start, block_order)
-    levels = near_steps(step_counts, own, near, own_coefs, near_coefs)
-    state = far_steps(step_counts, far, far_fields, own_coefs, levels)
+    ys, zs = start.shape[1], start.shape[2]
+    planes = start.reshape(-1, zs, K)
+    first, second, fields = pack(planes, diffusivity[0].transpose(1, 0, 2), velocity[0].transpose(0, 2, 1, 3))
+    near_first = exchange_pairs(first, "space", 0)
+    near_second = exchange_pairs(second, "space", 0)
+    far_first = exchange_pairs(first, "space", 1)
+    far_second = exchange_pairs(second, "space", 1)
+    own_coefs, near_coefs, order_here, order_next = spread(fields, near_first, block_order, ys)
+    levels = near_steps(step_counts, first, second, near_first, near_second, own_coefs, near_coefs, ys)
+    image_first, far_coefs, *levels = first_steps(
+        step_counts, far_first, own_coefs, levels, start.shape, fields.shape[0]
+    )
+    state = second_steps(step_counts, far_second, image_first, own_coefs, far_coefs, levels, start.shape)
     image, raw = products(ahead, state, order_next, order_here)
 
     bit = 1

time: 42.7 us -> 41.3 us (0.967)
  starting transfers between devices: 15.3 us -> 14.4 us
  waiting for transfers between devices: 11.9 us -> 12.7 us
  other arithmetic: 0.93 us -> 0.2 us
  Pallas kernels: 11.6 us -> 11 us
    ppermute x5, starting transfers between devices: 4.6 us -> 3.05 us  [swap(): return lax.ppermute(value, axis, [(i, i ^ bit) for i in range(size)])]
    ppermute x1, waiting for transfers between devices: 1 us -> 1.95 us  [per_device(): lax.ppermute(start, 'seg', [((i + 1) % total, i) for i in range(total)])]
    transpose x1 -> x0, other arithmetic: 0.73 us -> none  [per_device(): jnp.concatenate([diffusivity, velocity[0]], axis=0).transpose(0, 2, 1, 3)]
    pallas_call x3 -> x5, Pallas kernels: 10.7 us -> 10.1 us  [the longest x1 2.67 us: near_steps(): pl.pallas_call(near_kernel, out_shape=tuple((level_shape(layers, ys) for...]
  transfers between devices with their start and end apart: 12 -> 12, of which waited for: 7 -> 7; matrix products, arithmetic and copies ran while one was open for 2% -> 0% of each run, Pallas kernels for 25% -> 25%
where the time goes in v5:
time: 41.3 us; the launch traced here: 41 us
  starting transfers between devices  14.4 us (35%)
  waiting for transfers between devices  12.7 us (31%)
  Pallas kernels  11 us (27%)
  between operations  1.42 us (3%)
  matrix products  1.28 us (3%)
    ppermute x5, waiting for transfers between devices, swap(): return lax.ppermute(value, axis, [(i, i ^ bit) for i in range(size)])  5.94 us
    ppermute x1, starting transfers between devices, per_device(): lax.ppermute(start, 'seg', [((i + 1) % total, i) for i in range(total)])  5.1 us
    ppermute x2, waiting for transfers between devices, mixed_swap(): return lax.ppermute(value, ('seg', 'space'), route)  4.84 us
    ppermute x4, starting transfers between devices, exchange_pairs(): return lax.ppermute(value, axis, route)  4.32 us
    ppermute x5, starting transfers between devices, swap(): return lax.ppermute(value, axis, [(i, i ^ bit) for i in range(size)])  3.05 us
    pallas_call x1, Pallas kernels, near_steps(): pl.pallas_call(near_kernel, out_shape=tuple((level_shape(layers, ys) for...  2.67 us
    pallas_call x1, Pallas kernels, first_steps(): pl.pallas_call(first_kernel, out_shape=(jax.ShapeDtypeStruct((2, *shape[1...  2.5 us
    pallas_call x1, Pallas kernels, spread(): pl.pallas_call(coefs_kernel, out_shape=(factors(4, ys, zs), factors(3, ys...  2.07 us
  transfers between devices with their start and end apart: 12, of which 7 were waited for; matrix products, arithmetic and copies ran while one was open for 0% of the time, Pallas kernels for 25%

profile of v5, /device:TPU:0, one launch (start us, length us, event | category | flops | bytes accessed | tf_op | source)
XLA Modules:
  0.0 41.0 jit_solution(15126747048738155936)
XLA Ops:
  0.6 5.1 %collective-permute-start = (bf16[4,3,128,256]{3,2,1,0:T(8,128)(2,1)}, bf16[4,3,128,256]{3,2,1,0:T(8,128)(2,1)S(1)}, u32[]{:S(2)}, u32[]{:S(2)}) collective-permute-start(bf16[4,3,128,256]{3,2,1,0:T(8,128)(2,1)} %bitcast.12), channel_id=1, source_target_pairs={{4,0},{8,4},{12,8},{0,12},{5,1},{9,5},{13,9},{1,13},{6,2},{10,6},{... | collective-permute-start | bytes 2359304 | tf_op jit(solution)/shard_map/ppermute | solution.py:476
  5.7 1.2 %shard_map.68 = (bf16[7,128,256]{2,1,0:T(8,128)(2,1)S(1)}, bf16[6,128,256]{2,1,0:T(8,128)(2,1)S(1)}, f32[48,128]{1,0:T(8,128)S(1)}) custom-call(bf16[12,128,256]{2,1,0:T(8,128)(2,1)} %bitcast.13, f32[3,4,128]{2,1,0:T(4,128)} %bitcast.15, f32[3,3,4,128]{3,2,1,0:T(4,128)} %bitcast.14), custom_call_target="tpu_custom_call" | custom-call | tf_op jit(solution)/shard_map/pallas_call | solution.py:354
  6.9 0.1 collective-permute-start.3
  7.0 0.7 %collective-permute-start.2 = (bf16[7,128,256]{2,1,0:T(8,128)(2,1)S(1)}, bf16[7,128,256]{2,1,0:T(8,128)(2,1)S(1)}, u32[]{:S(2)}, u32[]{:S(2)}) collective-permute-start(bf16[7,128,256]{2,1,0:T(8,128)(2,1)S(1)} %get-tuple-element.22.own_first), channel_id=1, source_target_pairs={{1,2},{2,1},{5,6},{6,5},{9,10},{10,9},{13,14},{14,13},{17,18},{18,... | collective-permute-start | bytes 1376264 | tf_op jit(solution)/shard_map/ppermute | solution.py:28
  7.7 2.9 %collective-permute-start.4 = (bf16[6,128,256]{2,1,0:T(8,128)(2,1)S(1)}, bf16[6,128,256]{2,1,0:T(8,128)(2,1)S(1)}, u32[]{:S(2)}, u32[]{:S(2)}) collective-permute-start(bf16[6,128,256]{2,1,0:T(8,128)(2,1)S(1)} %get-tuple-element.21.own_second), channel_id=1, source_target_pairs={{0,1},{1,0},{2,3},{3,2},{4,5},{5,4},{6,7},{7,6},{8,9},{9,8},{10,11... | collective-permute-start | bytes 1179656 | tf_op jit(solution)/shard_map/ppermute | solution.py:28
  10.6 0.7 %collective-permute-start.1 = (bf16[6,128,256]{2,1,0:T(8,128)(2,1)S(1)}, bf16[6,128,256]{2,1,0:T(8,128)(2,1)S(1)}, u32[]{:S(2)}, u32[]{:S(2)}) collective-permute-start(bf16[6,128,256]{2,1,0:T(8,128)(2,1)S(1)} %get-tuple-element.21.own_second), channel_id=1, source_target_pairs={{1,2},{2,1},{5,6},{6,5},{9,10},{10,9},{13,14},{14,13},{17,18},{18,... | collective-permute-start | bytes 1179656 | tf_op jit(solution)/shard_map/ppermute | solution.py:28
  11.9 0.0 collective-permute-done.3.near_first.first
  11.9 2.1 %shard_map.69 = (f32[12,7,128,128]{3,2,1,0:T(8,128)S(1)}, f32[9,7,128,128]{3,2,1,0:T(8,128)S(1)}, bf16[256,256]{1,0:T(8,128)(2,1)S(1)}, bf16[256,256]{1,0:T(8,128)(2,1)S(1)}) custom-call(f32[48,128]{1,0:T(8,128)S(1)} %get-tuple-element.23.own_fields, bf16[7,128,256]{2,1,0:T(8,128)(2,1)S(1)} %collective-permute-done.3.near_first.first, s32[4,16]{1,0:T(4,128)} %order_home.1), custom_call_target="tpu_custom_call" | custom-call | tf_op jit(solution)/shard_map/pallas_call | solution.py:384
  14.0 0.0 collective-permute-done.4.second
  14.0 2.7 %shard_map.70 = (f32[8,3,2,144,128]{4,3,2,1,0:T(8,128)S(1)}, f32[6,3,2,144,128]{4,3,2,1,0:T(8,128)S(1)}, f32[4,3,2,144,128]{4,3,2,1,0:T(8,128)S(1)}, f32[2,3,2,144,128]{4,3,2,1,0:T(8,128)S(1)}) custom-call(s32[1]{0:T(128)S(6)} %copy.7.counts, bf16[7,128,256]{2,1,0:T(8,128)(2,1)S(1)} %get-tuple-element.22.own_first, ...), custom_call_target="tpu_custom_call" | custom-call | tf_op jit(solution)/shard_map/pallas_call | solution.py:402
  16.7 2.5 %shard_map.71 = (bf16[2,3,128,256]{3,2,1,0:T(8,128)(2,1)S(1)}, f32[9,7,128,128]{3,2,1,0:T(8,128)S(1)}, f32[2,3,2,144,128]{4,3,2,1,0:T(8,128)S(1)}, f32[2,3,2,144...) custom-call(s32[1]{0:T(128)S(6)} %copy.7.counts, ...), custom_call_target="tpu_custom_call" | custom-call | tf_op jit(solution)/shard_map/pallas_call | solution.py:414
  19.2 0.0 collective-permute-done.1.second
  19.2 1.7 %shard_map.72.state = bf16[4,3,128,256]{3,2,1,0:T(8,128)(2,1)S(1)} custom-call(s32[1]{0:T(128)S(6)} %copy.7.counts, bf16[6,128,256]{2,1,0:T(8,128)(2,1)S(1)} %collective-permute-done.1.second, bf16[2,3,128,256]{3,2,1,0:T(8,128)(2,1)S(1)} %get-tuple-element.30.done, f32[12,7,128,128]{3,2,1,0:T(8,128)S(1)} %get-tuple-element.24.own_coefs, ...), custom_call_target="tpu_custom_call" | custom-call | tf_op jit(solution)/shard_map/pallas_call | solution.py:431
  20.9 2.0 %collective-permute-done.ahead = bf16[4,3,128,256]{3,2,1,0:T(8,128)(2,1)S(1)} collective-permute-done((bf16[4,3,128,256]{3,2,1,0:T(8,128)(2,1)}, bf16[4,3,128,256]{3,2,1,0:T(8,128)(2,1)S(1)}, u32[]{:S(2)}, u32[]{:S(2)}) %collective-permute-start) | collective-permute-done | bytes 786464 | tf_op jit(solution)/shard_map/ppermute | solution.py:476
  22.8 0.9 %shard_map.73 = (bf16[4,3,128,256]{3,2,1,0:T(8,128)(2,1)}, bf16[256,256]{1,0:T(8,128)(2,1)S(1)}) custom-call(bf16[4,3,128,256]{3,2,1,0:T(8,128)(2,1)S(1)} %collective-permute-done.ahead, bf16[4,3,128,256]{3,2,1,0:T(8,128)(2,1)S(1)} %shard_map.72.state, bf16[256,256]{1,0:T(8,128)(2,1)S(1)} %get-tuple-element.36.order_next, ...), custom_call_target="tpu_custom_call" | custom-call | tf_op jit(solution)/shard_map/pallas_call | solution.py:443
  23.8 0.5 %collective-permute-start.5 = (bf16[256,256]{1,0:T(8,128)(2,1)S(1)}, bf16[256,256]{1,0:T(8,128)(2,1)S(1)}, u32[]{:S(2)}, u32[]{:S(2)}) collective-permute-start(bf16[256,256]{1,0:T(8,128)(2,1)S(1)} %get-tuple-element.39), channel_id=1, source_target_pairs={{0,1},{1,0},{2,3},{3,2},{4,5},{5,4},{6,7},{7,6},{8,9},{9,8},{10,11... | collective-permute-start | bytes 393224 | tf_op jit(solution)/shard_map/ppermute | solution.py:20
  24.2 1.0 %collective-permute-done.5 = bf16[256,256]{1,0:T(8,128)(2,1)S(1)} collective-permute-done((bf16[256,256]{1,0:T(8,128)(2,1)S(1)}, bf16[256,256]{1,0:T(8,128)(2,1)S(1)}, u32[]{:S(2)}, u32[]{:S(2)}) %collective-permute-start.5) | collective-permute-done | bytes 131104 | tf_op jit(solution)/shard_map/ppermute | solution.py:20
  25.2 1.5 %collective-permute-start.6 = (bf16[256,256]{1,0:T(8,128)(2,1)S(1)}, bf16[256,256]{1,0:T(8,128)(2,1)S(1)}, u32[]{:S(2)}, u32[]{:S(2)}) collective-permute-start(bf16[256,256]{1,0:T(8,128)(2,1)S(1)} %add_convert_fusion), channel_id=1, source_target_pairs={{0,2},{1,5},{2,0},{3,7},{4,6},{5,1},{6,4},{7,3},{8,10},{9,13},{10,... | collective-permute-start | bytes 393224 | tf_op jit(solution)/shard_map/ppermute | solution.py:467
  26.8 0.4 collective-permute-start.8
  27.2 3.5 %collective-permute-done.6 = bf16[256,256]{1,0:T(8,128)(2,1)S(1)} collective-permute-done((bf16[256,256]{1,0:T(8,128)(2,1)S(1)}, bf16[256,256]{1,0:T(8,128)(2,1)S(1)}, u32[]{:S(2)}, u32[]{:S(2)}) %collective-permute-start.6) | collective-permute-done | bytes 131104 | tf_op jit(solution)/shard_map/ppermute | solution.py:467
  30.7 1.3 %collective-permute-done.8 = bf16[256,128]{1,0:T(8,128)(2,1)S(1)} collective-permute-done((bf16[256,128]{1,0:T(8,128)(2,1)S(1)}, bf16[256,128]{1,0:T(8,128)(2,1)S(1)}, u32[]{:S(2)}, u32[]{:S(2)}) %collective-permute-start.8) | collective-permute-done | bytes 65568 | tf_op jit(solution)/shard_map/ppermute | solution.py:467
  32.0 0.0 collective-permute-start.9
  32.0 1.3 %collective-permute-done.9 = bf16[256,128]{1,0:T(8,128)(2,1)S(1)} collective-permute-done((bf16[256,128]{1,0:T(8,128)(2,1)S(1)}, bf16[256,128]{1,0:T(8,128)(2,1)S(1)}, u32[]{:S(2)}, u32[]{:S(2)}) %collective-permute-start.9) | collective-permute-done | bytes 65568 | tf_op jit(solution)/shard_map/ppermute | solution.py:20
  33.3 0.0 collective-permute-done.7
  33.3 0.1 broadcast_select_fusion
  33.4 0.2 fusion.1
  33.6 2.6 %collective-permute-start.10 = (bf16[256,128]{1,0:T(8,128)(2,1)S(1)}, bf16[256,128]{1,0:T(8,128)(2,1)S(1)}, u32[]{:S(2)}, u32[]{:S(2)}) collective-permute-start(bf16[256,128]{1,0:T(8,128)(2,1)S(1)} %fusion.1), channel_id=1, source_target_pairs={{0,8},{4,12},{8,0},{12,4},{1,9},{5,13},{9,1},{13,5},{2,10},{6,14},... | collective-permute-start | bytes 196616 | tf_op jit(solution)/shard_map/ppermute | solution.py:20
  36.2 2.7 %collective-permute-done.10 = bf16[256,128]{1,0:T(8,128)(2,1)S(1)} collective-permute-done((bf16[256,128]{1,0:T(8,128)(2,1)S(1)}, bf16[256,128]{1,0:T(8,128)(2,1)S(1)}, u32[]{:S(2)}, u32[]{:S(2)}) %collective-permute-start.10) | collective-permute-done | bytes 65568 | tf_op jit(solution)/shard_map/ppermute | solution.py:20
  38.9 0.0 collective-permute-start.11
  38.9 0.2 fusion
  39.1 1.0 %collective-permute-done.11 = bf16[256,128]{1,0:T(8,128)(2,1)S(1)} collective-permute-done((bf16[256,128]{1,0:T(8,128)(2,1)S(1)}, bf16[256,128]{1,0:T(8,128)(2,1)S(1)}, u32[]{:S(2)}, u32[]{:S(2)}) %collective-permute-start.11) | collective-permute-done | bytes 65568 | tf_op jit(solution)/shard_map/ppermute | solution.py:20
  40.1 0.9 %add_bitcast_fusion = f32[1,256,256]{2,1,0:T(8,128)} fusion(f32[256,256]{1,0:T(8,128)S(1)} %fusion, bf16[256,128]{1,0:T(8,128)(2,1)S(1)} %collective-permute-done.11, bf16[256,128]{1,0:T(8,128)(2,1)S(1)} %collective-permute-done.10, pred[]{:T(512)S(6)} %eq.18, pred[]{:T(512)S(6)} %eq.16), kind=kOutput, calls=%fused_computation.4 | convolution fusion | flops 35258368 | bytes 655362 | tf_op jit(solution)/shard_map/dot_general | solution.py:311
  (5 shorter events, 0.1 us)
Async XLA Ops:
  0.6 22.2 %collective-permute-start = (bf16[4,3,128,256]{3,2,1,0:T(8,128)(2,1)}, bf16[4,3,128,256]{3,2,1,0:T(8,128)(2,1)S(1)}, u32[]{:S(2)}, u32[]{:S(2)}) collective-permute-start(bf16[4,3,128,256]{3,2,1,0:T(8,128)(2,1)} %bitcast.12), channel_id=1, source_target_pairs={{4,0},{8,4},{12,8},{0,12},{5,1},{9,5},{13,9},{1,13},{6,2},{10,6},{... | collective-permute-start | bytes 2359304 | tf_op jit(solution)/shard_map/ppermute | solution.py:476
  6.9 5.0 %collective-permute-start.3 = (bf16[7,128,256]{2,1,0:T(8,128)(2,1)S(1)}, bf16[7,128,256]{2,1,0:T(8,128)(2,1)S(1)}, u32[]{:S(2)}, u32[]{:S(2)}) collective-permute-start(bf16[7,128,256]{2,1,0:T(8,128)(2,1)S(1)} %get-tuple-element.22.own_first), channel_id=1, source_target_pairs={{0,1},{1,0},{2,3},{3,2},{4,5},{5,4},{6,7},{7,6},{8,9},{9,8},{10,11... | collective-permute-start | bytes 1376264 | tf_op jit(solution)/shard_map/ppermute | solution.py:28
  7.0 9.7 %collective-permute-start.2 = (bf16[7,128,256]{2,1,0:T(8,128)(2,1)S(1)}, bf16[7,128,256]{2,1,0:T(8,128)(2,1)S(1)}, u32[]{:S(2)}, u32[]{:S(2)}) collective-permute-start(bf16[7,128,256]{2,1,0:T(8,128)(2,1)S(1)} %get-tuple-element.22.own_first), channel_id=1, source_target_pairs={{1,2},{2,1},{5,6},{6,5},{9,10},{10,9},{13,14},{14,13},{17,18},{18,... | collective-permute-start | bytes 1376264 | tf_op jit(solution)/shard_map/ppermute | solution.py:28
  7.7 6.3 %collective-permute-start.4 = (bf16[6,128,256]{2,1,0:T(8,128)(2,1)S(1)}, bf16[6,128,256]{2,1,0:T(8,128)(2,1)S(1)}, u32[]{:S(2)}, u32[]{:S(2)}) collective-permute-start(bf16[6,128,256]{2,1,0:T(8,128)(2,1)S(1)} %get-tuple-element.21.own_second), channel_id=1, source_target_pairs={{0,1},{1,0},{2,3},{3,2},{4,5},{5,4},{6,7},{7,6},{8,9},{9,8},{10,11... | collective-permute-start | bytes 1179656 | tf_op jit(solution)/shard_map/ppermute | solution.py:28
  10.6 8.6 %collective-permute-start.1 = (bf16[6,128,256]{2,1,0:T(8,128)(2,1)S(1)}, bf16[6,128,256]{2,1,0:T(8,128)(2,1)S(1)}, u32[]{:S(2)}, u32[]{:S(2)}) collective-permute-start(bf16[6,128,256]{2,1,0:T(8,128)(2,1)S(1)} %get-tuple-element.21.own_second), channel_id=1, source_target_pairs={{1,2},{2,1},{5,6},{6,5},{9,10},{10,9},{13,14},{14,13},{17,18},{18,... | collective-permute-start | bytes 1179656 | tf_op jit(solution)/shard_map/ppermute | solution.py:28
  23.8 1.5 %collective-permute-start.5 = (bf16[256,256]{1,0:T(8,128)(2,1)S(1)}, bf16[256,256]{1,0:T(8,128)(2,1)S(1)}, u32[]{:S(2)}, u32[]{:S(2)}) collective-permute-start(bf16[256,256]{1,0:T(8,128)(2,1)S(1)} %get-tuple-element.39), channel_id=1, source_target_pairs={{0,1},{1,0},{2,3},{3,2},{4,5},{5,4},{6,7},{7,6},{8,9},{9,8},{10,11... | collective-permute-start | bytes 393224 | tf_op jit(solution)/shard_map/ppermute | solution.py:20
  25.2 5.4 %collective-permute-start.6 = (bf16[256,256]{1,0:T(8,128)(2,1)S(1)}, bf16[256,256]{1,0:T(8,128)(2,1)S(1)}, u32[]{:S(2)}, u32[]{:S(2)}) collective-permute-start(bf16[256,256]{1,0:T(8,128)(2,1)S(1)} %add_convert_fusion), channel_id=1, source_target_pairs={{0,2},{1,5},{2,0},{3,7},{4,6},{5,1},{6,4},{7,3},{8,10},{9,13},{10,... | collective-permute-start | bytes 393224 | tf_op jit(solution)/shard_map/ppermute | solution.py:467
  26.8 5.2 %collective-permute-start.8 = (bf16[256,128]{1,0:T(8,128)(2,1)S(1)}, bf16[256,128]{1,0:T(8,128)(2,1)S(1)}, u32[]{:S(2)}, u32[]{:S(2)}) collective-permute-start(bf16[256,128]{1,0:T(8,128)(2,1)S(1)} %slice_select_fusion.3), channel_id=1, source_target_pairs={{0,6},{1,7},{2,4},{3,5},{4,2},{5,3},{6,0},{7,1},{8,14},{9,15},{10,... | collective-permute-start | bytes 196616 | tf_op jit(solution)/shard_map/ppermute | solution.py:467
  30.7 2.6 %collective-permute-start.7 = (bf16[256,256]{1,0:T(8,128)(2,1)S(1)}, bf16[256,256]{1,0:T(8,128)(2,1)S(1)}, u32[]{:S(2)}, u32[]{:S(2)}) collective-permute-start(bf16[256,256]{1,0:T(8,128)(2,1)S(1)} %collective-permute-done.6), channel_id=1, source_target_pairs={{0,1},{1,0},{2,3},{3,2},{4,5},{5,4},{6,7},{7,6},{8,9},{9,8},{10,11... | collective-permute-start | bytes 393224 | tf_op jit(solution)/shard_map/ppermute | solution.py:20
  32.0 1.3 %collective-permute-start.9 = (bf16[256,128]{1,0:T(8,128)(2,1)S(1)}, bf16[256,128]{1,0:T(8,128)(2,1)S(1)}, u32[]{:S(2)}, u32[]{:S(2)}) collective-permute-start(bf16[256,128]{1,0:T(8,128)(2,1)S(1)} %collective-permute-done.8), channel_id=1, source_target_pairs={{0,1},{1,0},{2,3},{3,2},{4,5},{5,4},{6,7},{7,6},{8,9},{9,8},{10,11... | collective-permute-start | bytes 196616 | tf_op jit(solution)/shard_map/ppermute | solution.py:20
  33.6 5.2 %collective-permute-start.10 = (bf16[256,128]{1,0:T(8,128)(2,1)S(1)}, bf16[256,128]{1,0:T(8,128)(2,1)S(1)}, u32[]{:S(2)}, u32[]{:S(2)}) collective-permute-start(bf16[256,128]{1,0:T(8,128)(2,1)S(1)} %fusion.1), channel_id=1, source_target_pairs={{0,8},{4,12},{8,0},{12,4},{1,9},{5,13},{9,1},{13,5},{2,10},{6,14},... | collective-permute-start | bytes 196616 | tf_op jit(solution)/shard_map/ppermute | solution.py:20
  38.9 1.3 %collective-permute-start.11 = (bf16[256,128]{1,0:T(8,128)(2,1)S(1)}, bf16[256,128]{1,0:T(8,128)(2,1)S(1)}, u32[]{:S(2)}, u32[]{:S(2)}) collective-permute-start(bf16[256,128]{1,0:T(8,128)(2,1)S(1)} %collective-permute-done.10), channel_id=1, source_target_pairs={{0,1},{1,0},{2,3},{3,2},{4,5},{5,4},{6,7},{7,6},{8,9},{9,8},{10,11... | collective-permute-start | bytes 196616 | tf_op jit(solution)/shard_map/ppermute | solution.py:20

commit v6 on v5

--- a/solution.py
+++ b/solution.py
@@ -319,16 +319,19 @@
     return value.astype(jnp.float32)
 
 
-def product_kernel(ahead, state, order_next, order_here, image, out, sem):
+def save_kernel(state, image, sem):
     save = pltpu.make_async_copy(state, image, sem)
     save.start()
+    save.wait()
+
+
+def product_kernel(ahead, state, order_next, order_here, out):
     left = ahead[...].reshape(-1, K)
     right = state[...].reshape(-1, K)
     raw = lax.dot_general(left, right, (((0,), (0,)), ((), ())), preferred_element_type=jnp.float32)
     raw = to_bf16(mul(order_next[...], to_bf16(raw)))
     turned = (((1,), (1,)), ((), ()))
     out[...] = to_bf16(lax.dot_general(raw, order_here[...], turned, preferred_element_type=jnp.float32))
-    save.wait()
 
 
 def specs(kinds):
@@ -442,16 +445,24 @@
 def products(ahead, state, order_next, order_here):
     return pl.pallas_call(
         product_kernel,
-        out_shape=(
-            jax.ShapeDtypeStruct(state.shape, state.dtype),
-            jax.ShapeDtypeStruct((K, K), jnp.bfloat16),
-        ),
+        out_shape=jax.ShapeDtypeStruct((K, K), jnp.bfloat16),
         in_specs=specs("vvvv"),
-        out_specs=tuple(specs("av")),
-        scratch_shapes=[pltpu.SemaphoreType.DMA],
+        out_specs=specs("v")[0],
         compiler_params=params(16),
         cost_estimate=cost(0, 0),
     )(ahead, state, order_next, order_here)
+
+
+def save(state):
+    return pl.pallas_call(
+        save_kernel,
+        out_shape=jax.ShapeDtypeStruct(state.shape, state.dtype),
+        in_specs=specs("v"),
+        out_specs=specs("a")[0],
+        scratch_shapes=[pltpu.SemaphoreType.DMA],
+        compiler_params=params(4),
+        cost_estimate=cost(0, 2 * state.size * state.dtype.itemsize),
+    )(state)
 
 
 def mixed_swap(value, along, across, core_along):
@@ -487,50 +498,72 @@
         step_counts, far_first, own_coefs, levels, start.shape, fields.shape[0]
     )
     state = second_steps(step_counts, far_second, image_first, own_coefs, far_coefs, levels, start.shape)
-    image, raw = products(ahead, state, order_next, order_here)
+    raw = products(ahead, state, order_next, order_here)
 
     bit = 1
     while 2 * bit < slabs:
         raw = to_bf16(to_f32(raw) + to_f32(swap(raw, "space", bit)))
         bit *= 2
     odd = lax.axis_index("space") % 2 == 1
+    upper = lax.axis_index("seg") % 2 == 1
 
     def my_half(full):
         return jnp.where(odd, full[:, HALF:], full[:, :HALF])
+
+    def my_rows(full):
+        return jnp.where(odd, full[HALF:], full[:HALF])
+
+    def folded(rows):
+        return jnp.concatenate([rows[:, :HALF], rows[:, HALF:]], 0)
+
+    def unfolded(part):
+        return jnp.concatenate([part[:HALF], part[HALF:]], 1)
 
     def both_halves(part):
         rest = swap(part, "space", 1)
         return jnp.where(odd, jnp.concatenate([rest, part], 1), jnp.concatenate([part, rest], 1))
 
+    def both_parts(part):
+        rest = swap(part, "space", 1)
+        low = jnp.where(odd, rest, part)
+        high = jnp.where(odd, part, rest)
+        rows = jnp.concatenate([unfolded(low), unfolded(high)], 0)
+        return jnp.where(upper, jnp.concatenate([low, high], 1), rows)
+
+    def chained(later, earlier):
+        return to_f32(later) + to_f32(earlier) + mul(later, earlier)
+
+    scale = coupling / math.sqrt(K * cells)
+
+    def factor(one, two):
+        return to_bf16((to_f32(one) + to_f32(two)) * scale)
+
     straight = mixed_swap(raw, 1, bit, True)
-    diagonal = mixed_swap(my_half(raw), 1, bit, False)
+    diagonal = mixed_swap(jnp.where(upper, folded(my_rows(raw)), my_half(raw)), 1, bit, False)
     straight_other = swap(straight, "space", 1)
-    diagonal_other = swap(diagonal, "space", 1)
-    scale = coupling / math.sqrt(K * cells)
     across = jnp.where(odd, straight_other, straight)
     along = jnp.where(odd, straight, straight_other)
-    diagonal = jnp.where(odd, jnp.concatenate([diagonal_other, diagonal], 1), jnp.concatenate([diagonal, diagonal_other], 1))
-    mine = to_bf16((to_f32(raw) + to_f32(across)) * scale)
-    theirs = to_bf16((to_f32(along) + to_f32(diagonal)) * scale)
-    def chained(later, earlier):
-        return to_f32(later) + to_f32(earlier) + mul(later, earlier)
-
-    upper = lax.axis_index("seg") % 2 == 1
-    later = jnp.where(upper, mine, theirs)
-    earlier = jnp.where(upper, theirs, mine)
-    half = to_bf16(to_f32(my_half(later)) + to_f32(my_half(earlier)) + mul(later, my_half(earlier)))
-    block = chained(later, earlier)
+    mine = factor(raw, across)
+    columns = factor(my_half(along), diagonal)
+    rows = factor(my_rows(along), unfolded(diagonal))
+    up = to_f32(my_half(mine)) + to_f32(columns) + mul(mine, columns)
+    down = to_f32(my_rows(mine)) + to_f32(rows) + mul(rows, mine)
+    half = jnp.where(upper, to_bf16(up), folded(to_bf16(down)))
+    got_part = swap(half, "seg", 2) if total > 2 else None
+
+    state, diagonal, half = lax.optimization_barrier((state, diagonal, half))
+    image = save(state)
+    theirs = factor(along, both_parts(diagonal))
+    block = chained(jnp.where(upper, mine, theirs), jnp.where(upper, theirs, mine))
     wide = jnp.where(upper, block, to_f32(mine))
     bit = 2
     while bit < total:
-        upper = (lax.axis_index("seg") // bit) % 2 == 1
-        got = both_halves(swap(half, "seg", bit))
-        wide = jnp.where(upper, wide + to_f32(got) + mul(to_bf16(wide), got), wide)
+        higher = (lax.axis_index("seg") // bit) % 2 == 1
         block = to_bf16(block)
-        later = jnp.where(upper, block, got)
-        earlier = jnp.where(upper, got, block)
-        block = chained(later, earlier)
-        half = to_bf16(my_half(block))
+        got = both_parts(got_part) if bit == 2 else both_halves(swap(my_half(block), "seg", bit))
+        wide = jnp.where(higher, wide + to_f32(got) + mul(to_bf16(wide), got), wide)
+        if 2 * bit < total:
+            block = chained(jnp.where(higher, block, got), jnp.where(higher, got, block))
         bit *= 2
     monodromy = wide + jnp.eye(K, dtype=jnp.float32)
     return (image[None], monodromy[None])

time: 41.3 us -> 40.6 us (0.983)
  waiting for transfers between devices: 12.7 us -> 10.6 us
  Pallas kernels: 11 us -> 11.7 us
    ppermute x5, waiting for transfers between devices: 5.94 us -> 3.79 us  [swap(): return lax.ppermute(value, axis, [(i, i ^ bit) for i in range(size)])]
    pallas_call x1 -> x2, Pallas kernels: 0.9 us -> 1.63 us  [the longest x1 0.89 us: save(): pl.pallas_call(save_kernel, out_shape=jax.ShapeDtypeStruct(state.shape, s...]
    dot_general x3 -> x4, matrix products: 1.28 us -> 1.55 us  [mul(): return jnp.dot(left, right, preferred_element_type=jnp.float32)]
  transfers between devices with their start and end apart: 12 -> 12, of which waited for: 7 -> 6; matrix products, arithmetic and copies ran while one was open for 0% -> 1% of each run, Pallas kernels for 25% -> 27%
where the time goes in v6:
time: 40.6 us; the launch traced here: 40.1 us
  starting transfers between devices  14.5 us (36%)
  Pallas kernels  11.7 us (29%)
  waiting for transfers between devices  10.6 us (26%)
  matrix products  1.55 us (4%)
  between operations  1.49 us (4%)
    ppermute x1, starting transfers between devices, per_device(): lax.ppermute(start, 'seg', [((i + 1) % total, i) for i in range(total)])  5.1 us
    ppermute x2, waiting for transfers between devices, mixed_swap(): return lax.ppermute(value, ('seg', 'space'), route)  4.84 us
    ppermute x4, starting transfers between devices, exchange_pairs(): return lax.ppermute(value, axis, route)  4.32 us
    ppermute x5, waiting for transfers between devices, swap(): return lax.ppermute(value, axis, [(i, i ^ bit) for i in range(size)])  3.79 us
    ppermute x5, starting transfers between devices, swap(): return lax.ppermute(value, axis, [(i, i ^ bit) for i in range(size)])  3.2 us
    pallas_call x1, Pallas kernels, near_steps(): pl.pallas_call(near_kernel, out_shape=tuple((level_shape(layers, ys) for...  2.67 us
    pallas_call x1, Pallas kernels, first_steps(): pl.pallas_call(first_kernel, out_shape=(jax.ShapeDtypeStruct((2, *shape[1...  2.5 us
    pallas_call x1, Pallas kernels, spread(): pl.pallas_call(coefs_kernel, out_shape=(factors(4, ys, zs), factors(3, ys...  2.07 us
  transfers between devices with their start and end apart: 12, of which 6 were waited for; matrix products, arithmetic and copies ran while one was open for 1% of the time, Pallas kernels for 27%

profile of v6, /device:TPU:0, one launch (start us, length us, event | category | flops | bytes accessed | tf_op | source)
XLA Modules:
  0.0 40.1 jit_solution(2309117893384954243)
XLA Ops:
  0.6 5.1 %collective-permute-start.4 = (bf16[4,3,128,256]{3,2,1,0:T(8,128)(2,1)}, bf16[4,3,128,256]{3,2,1,0:T(8,128)(2,1)S(1)}, u32[]{:S(2)}, u32[]{:S(2)}) collective-permute-start(bf16[4,3,128,256]{3,2,1,0:T(8,128)(2,1)} %bitcast.13), channel_id=1, source_target_pairs={{4,0},{8,4},{12,8},{0,12},{5,1},{9,5},{13,9},{1,13},{6,2},{10,6},{... | collective-permute-start | bytes 2359304 | tf_op jit(solution)/shard_map/ppermute | solution.py:487
  5.7 1.2 %shard_map.68 = (bf16[7,128,256]{2,1,0:T(8,128)(2,1)S(1)}, bf16[6,128,256]{2,1,0:T(8,128)(2,1)S(1)}, f32[48,128]{1,0:T(8,128)S(1)}) custom-call(bf16[12,128,256]{2,1,0:T(8,128)(2,1)} %bitcast.14, f32[3,4,128]{2,1,0:T(4,128)} %bitcast.17, f32[3,3,4,128]{3,2,1,0:T(4,128)} %bitcast.16), custom_call_target="tpu_custom_call" | custom-call | tf_op jit(solution)/shard_map/pallas_call | solution.py:357
  6.9 0.1 collective-permute-start.2
  7.0 0.7 %collective-permute-start.1 = (bf16[7,128,256]{2,1,0:T(8,128)(2,1)S(1)}, bf16[7,128,256]{2,1,0:T(8,128)(2,1)S(1)}, u32[]{:S(2)}, u32[]{:S(2)}) collective-permute-start(bf16[7,128,256]{2,1,0:T(8,128)(2,1)S(1)} %get-tuple-element.22.own_first), channel_id=1, source_target_pairs={{1,2},{2,1},{5,6},{6,5},{9,10},{10,9},{13,14},{14,13},{17,18},{18,... | collective-permute-start | bytes 1376264 | tf_op jit(solution)/shard_map/ppermute | solution.py:28
  7.7 2.9 %collective-permute-start.3 = (bf16[6,128,256]{2,1,0:T(8,128)(2,1)S(1)}, bf16[6,128,256]{2,1,0:T(8,128)(2,1)S(1)}, u32[]{:S(2)}, u32[]{:S(2)}) collective-permute-start(bf16[6,128,256]{2,1,0:T(8,128)(2,1)S(1)} %get-tuple-element.21.own_second), channel_id=1, source_target_pairs={{0,1},{1,0},{2,3},{3,2},{4,5},{5,4},{6,7},{7,6},{8,9},{9,8},{10,11... | collective-permute-start | bytes 1179656 | tf_op jit(solution)/shard_map/ppermute | solution.py:28
  10.6 0.7 %collective-permute-start = (bf16[6,128,256]{2,1,0:T(8,128)(2,1)S(1)}, bf16[6,128,256]{2,1,0:T(8,128)(2,1)S(1)}, u32[]{:S(2)}, u32[]{:S(2)}) collective-permute-start(bf16[6,128,256]{2,1,0:T(8,128)(2,1)S(1)} %get-tuple-element.21.own_second), channel_id=1, source_target_pairs={{1,2},{2,1},{5,6},{6,5},{9,10},{10,9},{13,14},{14,13},{17,18},{18,... | collective-permute-start | bytes 1179656 | tf_op jit(solution)/shard_map/ppermute | solution.py:28
  11.9 2.1 %shard_map.69 = (f32[12,7,128,128]{3,2,1,0:T(8,128)S(1)}, f32[9,7,128,128]{3,2,1,0:T(8,128)S(1)}, bf16[256,256]{1,0:T(8,128)(2,1)S(1)}, bf16[256,256]{1,0:T(8,128)(2,1)S(1)}) custom-call(f32[48,128]{1,0:T(8,128)S(1)} %get-tuple-element.23.own_fields, bf16[7,128,256]{2,1,0:T(8,128)(2,1)S(1)} %collective-permute-done.2.near_first.first, s32[4,16]{1,0:T(4,128)} %order_home.1), custom_call_target="tpu_custom_call" | custom-call | tf_op jit(solution)/shard_map/pallas_call | solution.py:387
  14.0 0.0 collective-permute-done.3.second
  14.0 2.7 %shard_map.70 = (f32[8,3,2,144,128]{4,3,2,1,0:T(8,128)S(1)}, f32[6,3,2,144,128]{4,3,2,1,0:T(8,128)S(1)}, f32[4,3,2,144,128]{4,3,2,1,0:T(8,128)S(1)}, f32[2,3,2,144,128]{4,3,2,1,0:T(8,128)S(1)}) custom-call(s32[1]{0:T(128)S(6)} %copy.7.counts, bf16[7,128,256]{2,1,0:T(8,128)(2,1)S(1)} %get-tuple-element.22.own_first, ...), custom_call_target="tpu_custom_call" | custom-call | tf_op jit(solution)/shard_map/pallas_call | solution.py:405
  16.7 0.0 collective-permute-done.1.first
  16.7 2.5 %shard_map.71 = (bf16[2,3,128,256]{3,2,1,0:T(8,128)(2,1)S(1)}, f32[9,7,128,128]{3,2,1,0:T(8,128)S(1)}, f32[2,3,2,144,128]{4,3,2,1,0:T(8,128)S(1)}, f32[2,3,2,144...) custom-call(s32[1]{0:T(128)S(6)} %copy.7.counts, ...), custom_call_target="tpu_custom_call" | custom-call | tf_op jit(solution)/shard_map/pallas_call | solution.py:417
  19.2 0.0 collective-permute-done.second
  19.2 1.7 %shard_map.72.state = bf16[4,3,128,256]{3,2,1,0:T(8,128)(2,1)S(1)} custom-call(s32[1]{0:T(128)S(6)} %copy.7.counts, bf16[6,128,256]{2,1,0:T(8,128)(2,1)S(1)} %collective-permute-done.second, bf16[2,3,128,256]{3,2,1,0:T(8,128)(2,1)S(1)} %get-tuple-element.30.done, f32[12,7,128,128]{3,2,1,0:T(8,128)S(1)} %get-tuple-element.24.own_coefs, ...), custom_call_target="tpu_custom_call" | custom-call | tf_op jit(solution)/shard_map/pallas_call | solution.py:434
  20.9 2.0 %collective-permute-done.4.ahead = bf16[4,3,128,256]{3,2,1,0:T(8,128)(2,1)S(1)} collective-permute-done((bf16[4,3,128,256]{3,2,1,0:T(8,128)(2,1)}, bf16[4,3,128,256]{3,2,1,0:T(8,128)(2,1)S(1)}, u32[]{:S(2)}, u32[]{:S(2)}) %collective-permute-start.4) | collective-permute-done | bytes 786464 | tf_op jit(solution)/shard_map/ppermute | solution.py:487
  22.8 0.7 %shard_map.73 = bf16[256,256]{1,0:T(8,128)(2,1)S(1)} custom-call(bf16[4,3,128,256]{3,2,1,0:T(8,128)(2,1)S(1)} %collective-permute-done.4.ahead, bf16[4,3,128,256]{3,2,1,0:T(8,128)(2,1)S(1)} %shard_map.72.state, bf16[256,256]{1,0:T(8,128)(2,1)S(1)} %get-tuple-element.36.order_next, bf16[256,256]{1,0:T(8,128)(2,1)S(1)} %get-tuple-element.37.order_here), custom_call_target="tpu_custom_call" | custom-call | tf_op jit(solution)/shard_map/pallas_call | solution.py:446
  23.6 0.5 %collective-permute-start.5 = (bf16[256,256]{1,0:T(8,128)(2,1)S(1)}, bf16[256,256]{1,0:T(8,128)(2,1)S(1)}, u32[]{:S(2)}, u32[]{:S(2)}) collective-permute-start(bf16[256,256]{1,0:T(8,128)(2,1)S(1)} %shard_map.73), channel_id=1, source_target_pairs={{0,1},{1,0},{2,3},{3,2},{4,5},{5,4},{6,7},{7,6},{8,9},{9,8},{10,11... | collective-permute-start | bytes 393224 | tf_op jit(solution)/shard_map/ppermute | solution.py:20
  24.1 1.0 %collective-permute-done.5 = bf16[256,256]{1,0:T(8,128)(2,1)S(1)} collective-permute-done((bf16[256,256]{1,0:T(8,128)(2,1)S(1)}, bf16[256,256]{1,0:T(8,128)(2,1)S(1)}, u32[]{:S(2)}, u32[]{:S(2)}) %collective-permute-start.5) | collective-permute-done | bytes 131104 | tf_op jit(solution)/shard_map/ppermute | solution.py:20
  25.1 1.5 %collective-permute-start.7 = (bf16[256,256]{1,0:T(8,128)(2,1)S(1)}, bf16[256,256]{1,0:T(8,128)(2,1)S(1)}, u32[]{:S(2)}, u32[]{:S(2)}) collective-permute-start(bf16[256,256]{1,0:T(8,128)(2,1)S(1)} %add_convert_fusion), channel_id=1, source_target_pairs={{0,2},{1,5},{2,0},{3,7},{4,6},{5,1},{6,4},{7,3},{8,10},{9,13},{10,... | collective-permute-start | bytes 393224 | tf_op jit(solution)/shard_map/ppermute | solution.py:478
  26.7 0.4 collective-permute-start.6
  27.1 3.5 %collective-permute-done.7 = bf16[256,256]{1,0:T(8,128)(2,1)S(1)} collective-permute-done((bf16[256,256]{1,0:T(8,128)(2,1)S(1)}, bf16[256,256]{1,0:T(8,128)(2,1)S(1)}, u32[]{:S(2)}, u32[]{:S(2)}) %collective-permute-start.7) | collective-permute-done | bytes 131104 | tf_op jit(solution)/shard_map/ppermute | solution.py:478
  30.5 0.0 collective-permute-start.8
  30.5 1.4 %collective-permute-done.6 = bf16[256,128]{1,0:T(8,128)(2,1)S(1)} collective-permute-done((bf16[256,128]{1,0:T(8,128)(2,1)S(1)}, bf16[256,128]{1,0:T(8,128)(2,1)S(1)}, u32[]{:S(2)}, u32[]{:S(2)}) %collective-permute-start.6) | collective-permute-done | bytes 65568 | tf_op jit(solution)/shard_map/ppermute | solution.py:478
  31.9 0.1 multiply_convert_fusion.1
  32.0 0.2 fusion.5
  32.2 0.2 fusion.6
  32.4 0.2 collective-permute-start.9
  32.6 2.6 %collective-permute-start.10 = (bf16[256,128]{1,0:T(8,128)(2,1)S(1)}, bf16[256,128]{1,0:T(8,128)(2,1)S(1)}, u32[]{:S(2)}, u32[]{:S(2)}) collective-permute-start(bf16[256,128]{1,0:T(8,128)(2,1)S(1)} %fusion.6), channel_id=1, source_target_pairs={{0,8},{4,12},{8,0},{12,4},{1,9},{5,13},{9,1},{13,5},{2,10},{6,14},... | collective-permute-start | bytes 196616 | tf_op jit(solution)/shard_map/ppermute | solution.py:20
  35.1 0.9 %shard_map.74 = bf16[4,3,128,256]{3,2,1,0:T(8,128)(2,1)} custom-call(bf16[4,3,128,256]{3,2,1,0:T(8,128)(2,1)S(1)} %shard_map.72.state), custom_call_target="tpu_custom_call" | custom-call | bytes 1572864 | tf_op jit(solution)/shard_map/pallas_call | solution.py:457
  36.1 1.8 %collective-permute-done.10 = bf16[256,128]{1,0:T(8,128)(2,1)S(1)} collective-permute-done((bf16[256,128]{1,0:T(8,128)(2,1)S(1)}, bf16[256,128]{1,0:T(8,128)(2,1)S(1)}, u32[]{:S(2)}, u32[]{:S(2)}) %collective-permute-start.10) | collective-permute-done | bytes 65568 | tf_op jit(solution)/shard_map/ppermute | solution.py:20
  37.9 0.3 fusion.3
  38.2 1.0 %collective-permute-done.11 = bf16[256,128]{1,0:T(8,128)(2,1)S(1)} collective-permute-done((bf16[256,128]{1,0:T(8,128)(2,1)S(1)}, bf16[256,128]{1,0:T(8,128)(2,1)S(1)}, u32[]{:S(2)}, u32[]{:S(2)}) %collective-permute-start.11) | collective-permute-done | bytes 65568 | tf_op jit(solution)/shard_map/ppermute | solution.py:20
  39.2 0.9 %fusion.2 = f32[1,256,256]{2,1,0:T(8,128)} fusion(f32[256,256]{1,0:T(8,128)S(1)} %fusion.3, bf16[256,128]{1,0:T(8,128)(2,1)S(1)} %get-tuple-element.41, bf16[256,128]{1,0:T(8,128)(2,1)S(1)} %get-tuple-element.40, bf16[128,128]{1,0:T(8,128)(2,1)S(1)} %get-tuple-element.60, bf16[128,128]{1,0:T(8,128)(2,1)S(1)} %get-tuple-element.61, ...), kind=kOutput, calls=%fused_computation.3 | convolution fusion | flops 35782656 | bytes 786434 | tf_op jit(solution)/shard_map/dot_general | solution.py:311
  (15 shorter events, 0.2 us)
Async XLA Ops:
  0.6 22.2 %collective-permute-start.4 = (bf16[4,3,128,256]{3,2,1,0:T(8,128)(2,1)}, bf16[4,3,128,256]{3,2,1,0:T(8,128)(2,1)S(1)}, u32[]{:S(2)}, u32[]{:S(2)}) collective-permute-start(bf16[4,3,128,256]{3,2,1,0:T(8,128)(2,1)} %bitcast.13), channel_id=1, source_target_pairs={{4,0},{8,4},{12,8},{0,12},{5,1},{9,5},{13,9},{1,13},{6,2},{10,6},{... | collective-permute-start | bytes 2359304 | tf_op jit(solution)/shard_map/ppermute | solution.py:487
  6.9 5.0 %collective-permute-start.2 = (bf16[7,128,256]{2,1,0:T(8,128)(2,1)S(1)}, bf16[7,128,256]{2,1,0:T(8,128)(2,1)S(1)}, u32[]{:S(2)}, u32[]{:S(2)}) collective-permute-start(bf16[7,128,256]{2,1,0:T(8,128)(2,1)S(1)} %get-tuple-element.22.own_first), channel_id=1, source_target_pairs={{0,1},{1,0},{2,3},{3,2},{4,5},{5,4},{6,7},{7,6},{8,9},{9,8},{10,11... | collective-permute-start | bytes 1376264 | tf_op jit(solution)/shard_map/ppermute | solution.py:28
  7.0 9.7 %collective-permute-start.1 = (bf16[7,128,256]{2,1,0:T(8,128)(2,1)S(1)}, bf16[7,128,256]{2,1,0:T(8,128)(2,1)S(1)}, u32[]{:S(2)}, u32[]{:S(2)}) collective-permute-start(bf16[7,128,256]{2,1,0:T(8,128)(2,1)S(1)} %get-tuple-element.22.own_first), channel_id=1, source_target_pairs={{1,2},{2,1},{5,6},{6,5},{9,10},{10,9},{13,14},{14,13},{17,18},{18,... | collective-permute-start | bytes 1376264 | tf_op jit(solution)/shard_map/ppermute | solution.py:28
  7.7 6.3 %collective-permute-start.3 = (bf16[6,128,256]{2,1,0:T(8,128)(2,1)S(1)}, bf16[6,128,256]{2,1,0:T(8,128)(2,1)S(1)}, u32[]{:S(2)}, u32[]{:S(2)}) collective-permute-start(bf16[6,128,256]{2,1,0:T(8,128)(2,1)S(1)} %get-tuple-element.21.own_second), channel_id=1, source_target_pairs={{0,1},{1,0},{2,3},{3,2},{4,5},{5,4},{6,7},{7,6},{8,9},{9,8},{10,11... | collective-permute-start | bytes 1179656 | tf_op jit(solution)/shard_map/ppermute | solution.py:28
  10.6 8.6 %collective-permute-start = (bf16[6,128,256]{2,1,0:T(8,128)(2,1)S(1)}, bf16[6,128,256]{2,1,0:T(8,128)(2,1)S(1)}, u32[]{:S(2)}, u32[]{:S(2)}) collective-permute-start(bf16[6,128,256]{2,1,0:T(8,128)(2,1)S(1)} %get-tuple-element.21.own_second), channel_id=1, source_target_pairs={{1,2},{2,1},{5,6},{6,5},{9,10},{10,9},{13,14},{14,13},{17,18},{18,... | collective-permute-start | bytes 1179656 | tf_op jit(solution)/shard_map/ppermute | solution.py:28
  23.6 1.4 %collective-permute-start.5 = (bf16[256,256]{1,0:T(8,128)(2,1)S(1)}, bf16[256,256]{1,0:T(8,128)(2,1)S(1)}, u32[]{:S(2)}, u32[]{:S(2)}) collective-permute-start(bf16[256,256]{1,0:T(8,128)(2,1)S(1)} %shard_map.73), channel_id=1, source_target_pairs={{0,1},{1,0},{2,3},{3,2},{4,5},{5,4},{6,7},{7,6},{8,9},{9,8},{10,11... | collective-permute-start | bytes 393224 | tf_op jit(solution)/shard_map/ppermute | solution.py:20
  25.1 5.4 %collective-permute-start.7 = (bf16[256,256]{1,0:T(8,128)(2,1)S(1)}, bf16[256,256]{1,0:T(8,128)(2,1)S(1)}, u32[]{:S(2)}, u32[]{:S(2)}) collective-permute-start(bf16[256,256]{1,0:T(8,128)(2,1)S(1)} %add_convert_fusion), channel_id=1, source_target_pairs={{0,2},{1,5},{2,0},{3,7},{4,6},{5,1},{6,4},{7,3},{8,10},{9,13},{10,... | collective-permute-start | bytes 393224 | tf_op jit(solution)/shard_map/ppermute | solution.py:478
  26.7 5.2 %collective-permute-start.6 = (bf16[256,128]{1,0:T(8,128)(2,1)S(1)}, bf16[256,128]{1,0:T(8,128)(2,1)S(1)}, u32[]{:S(2)}, u32[]{:S(2)}) collective-permute-start(bf16[256,128]{1,0:T(8,128)(2,1)S(1)} %fusion.33), channel_id=1, source_target_pairs={{0,6},{1,7},{2,4},{3,5},{4,2},{5,3},{6,0},{7,1},{8,14},{9,15},{10,... | collective-permute-start | bytes 196616 | tf_op jit(solution)/shard_map/ppermute | solution.py:478
  30.5 1.4 %collective-permute-start.8 = (bf16[256,256]{1,0:T(8,128)(2,1)S(1)}, bf16[256,256]{1,0:T(8,128)(2,1)S(1)}, u32[]{:S(2)}, u32[]{:S(2)}) collective-permute-start(bf16[256,256]{1,0:T(8,128)(2,1)S(1)} %collective-permute-done.7), channel_id=1, source_target_pairs={{0,1},{1,0},{2,3},{3,2},{4,5},{5,4},{6,7},{7,6},{8,9},{9,8},{10,11... | collective-permute-start | bytes 393224 | tf_op jit(solution)/shard_map/ppermute | solution.py:20
  32.4 3.6 %collective-permute-start.9 = (bf16[256,128]{1,0:T(8,128)(2,1)S(1)}, bf16[256,128]{1,0:T(8,128)(2,1)S(1)}, u32[]{:S(2)}, u32[]{:S(2)}) collective-permute-start(bf16[256,128]{1,0:T(8,128)(2,1)S(1)} %collective-permute-done.6), channel_id=1, source_target_pairs={{0,1},{1,0},{2,3},{3,2},{4,5},{5,4},{6,7},{7,6},{8,9},{9,8},{10,11... | collective-permute-start | bytes 196616 | tf_op jit(solution)/shard_map/ppermute | solution.py:20
  32.6 5.3 %collective-permute-start.10 = (bf16[256,128]{1,0:T(8,128)(2,1)S(1)}, bf16[256,128]{1,0:T(8,128)(2,1)S(1)}, u32[]{:S(2)}, u32[]{:S(2)}) collective-permute-start(bf16[256,128]{1,0:T(8,128)(2,1)S(1)} %fusion.6), channel_id=1, source_target_pairs={{0,8},{4,12},{8,0},{12,4},{1,9},{5,13},{9,1},{13,5},{2,10},{6,14},... | collective-permute-start | bytes 196616 | tf_op jit(solution)/shard_map/ppermute | solution.py:20
  37.9 1.3 %collective-permute-start.11 = (bf16[256,128]{1,0:T(8,128)(2,1)S(1)}, bf16[256,128]{1,0:T(8,128)(2,1)S(1)}, u32[]{:S(2)}, u32[]{:S(2)}) collective-permute-start(bf16[256,128]{1,0:T(8,128)(2,1)S(1)} %collective-permute-done.10), channel_id=1, source_target_pairs={{0,1},{1,0},{2,3},{3,2},{4,5},{5,4},{6,7},{7,6},{8,9},{9,8},{10,11... | collective-permute-start | bytes 196616 | tf_op jit(solution)/shard_map/ppermute | solution.py:20

commit v7 on v6

--- a/solution.py
+++ b/solution.py
@@ -72,10 +72,12 @@
 
 
 def unpack_layer(source, index, ys, dest, slot):
-    zs = source.shape[1]
+    zs = dest.shape[3] - 2 * TOP
+    per = zs // BLOCK
     for y in range(ys):
         for h in range(2):
-            value = source[index * ys + y, :, h * HALF : (h + 1) * HALF].astype(jnp.float32)
+            value = source[pl.ds((index * ys + y) * per, per), :, h * HALF : (h + 1) * HALF]
+            value = value.reshape(zs, HALF).astype(jnp.float32)
             dest[slot, y, h, TOP : TOP + zs, :] = value
             dest[slot, y, h, TOP - 1 : TOP, :] = value[zs - 1 : zs]
             dest[slot, y, h, TOP + zs : TOP + zs + 1, :] = value[0:1]
@@ -147,23 +149,22 @@
     rest = value - to_f32(high)
     middle = to_bf16(rest)
     low = to_bf16(rest - to_f32(middle))
-    rows = value.shape[0]
-    first[half, :rows, :HALF] = high
-    first[half, :rows, HALF:] = middle
-    first[half, rows : 2 * rows, :HALF] = low
-    first[half, rows : 2 * rows, HALF:] = jnp.zeros_like(low)
-    if first.shape[1] > 2 * rows:
-        first[half, 2 * rows :, :] = jnp.zeros((first.shape[1] - 2 * rows, K), jnp.bfloat16)
+    per = value.shape[0] // BLOCK
+    shape = (per, BLOCK, HALF)
+    first[half : half + per, :, :HALF] = high.reshape(shape)
+    first[half : half + per, :, HALF:] = middle.reshape(shape)
+    first[half + per : half + 2 * per, :, :HALF] = low.reshape(shape)
+    first[half + per : half + 2 * per, :, HALF:] = jnp.zeros(shape, jnp.bfloat16)
     for copy in copies:
         copy.wait()
 
 
 def unpack_fields(packed, fields):
-    rows = fields.shape[0]
-    at = packed.shape[0] - 1
-    high = to_f32(packed[at, :rows, :HALF])
-    middle = to_f32(packed[at, :rows, HALF:])
-    low = to_f32(packed[at, rows : 2 * rows, :HALF])
+    per = fields.shape[0] // BLOCK
+    at = packed.shape[0] - 2 * per
+    high = to_f32(packed[at : at + per, :, :HALF].reshape(fields.shape))
+    middle = to_f32(packed[at : at + per, :, HALF:].reshape(fields.shape))
+    low = to_f32(packed[at + per : at + 2 * per, :, :HALF].reshape(fields.shape))
     fields[...] = high + (middle + low)
 
 
@@ -352,13 +353,13 @@
 
 
 def pack(start, diffusivity, velocity):
-    planes, zs = start.shape[0], start.shape[1]
+    planes, zs = start.shape[0], diffusivity.shape[2]
     rows = diffusivity.shape[0] * diffusivity.shape[1] * FIELDS
     return pl.pallas_call(
         pack_kernel,
         out_shape=(
-            jax.ShapeDtypeStruct((planes // 2 + 1, zs, K), jnp.bfloat16),
-            jax.ShapeDtypeStruct((planes // 2, zs, K), jnp.bfloat16),
+            jax.ShapeDtypeStruct((planes // 2 + 2 * rows // BLOCK, BLOCK, K), jnp.bfloat16),
+            jax.ShapeDtypeStruct((planes // 2, BLOCK, K), jnp.bfloat16),
             jax.ShapeDtypeStruct((rows, zs), jnp.float32),
         ),
         in_specs=specs("hhh"),
@@ -486,7 +487,7 @@
 
     ahead = lax.ppermute(start, "seg", [((i + 1) % total, i) for i in range(total)])
     ys, zs = start.shape[1], start.shape[2]
-    planes = start.reshape(-1, zs, K)
+    planes = start.reshape(-1, BLOCK, K)
     first, second, fields = pack(planes, diffusivity[0].transpose(1, 0, 2), velocity[0].transpose(0, 2, 1, 3))
     near_first = exchange_pairs(first, "space", 0)
     near_second = exchange_pairs(second, "space", 0)

time: 40.6 us -> 40.6 us (level)
  no operation moved by 1% of the time
where the time goes in v7:
time: 40.6 us; the launch traced here: 40.1 us
  starting transfers between devices  14.5 us (36%)
  Pallas kernels  11.7 us (29%)
  waiting for transfers between devices  10.6 us (26%)
  matrix products  1.55 us (4%)
  between operations  1.49 us (4%)
    ppermute x1, starting transfers between devices, per_device(): lax.ppermute(start, 'seg', [((i + 1) % total, i) for i in range(total)])  5.1 us
    ppermute x2, waiting for transfers between devices, mixed_swap(): return lax.ppermute(value, ('seg', 'space'), route)  4.84 us
    ppermute x4, starting transfers between devices, exchange_pairs(): return lax.ppermute(value, axis, route)  4.32 us
    ppermute x5, waiting for transfers between devices, swap(): return lax.ppermute(value, axis, [(i, i ^ bit) for i in range(size)])  3.79 us
    ppermute x5, starting transfers between devices, swap(): return lax.ppermute(value, axis, [(i, i ^ bit) for i in range(size)])  3.2 us
    pallas_call x1, Pallas kernels, near_steps(): pl.pallas_call(near_kernel, out_shape=tuple((level_shape(layers, ys) for...  2.67 us
    pallas_call x1, Pallas kernels, first_steps(): pl.pallas_call(first_kernel, out_shape=(jax.ShapeDtypeStruct((2, *shape[1...  2.5 us
    pallas_call x1, Pallas kernels, spread(): pl.pallas_call(coefs_kernel, out_shape=(factors(4, ys, zs), factors(3, ys...  2.06 us
  transfers between devices with their start and end apart: 12, of which 6 were waited for; matrix products, arithmetic and copies ran while one was open for 1% of the time, Pallas kernels for 27%

profile of v7, /device:TPU:0, one launch (start us, length us, event | category | flops | bytes accessed | tf_op | source)
XLA Modules:
  0.0 40.1 jit_solution(365016222205790009)
XLA Ops:
  0.6 5.1 %collective-permute-start.4 = (bf16[4,3,128,256]{3,2,1,0:T(8,128)(2,1)}, bf16[4,3,128,256]{3,2,1,0:T(8,128)(2,1)S(1)}, u32[]{:S(2)}, u32[]{:S(2)}) collective-permute-start(bf16[4,3,128,256]{3,2,1,0:T(8,128)(2,1)} %bitcast.13), channel_id=1, source_target_pairs={{4,0},{8,4},{12,8},{0,12},{5,1},{9,5},{13,9},{1,13},{6,2},{10,6},{... | collective-permute-start | bytes 2359304 | tf_op jit(solution)/shard_map/ppermute | solution.py:488
  5.7 1.2 %shard_map.68 = (bf16[54,16,256]{2,1,0:T(8,128)(2,1)S(1)}, bf16[48,16,256]{2,1,0:T(8,128)(2,1)S(1)}, f32[48,128]{1,0:T(8,128)S(1)}) custom-call(bf16[96,16,256]{2,1,0:T(8,128)(2,1)} %bitcast.14, f32[3,4,128]{2,1,0:T(4,128)} %bitcast.17, f32[3,3,4,128]{3,2,1,0:T(4,128)} %bitcast.16), custom_call_target="tpu_custom_call" | custom-call | tf_op jit(solution)/shard_map/pallas_call | solution.py:358
  6.9 0.1 collective-permute-start.2
  7.0 0.7 %collective-permute-start.1 = (bf16[54,16,256]{2,1,0:T(8,128)(2,1)S(1)}, bf16[54,16,256]{2,1,0:T(8,128)(2,1)S(1)}, u32[]{:S(2)}, u32[]{:S(2)}) collective-permute-start(bf16[54,16,256]{2,1,0:T(8,128)(2,1)S(1)} %get-tuple-element.22.own_first), channel_id=1, source_target_pairs={{1,2},{2,1},{5,6},{6,5},{9,10},{10,9},{13,14},{14,13},{17,18},{18,... | collective-permute-start | bytes 1327112 | tf_op jit(solution)/shard_map/ppermute | solution.py:28
  7.7 2.9 %collective-permute-start.3 = (bf16[48,16,256]{2,1,0:T(8,128)(2,1)S(1)}, bf16[48,16,256]{2,1,0:T(8,128)(2,1)S(1)}, u32[]{:S(2)}, u32[]{:S(2)}) collective-permute-start(bf16[48,16,256]{2,1,0:T(8,128)(2,1)S(1)} %get-tuple-element.21.own_second), channel_id=1, source_target_pairs={{0,1},{1,0},{2,3},{3,2},{4,5},{5,4},{6,7},{7,6},{8,9},{9,8},{10,11... | collective-permute-start | bytes 1179656 | tf_op jit(solution)/shard_map/ppermute | solution.py:28
  10.6 0.7 %collective-permute-start = (bf16[48,16,256]{2,1,0:T(8,128)(2,1)S(1)}, bf16[48,16,256]{2,1,0:T(8,128)(2,1)S(1)}, u32[]{:S(2)}, u32[]{:S(2)}) collective-permute-start(bf16[48,16,256]{2,1,0:T(8,128)(2,1)S(1)} %get-tuple-element.21.own_second), channel_id=1, source_target_pairs={{1,2},{2,1},{5,6},{6,5},{9,10},{10,9},{13,14},{14,13},{17,18},{18,... | collective-permute-start | bytes 1179656 | tf_op jit(solution)/shard_map/ppermute | solution.py:28
  11.9 0.0 collective-permute-done.2.near_first.first
  11.9 2.1 %shard_map.69 = (f32[12,7,128,128]{3,2,1,0:T(8,128)S(1)}, f32[9,7,128,128]{3,2,1,0:T(8,128)S(1)}, bf16[256,256]{1,0:T(8,128)(2,1)S(1)}, bf16[256,256]{1,0:T(8,128)(2,1)S(1)}) custom-call(f32[48,128]{1,0:T(8,128)S(1)} %get-tuple-element.23.own_fields, bf16[54,16,256]{2,1,0:T(8,128)(2,1)S(1)} %collective-permute-done.2.near_first.first, s32[4,16]{1,0:T(4,128)} %order_home.1), custom_call_target="tpu_custom_call" | custom-call | tf_op jit(solution)/shard_map/pallas_call | solution.py:388
  14.0 2.7 %shard_map.70 = (f32[8,3,2,144,128]{4,3,2,1,0:T(8,128)S(1)}, f32[6,3,2,144,128]{4,3,2,1,0:T(8,128)S(1)}, f32[4,3,2,144,128]{4,3,2,1,0:T(8,128)S(1)}, f32[2,3,2,144,128]{4,3,2,1,0:T(8,128)S(1)}) custom-call(s32[1]{0:T(128)S(6)} %copy.7.counts, bf16[54,16,256]{2,1,0:T(8,128)(2,1)S(1)} %get-tuple-element.22.own_first, ...), custom_call_target="tpu_custom_call" | custom-call | tf_op jit(solution)/shard_map/pallas_call | solution.py:406
  16.7 0.0 collective-permute-done.1.first
  16.7 2.5 %shard_map.71 = (bf16[2,3,128,256]{3,2,1,0:T(8,128)(2,1)S(1)}, f32[9,7,128,128]{3,2,1,0:T(8,128)S(1)}, f32[2,3,2,144,128]{4,3,2,1,0:T(8,128)S(1)}, f32[2,3,2,144...) custom-call(s32[1]{0:T(128)S(6)} %copy.7.counts, ...), custom_call_target="tpu_custom_call" | custom-call | tf_op jit(solution)/shard_map/pallas_call | solution.py:418
  19.2 1.7 %shard_map.72.state = bf16[4,3,128,256]{3,2,1,0:T(8,128)(2,1)S(1)} custom-call(s32[1]{0:T(128)S(6)} %copy.7.counts, bf16[48,16,256]{2,1,0:T(8,128)(2,1)S(1)} %collective-permute-done.second, bf16[2,3,128,256]{3,2,1,0:T(8,128)(2,1)S(1)} %get-tuple-element.30.done, f32[12,7,128,128]{3,2,1,0:T(8,128)S(1)} %get-tuple-element.24.own_coefs, ...), custom_call_target="tpu_custom_call" | custom-call | tf_op jit(solution)/shard_map/pallas_call | solution.py:435
  20.9 2.0 %collective-permute-done.4.ahead = bf16[4,3,128,256]{3,2,1,0:T(8,128)(2,1)S(1)} collective-permute-done((bf16[4,3,128,256]{3,2,1,0:T(8,128)(2,1)}, bf16[4,3,128,256]{3,2,1,0:T(8,128)(2,1)S(1)}, u32[]{:S(2)}, u32[]{:S(2)}) %collective-permute-start.4) | collective-permute-done | bytes 786464 | tf_op jit(solution)/shard_map/ppermute | solution.py:488
  22.8 0.7 %shard_map.73 = bf16[256,256]{1,0:T(8,128)(2,1)S(1)} custom-call(bf16[4,3,128,256]{3,2,1,0:T(8,128)(2,1)S(1)} %collective-permute-done.4.ahead, bf16[4,3,128,256]{3,2,1,0:T(8,128)(2,1)S(1)} %shard_map.72.state, bf16[256,256]{1,0:T(8,128)(2,1)S(1)} %get-tuple-element.36.order_next, bf16[256,256]{1,0:T(8,128)(2,1)S(1)} %get-tuple-element.37.order_here), custom_call_target="tpu_custom_call" | custom-call | tf_op jit(solution)/shard_map/pallas_call | solution.py:447
  23.6 0.5 %collective-permute-start.5 = (bf16[256,256]{1,0:T(8,128)(2,1)S(1)}, bf16[256,256]{1,0:T(8,128)(2,1)S(1)}, u32[]{:S(2)}, u32[]{:S(2)}) collective-permute-start(bf16[256,256]{1,0:T(8,128)(2,1)S(1)} %shard_map.73), channel_id=1, source_target_pairs={{0,1},{1,0},{2,3},{3,2},{4,5},{5,4},{6,7},{7,6},{8,9},{9,8},{10,11... | collective-permute-start | bytes 393224 | tf_op jit(solution)/shard_map/ppermute | solution.py:20
  24.1 1.0 %collective-permute-done.5 = bf16[256,256]{1,0:T(8,128)(2,1)S(1)} collective-permute-done((bf16[256,256]{1,0:T(8,128)(2,1)S(1)}, bf16[256,256]{1,0:T(8,128)(2,1)S(1)}, u32[]{:S(2)}, u32[]{:S(2)}) %collective-permute-start.5) | collective-permute-done | bytes 131104 | tf_op jit(solution)/shard_map/ppermute | solution.py:20
  25.1 1.5 %collective-permute-start.7 = (bf16[256,256]{1,0:T(8,128)(2,1)S(1)}, bf16[256,256]{1,0:T(8,128)(2,1)S(1)}, u32[]{:S(2)}, u32[]{:S(2)}) collective-permute-start(bf16[256,256]{1,0:T(8,128)(2,1)S(1)} %add_convert_fusion), channel_id=1, source_target_pairs={{0,2},{1,5},{2,0},{3,7},{4,6},{5,1},{6,4},{7,3},{8,10},{9,13},{10,... | collective-permute-start | bytes 393224 | tf_op jit(solution)/shard_map/ppermute | solution.py:479
  26.7 0.4 collective-permute-start.6
  27.1 3.5 %collective-permute-done.7 = bf16[256,256]{1,0:T(8,128)(2,1)S(1)} collective-permute-done((bf16[256,256]{1,0:T(8,128)(2,1)S(1)}, bf16[256,256]{1,0:T(8,128)(2,1)S(1)}, u32[]{:S(2)}, u32[]{:S(2)}) %collective-permute-start.7) | collective-permute-done | bytes 131104 | tf_op jit(solution)/shard_map/ppermute | solution.py:479
  30.5 0.0 collective-permute-start.8
  30.5 1.4 %collective-permute-done.6 = bf16[256,128]{1,0:T(8,128)(2,1)S(1)} collective-permute-done((bf16[256,128]{1,0:T(8,128)(2,1)S(1)}, bf16[256,128]{1,0:T(8,128)(2,1)S(1)}, u32[]{:S(2)}, u32[]{:S(2)}) %collective-permute-start.6) | collective-permute-done | bytes 65568 | tf_op jit(solution)/shard_map/ppermute | solution.py:479
  31.9 0.1 multiply_convert_fusion.1
  32.0 0.2 fusion.5
  32.2 0.2 fusion.6
  32.4 0.2 collective-permute-start.9
  32.6 2.6 %collective-permute-start.10 = (bf16[256,128]{1,0:T(8,128)(2,1)S(1)}, bf16[256,128]{1,0:T(8,128)(2,1)S(1)}, u32[]{:S(2)}, u32[]{:S(2)}) collective-permute-start(bf16[256,128]{1,0:T(8,128)(2,1)S(1)} %fusion.6), channel_id=1, source_target_pairs={{0,8},{4,12},{8,0},{12,4},{1,9},{5,13},{9,1},{13,5},{2,10},{6,14},... | collective-permute-start | bytes 196616 | tf_op jit(solution)/shard_map/ppermute | solution.py:20
  35.1 0.9 %shard_map.74 = bf16[4,3,128,256]{3,2,1,0:T(8,128)(2,1)} custom-call(bf16[4,3,128,256]{3,2,1,0:T(8,128)(2,1)S(1)} %shard_map.72.state), custom_call_target="tpu_custom_call" | custom-call | bytes 1572864 | tf_op jit(solution)/shard_map/pallas_call | solution.py:458
  36.1 1.8 %collective-permute-done.10 = bf16[256,128]{1,0:T(8,128)(2,1)S(1)} collective-permute-done((bf16[256,128]{1,0:T(8,128)(2,1)S(1)}, bf16[256,128]{1,0:T(8,128)(2,1)S(1)}, u32[]{:S(2)}, u32[]{:S(2)}) %collective-permute-start.10) | collective-permute-done | bytes 65568 | tf_op jit(solution)/shard_map/ppermute | solution.py:20
  37.9 0.0 collective-permute-start.11
  37.9 0.3 fusion.3
  38.2 1.0 %collective-permute-done.11 = bf16[256,128]{1,0:T(8,128)(2,1)S(1)} collective-permute-done((bf16[256,128]{1,0:T(8,128)(2,1)S(1)}, bf16[256,128]{1,0:T(8,128)(2,1)S(1)}, u32[]{:S(2)}, u32[]{:S(2)}) %collective-permute-start.11) | collective-permute-done | bytes 65568 | tf_op jit(solution)/shard_map/ppermute | solution.py:20
  39.2 0.9 %fusion.2 = f32[1,256,256]{2,1,0:T(8,128)} fusion(f32[256,256]{1,0:T(8,128)S(1)} %fusion.3, bf16[256,128]{1,0:T(8,128)(2,1)S(1)} %get-tuple-element.41, bf16[256,128]{1,0:T(8,128)(2,1)S(1)} %get-tuple-element.40, bf16[128,128]{1,0:T(8,128)(2,1)S(1)} %get-tuple-element.60, bf16[128,128]{1,0:T(8,128)(2,1)S(1)} %get-tuple-element.61, ...), kind=kOutput, calls=%fused_computation.3 | convolution fusion | flops 35782656 | bytes 786434 | tf_op jit(solution)/shard_map/dot_general | solution.py:312
  (15 shorter events, 0.2 us)
Async XLA Ops:
  0.6 22.2 %collective-permute-start.4 = (bf16[4,3,128,256]{3,2,1,0:T(8,128)(2,1)}, bf16[4,3,128,256]{3,2,1,0:T(8,128)(2,1)S(1)}, u32[]{:S(2)}, u32[]{:S(2)}) collective-permute-start(bf16[4,3,128,256]{3,2,1,0:T(8,128)(2,1)} %bitcast.13), channel_id=1, source_target_pairs={{4,0},{8,4},{12,8},{0,12},{5,1},{9,5},{13,9},{1,13},{6,2},{10,6},{... | collective-permute-start | bytes 2359304 | tf_op jit(solution)/shard_map/ppermute | solution.py:488
  6.9 5.0 %collective-permute-start.2 = (bf16[54,16,256]{2,1,0:T(8,128)(2,1)S(1)}, bf16[54,16,256]{2,1,0:T(8,128)(2,1)S(1)}, u32[]{:S(2)}, u32[]{:S(2)}) collective-permute-start(bf16[54,16,256]{2,1,0:T(8,128)(2,1)S(1)} %get-tuple-element.22.own_first), channel_id=1, source_target_pairs={{0,1},{1,0},{2,3},{3,2},{4,5},{5,4},{6,7},{7,6},{8,9},{9,8},{10,11... | collective-permute-start | bytes 1327112 | tf_op jit(solution)/shard_map/ppermute | solution.py:28
  7.0 9.7 %collective-permute-start.1 = (bf16[54,16,256]{2,1,0:T(8,128)(2,1)S(1)}, bf16[54,16,256]{2,1,0:T(8,128)(2,1)S(1)}, u32[]{:S(2)}, u32[]{:S(2)}) collective-permute-start(bf16[54,16,256]{2,1,0:T(8,128)(2,1)S(1)} %get-tuple-element.22.own_first), channel_id=1, source_target_pairs={{1,2},{2,1},{5,6},{6,5},{9,10},{10,9},{13,14},{14,13},{17,18},{18,... | collective-permute-start | bytes 1327112 | tf_op jit(solution)/shard_map/ppermute | solution.py:28
  7.7 6.3 %collective-permute-start.3 = (bf16[48,16,256]{2,1,0:T(8,128)(2,1)S(1)}, bf16[48,16,256]{2,1,0:T(8,128)(2,1)S(1)}, u32[]{:S(2)}, u32[]{:S(2)}) collective-permute-start(bf16[48,16,256]{2,1,0:T(8,128)(2,1)S(1)} %get-tuple-element.21.own_second), channel_id=1, source_target_pairs={{0,1},{1,0},{2,3},{3,2},{4,5},{5,4},{6,7},{7,6},{8,9},{9,8},{10,11... | collective-permute-start | bytes 1179656 | tf_op jit(solution)/shard_map/ppermute | solution.py:28
  10.6 8.6 %collective-permute-start = (bf16[48,16,256]{2,1,0:T(8,128)(2,1)S(1)}, bf16[48,16,256]{2,1,0:T(8,128)(2,1)S(1)}, u32[]{:S(2)}, u32[]{:S(2)}) collective-permute-start(bf16[48,16,256]{2,1,0:T(8,128)(2,1)S(1)} %get-tuple-element.21.own_second), channel_id=1, source_target_pairs={{1,2},{2,1},{5,6},{6,5},{9,10},{10,9},{13,14},{14,13},{17,18},{18,... | collective-permute-start | bytes 1179656 | tf_op jit(solution)/shard_map/ppermute | solution.py:28
  23.6 1.4 %collective-permute-start.5 = (bf16[256,256]{1,0:T(8,128)(2,1)S(1)}, bf16[256,256]{1,0:T(8,128)(2,1)S(1)}, u32[]{:S(2)}, u32[]{:S(2)}) collective-permute-start(bf16[256,256]{1,0:T(8,128)(2,1)S(1)} %shard_map.73), channel_id=1, source_target_pairs={{0,1},{1,0},{2,3},{3,2},{4,5},{5,4},{6,7},{7,6},{8,9},{9,8},{10,11... | collective-permute-start | bytes 393224 | tf_op jit(solution)/shard_map/ppermute | solution.py:20
  25.1 5.4 %collective-permute-start.7 = (bf16[256,256]{1,0:T(8,128)(2,1)S(1)}, bf16[256,256]{1,0:T(8,128)(2,1)S(1)}, u32[]{:S(2)}, u32[]{:S(2)}) collective-permute-start(bf16[256,256]{1,0:T(8,128)(2,1)S(1)} %add_convert_fusion), channel_id=1, source_target_pairs={{0,2},{1,5},{2,0},{3,7},{4,6},{5,1},{6,4},{7,3},{8,10},{9,13},{10,... | collective-permute-start | bytes 393224 | tf_op jit(solution)/shard_map/ppermute | solution.py:479
  26.7 5.2 %collective-permute-start.6 = (bf16[256,128]{1,0:T(8,128)(2,1)S(1)}, bf16[256,128]{1,0:T(8,128)(2,1)S(1)}, u32[]{:S(2)}, u32[]{:S(2)}) collective-permute-start(bf16[256,128]{1,0:T(8,128)(2,1)S(1)} %fusion.33), channel_id=1, source_target_pairs={{0,6},{1,7},{2,4},{3,5},{4,2},{5,3},{6,0},{7,1},{8,14},{9,15},{10,... | collective-permute-start | bytes 196616 | tf_op jit(solution)/shard_map/ppermute | solution.py:479
  30.5 1.4 %collective-permute-start.8 = (bf16[256,256]{1,0:T(8,128)(2,1)S(1)}, bf16[256,256]{1,0:T(8,128)(2,1)S(1)}, u32[]{:S(2)}, u32[]{:S(2)}) collective-permute-start(bf16[256,256]{1,0:T(8,128)(2,1)S(1)} %collective-permute-done.7), channel_id=1, source_target_pairs={{0,1},{1,0},{2,3},{3,2},{4,5},{5,4},{6,7},{7,6},{8,9},{9,8},{10,11... | collective-permute-start | bytes 393224 | tf_op jit(solution)/shard_map/ppermute | solution.py:20
  32.4 3.6 %collective-permute-start.9 = (bf16[256,128]{1,0:T(8,128)(2,1)S(1)}, bf16[256,128]{1,0:T(8,128)(2,1)S(1)}, u32[]{:S(2)}, u32[]{:S(2)}) collective-permute-start(bf16[256,128]{1,0:T(8,128)(2,1)S(1)} %collective-permute-done.6), channel_id=1, source_target_pairs={{0,1},{1,0},{2,3},{3,2},{4,5},{5,4},{6,7},{7,6},{8,9},{9,8},{10,11... | collective-permute-start | bytes 196616 | tf_op jit(solution)/shard_map/ppermute | solution.py:20
  32.6 5.3 %collective-permute-start.10 = (bf16[256,128]{1,0:T(8,128)(2,1)S(1)}, bf16[256,128]{1,0:T(8,128)(2,1)S(1)}, u32[]{:S(2)}, u32[]{:S(2)}) collective-permute-start(bf16[256,128]{1,0:T(8,128)(2,1)S(1)} %fusion.6), channel_id=1, source_target_pairs={{0,8},{4,12},{8,0},{12,4},{1,9},{5,13},{9,1},{13,5},{2,10},{6,14},... | collective-permute-start | bytes 196616 | tf_op jit(solution)/shard_map/ppermute | solution.py:20
  37.9 1.3 %collective-permute-start.11 = (bf16[256,128]{1,0:T(8,128)(2,1)S(1)}, bf16[256,128]{1,0:T(8,128)(2,1)S(1)}, u32[]{:S(2)}, u32[]{:S(2)}) collective-permute-start(bf16[256,128]{1,0:T(8,128)(2,1)S(1)} %collective-permute-done.10), channel_id=1, source_target_pairs={{0,1},{1,0},{2,3},{3,2},{4,5},{5,4},{6,7},{7,6},{8,9},{9,8},{10,11... | collective-permute-start | bytes 196616 | tf_op jit(solution)/shard_map/ppermute | solution.py:20
